TPU v7x, 32 devices: a whole 2x2x4 slice. The times are simulated.
32 devices in a mesh: stretch: 4 (over y, x), seq: 8 (over z, core).
Axes of the slice: x: 2, y: 2, z: 4, core: 2. Of those that a mesh axis runs over, the one named last changes fastest.
Arguments:
- query_rows: bfloat16 [4, 256, 4096], P('stretch', 'seq'), may hold values from -160 to 160
- key_rows: bfloat16 [4, 256, 4096], P('stretch', 'seq'), may hold values from -5 to 5
- value_rows: bfloat16 [4, 256, 4096], P('stretch', 'seq'), may hold values from -6 to 6
- cache_from: int32 [4], P('stretch'), may hold values from 0 to 255
- time_index: int32 [4], P('stretch'), may hold values from 0 to 49
- gate_table: float32 [50, 4096], replicated, may hold values from 4 to 16
Outputs:
- attn_out: bfloat16 [4, 256, 4096], P('stretch', 'seq')
All inputs are finite; a program needn't handle non-finite values.
Results may differ from a plain program's by a relative error of at most 0.0055.
Values may be sent and summed in bfloat16 or wider, within the bound.
No kernel may reach another device: no remote copies, remote signals or barrier semaphores. Data moves between devices by JAX's collectives and lax.ppermute only.
A program may use at most 64 MiB of HBM per device.

v0:
```python
import math

import jax
import jax.numpy as jnp
from jax import lax
from jax.sharding import PartitionSpec as P

HEADS = 32
HD = 128


def passed_along(block, axis, distance):
    devices = range(lax.axis_size(axis))
    route = [(i - distance, i) for i in devices if i - distance in devices]
    return lax.ppermute(block, axis, route)


def spread(rows, groups, per_dev, blocks):
    count = rows.shape[0]
    arranged = rows.reshape(count, groups, per_dev, HD).transpose(1, 0, 2, 3)
    return jnp.repeat(arranged, blocks, axis=0)


def body(query_rows, key_rows, value_rows, cache_from, time_index, gate_table):
    seq_count = lax.axis_size("seq")
    own_count = query_rows.shape[1]
    blocks = max(seq_count // HEADS, 1)
    per_dev = HEADS * blocks // seq_count
    groups = HEADS // per_dev
    part_len = own_count // blocks
    queries = query_rows[0].reshape(blocks, part_len, groups, per_dev, HD).transpose(2, 0, 1, 3, 4)
    queries = queries.reshape(groups * blocks, part_len, per_dev, HD)
    got_query, got_key, got_value = (
        lax.all_to_all(queries, "seq", split_axis=0, concat_axis=1, tiled=True),
        lax.all_to_all(
            spread(key_rows[0], groups, per_dev, blocks),
            "seq",
            split_axis=0,
            concat_axis=1,
            tiled=True,
        ),
        lax.all_to_all(
            spread(value_rows[0], groups, per_dev, blocks),
            "seq",
            split_axis=0,
            concat_axis=1,
            tiled=True,
        ),
    )
    got_past_key, got_past_value = passed_along((got_key, got_value), "stretch", 1)
    head_queries = got_query[0]
    total_tokens = got_key.shape[1]
    position = jnp.arange(total_tokens)
    later = lax.axis_index("stretch") > 0
    past_visible = jnp.logical_and(position >= cache_from[0], later)
    visible = jnp.concatenate([jnp.ones((total_tokens,), bool), past_visible])
    keys_all = jnp.concatenate([got_key[0], got_past_key[0]], 0)
    values_all = jnp.concatenate([got_value[0], got_past_value[0]], 0)
    span = math.gcd(512, 2 * total_tokens)
    count_blocks = 2 * total_tokens // span
    key_blocks = keys_all.reshape(count_blocks, span, per_dev, HD)
    value_blocks = values_all.reshape(count_blocks, span, per_dev, HD)
    visible_blocks = visible.reshape(count_blocks, span)
    query_count = head_queries.shape[0]
    scale = HD ** (-0.5)

    def absorb(carry, packed):
        largest, total, numer = carry
        key_block, value_block, seen = packed
        scores = (
            jnp.einsum("qhd,khd->hqk", head_queries, key_block, preferred_element_type=jnp.float32)
            * scale
        )
        scores = jnp.where(seen[None, None, :], scores, -1e30)
        updated = jnp.maximum(largest, jnp.max(scores, axis=2))
        factor = jnp.exp(largest - updated)
        weights = jnp.where(seen[None, None, :], jnp.exp(scores - updated[:, :, None]), 0.0)
        total = total * factor + jnp.sum(weights, axis=2)
        numer = numer * jnp.transpose(factor)[:, :, None] + jnp.einsum(
            "hqk,khd->qhd",
            weights.astype(jnp.bfloat16),
            value_block,
            preferred_element_type=jnp.float32,
        )
        return ((updated, total, numer), None)

    initial = (
        jnp.full((per_dev, query_count), -1e30, jnp.float32),
        jnp.zeros((per_dev, query_count), jnp.float32),
        jnp.zeros((query_count, per_dev, HD), jnp.float32),
    )
    (largest, total, numer), unused = lax.scan(
        absorb, initial, (key_blocks, value_blocks, visible_blocks)
    )
    attended = (numer / jnp.transpose(total)[:, :, None]).astype(jnp.bfloat16)
    returned = lax.all_to_all(attended[None], "seq", split_axis=1, concat_axis=0, tiled=True)
    tokens_out = returned.reshape(groups, blocks, part_len, per_dev, HD).transpose(1, 2, 0, 3, 4)
    tokens_out = tokens_out.reshape(own_count, HEADS * HD)
    matched = jnp.arange(gate_table.shape[0]) == time_index[0]
    gate_row = jnp.sum(jnp.where(matched[:, None], gate_table, 0.0), axis=0)
    attn_out = (tokens_out.astype(jnp.float32) * gate_row).astype(jnp.bfloat16)[None]
    return attn_out


def solution(mesh):
    return jax.shard_map(
        body,
        mesh=mesh,
        in_specs=(
            P("stretch", "seq", None),
            P("stretch", "seq", None),
            P("stretch", "seq", None),
            P("stretch"),
            P("stretch"),
            P(),
        ),
        out_specs=P("stretch", "seq", None),
        check_vma=False,
    )
```

profile of v0, /device:TPU:0, one launch (start us, length us, event | category | flops | bytes accessed | tf_op | source)
XLA Modules:
  0.0 67.2 jit_solution(5573573394884499893)
XLA Ops:
  0.0 0.0 copy-start.1
  0.0 1.2 %reshape_squeeze.9 = bf16[32,8,4,128]{3,2,1,0:T(4,128)(2,1)S(1)} reshape(bf16[1,32,4096]{2,1,0:T(8,128)(2,1)} %param.7) | data formatting | bytes 524288 | tf_op jit(solution)/shard_map/reshape;squeeze | solution.py:20
  1.2 0.8 %copy.56 = bf16[8,32,4,128]{3,1,2,0:T(8,128)(2,1)} copy(bf16[8,32,4,128]{3,2,0,1:T(4,128)(2,1)S(1)} %bitcast.56) | data formatting | bytes 524288 | tf_op jit(solution)/shard_map/transpose | solution.py:20
  2.0 6.3 %all-to-all-start = ((bf16[8,32,4,128]{3,1,2,0:T(8,128)(2,1)}), bf16[8,32,4,128]{3,1,2,0:T(8,128)(2,1)S(1)}, u32[]{:S(2)}, u32[]{:S(2)}) async-start(bf16[8,32,4,128]{3,1,2,0:T(8,128)(2,1)} %copy.56), calls=%async_computation | async-start | bytes 524288 | tf_op jit(solution)/shard_map/all_to_all | solution.py:35
  8.3 1.1 %reshape_squeeze.11 = bf16[32,8,4,128]{3,2,1,0:T(4,128)(2,1)S(1)} reshape(bf16[1,32,4096]{2,1,0:T(8,128)(2,1)} %param.8) | data formatting | bytes 524288 | tf_op jit(solution)/shard_map/reshape;squeeze | solution.py:20
  9.4 0.8 %copy.61 = bf16[8,32,4,128]{3,2,1,0:T(4,128)(2,1)} copy(bf16[8,32,4,128]{3,2,0,1:T(4,128)(2,1)S(1)} %bitcast.57) | data formatting | bytes 524288 | tf_op jit(solution)/shard_map/transpose | solution.py:20
  10.2 7.8 %all-to-all-done = bf16[8,32,4,128]{3,1,2,0:T(8,128)(2,1)S(1)} async-done(((bf16[8,32,4,128]{3,1,2,0:T(8,128)(2,1)}), bf16[8,32,4,128]{3,1,2,0:T(8,128)(2,1)S(1)}, u32[]{:S(2)}, u32[]{:S(2)}) %all-to-all-start) | async-done | bytes 262176 | tf_op jit(solution)/shard_map/all_to_all | solution.py:35
  18.0 3.4 %all-to-all-start.2 = ((bf16[8,32,4,128]{3,2,1,0:T(4,128)(2,1)}), bf16[8,32,4,128]{3,2,1,0:T(4,128)(2,1)S(1)}, u32[]{:S(2)}, u32[]{:S(2)}) async-start(bf16[8,32,4,128]{3,2,1,0:T(4,128)(2,1)} %copy.61), calls=%async_computation.2 | async-start | bytes 524288 | tf_op jit(solution)/shard_map/all_to_all | solution.py:42
  21.5 0.0 copy-done.1
  21.5 0.2 reshape_squeeze.10
  21.6 0.8 %copy.59 = bf16[8,32,4,128]{3,1,2,0:T(8,128)(2,1)} copy(bf16[8,32,4,128]{3,2,0,1:T(4,128)(2,1)S(1)} %bitcast.58) | data formatting | bytes 524288 | tf_op jit(solution)/shard_map/reshape | solution.py:32
  22.5 8.7 %all-to-all-done.2 = bf16[8,32,4,128]{3,2,1,0:T(4,128)(2,1)S(1)} async-done(((bf16[8,32,4,128]{3,2,1,0:T(4,128)(2,1)}), bf16[8,32,4,128]{3,2,1,0:T(4,128)(2,1)S(1)}, u32[]{:S(2)}, u32[]{:S(2)}) %all-to-all-start.2) | async-done | bytes 262176 | tf_op jit(solution)/shard_map/all_to_all | solution.py:42
  31.1 3.4 %all-to-all-start.1 = ((bf16[8,32,4,128]{3,1,2,0:T(8,128)(2,1)}), bf16[8,32,4,128]{3,1,2,0:T(8,128)(2,1)S(1)}, u32[]{:S(2)}, u32[]{:S(2)}) async-start(bf16[8,32,4,128]{3,1,2,0:T(8,128)(2,1)} %copy.59), calls=%async_computation.1 | async-start | bytes 524288 | tf_op jit(solution)/shard_map/all_to_all | solution.py:34
  34.6 3.4 %collective-permute-start = (bf16[1,256,4,128]{3,1,2,0:T(8,128)(2,1)S(1)}, bf16[1,256,4,128]{3,1,2,0:T(8,128)(2,1)S(1)}, u32[]{:S(2)}, u32[]{:S(2)}) collective-permute-start(bf16[1,256,4,128]{3,1,2,0:T(8,128)(2,1)S(1)} %bitcast.59), channel_id=1, source_target_pairs={{0,8},{8,16},{16,24},{1,9},{9,17},{17,25},{2,10},{10,18},{18,26},{... | collective-permute-start | bytes 786440 | tf_op jit(solution)/shard_map/ppermute | solution.py:15
  38.7 0.2 copy.64
  38.9 3.4 %collective-permute-start.1 = (bf16[1,256,4,128]{1,3,2,0:T(8,128)(2,1)S(1)}, bf16[1,256,4,128]{1,3,2,0:T(8,128)(2,1)S(1)}, u32[]{:S(2)}, u32[]{:S(2)}) collective-permute-start(bf16[1,256,4,128]{1,3,2,0:T(8,128)(2,1)S(1)} %copy.64), channel_id=1, source_target_pairs={{0,8},{8,16},{16,24},{1,9},{9,17},{17,25},{2,10},{10,18},{18,26},{... | collective-permute-start | bytes 786440 | tf_op jit(solution)/shard_map/ppermute | solution.py:15
  42.3 0.2 copy.65
  42.4 1.8 %all-to-all-done.1 = bf16[8,32,4,128]{3,1,2,0:T(8,128)(2,1)S(1)} async-done(((bf16[8,32,4,128]{3,1,2,0:T(8,128)(2,1)}), bf16[8,32,4,128]{3,1,2,0:T(8,128)(2,1)S(1)}, u32[]{:S(2)}, u32[]{:S(2)}) %all-to-all-start.1) | async-done | bytes 262176 | tf_op jit(solution)/shard_map/all_to_all | solution.py:34
  44.2 0.4 collective-permute-done
  44.6 0.5 bitcast_reduce_fusion
  45.1 0.6 fusion.2
  45.7 4.0 %collective-permute-done.1 = bf16[1,256,4,128]{1,3,2,0:T(8,128)(2,1)S(1)} collective-permute-done((bf16[1,256,4,128]{1,3,2,0:T(8,128)(2,1)S(1)}, bf16[1,256,4,128]{1,3,2,0:T(8,128)(2,1)S(1)}, u32[]{:S(2)}, u32[]{:S(2)}) %collective-permute-start.1) | collective-permute-done | bytes 262176 | tf_op jit(solution)/shard_map/ppermute | solution.py:15
  49.7 0.0 copy-start
  49.7 0.7 %fusion.7 = bf16[1,256,4,128]{1,3,2,0:T(8,128)(2,1)S(1)} fusion(f32[4,512,256]{2,1,0:T(8,128)S(1)} %get-tuple-element.22, f32[4,256]{1,0:T(4,128)S(1)} %get-tuple-element.20, pred[512]{0:T(512)(128)(4,1)S(1)} %concatenate.9, bf16[256,4,128]{0,2,1:T(8,128)(2,1)S(1)} %bitcast.63, bf16[256,4,128]{0,2,1:T(8,128)(2,1)S(1)} %copy.65, ...), kind=kOutput, calls=%fused_computation.11 | convolution fusion | flops 138280960 | bytes 2896384 | tf_op jit(solution)/shard_map/while/body/eval_jaxpr/hqk,khd->qhd/dot_general | solution.py:79
  50.4 0.9 %copy.67 = bf16[1,256,4,128]{3,2,0,1:T(4,128)(2,1)} copy(bf16[1,256,4,128]{1,3,2,0:T(8,128)(2,1)S(1)} %fusion.7) | data formatting | bytes 524288 | tf_op jit(solution)/shard_map/broadcast_in_dim | solution.py:96
  51.3 4.7 %all-to-all-start.3 = ((bf16[1,256,4,128]{3,2,0,1:T(4,128)(2,1)}), bf16[1,256,4,128]{3,2,0,1:T(4,128)(2,1)S(1)}, u32[]{:S(2)}, u32[]{:S(2)}) async-start(bf16[1,256,4,128]{3,2,0,1:T(4,128)(2,1)} %copy.67), calls=%async_computation.3 | async-start | bytes 524288 | tf_op jit(solution)/shard_map/all_to_all | solution.py:96
  56.7 0.0 copy-done
  56.7 0.2 select_reduce_fusion
  56.9 8.9 %all-to-all-done.3 = bf16[1,256,4,128]{3,2,0,1:T(4,128)(2,1)S(1)} async-done(((bf16[1,256,4,128]{3,2,0,1:T(4,128)(2,1)}), bf16[1,256,4,128]{3,2,0,1:T(4,128)(2,1)S(1)}, u32[]{:S(2)}, u32[]{:S(2)}) %all-to-all-start.3) | async-done | bytes 262176 | tf_op jit(solution)/shard_map/all_to_all | solution.py:96
  65.8 0.1 convert_bitcast_fusion
  65.9 0.3 copy.69
  66.2 1.0 %fusion.21 = bf16[1,32,4096]{2,1,0:T(8,128)(2,1)} fusion(f32[1,32,4096]{2,0,1:T(1,128)S(1)} %bitcast.54, f32[4096]{0:T(1024)S(1)} %select_reduce_fusion), kind=kLoop, calls=%fused_computation.27 | loop fusion | flops 262144 | bytes 802816 | tf_op jit(solution)/shard_map/convert_element_type | solution.py:101
  (8 shorter events, 0.1 us)
Async XLA Ops:
  0.0 21.5 %copy-start.1 = (bf16[1,32,4096]{2,1,0:T(8,128)(2,1)S(1)}, bf16[1,32,4096]{2,1,0:T(8,128)(2,1)}, u32[]{:S(2)}) copy-start(bf16[1,32,4096]{2,1,0:T(8,128)(2,1)} %param.6) | copy-start | bytes 786436
  2.0 16.1 %all-to-all-start = ((bf16[8,32,4,128]{3,1,2,0:T(8,128)(2,1)}), bf16[8,32,4,128]{3,1,2,0:T(8,128)(2,1)S(1)}, u32[]{:S(2)}, u32[]{:S(2)}) async-start(bf16[8,32,4,128]{3,1,2,0:T(8,128)(2,1)} %copy.56), calls=%async_computation | async-start | bytes 524288 | tf_op jit(solution)/shard_map/all_to_all | solution.py:35
  18.0 13.1 %all-to-all-start.2 = ((bf16[8,32,4,128]{3,2,1,0:T(4,128)(2,1)}), bf16[8,32,4,128]{3,2,1,0:T(4,128)(2,1)S(1)}, u32[]{:S(2)}, u32[]{:S(2)}) async-start(bf16[8,32,4,128]{3,2,1,0:T(4,128)(2,1)} %copy.61), calls=%async_computation.2 | async-start | bytes 524288 | tf_op jit(solution)/shard_map/all_to_all | solution.py:42
  31.1 13.1 %all-to-all-start.1 = ((bf16[8,32,4,128]{3,1,2,0:T(8,128)(2,1)}), bf16[8,32,4,128]{3,1,2,0:T(8,128)(2,1)S(1)}, u32[]{:S(2)}, u32[]{:S(2)}) async-start(bf16[8,32,4,128]{3,1,2,0:T(8,128)(2,1)} %copy.59), calls=%async_computation.1 | async-start | bytes 524288 | tf_op jit(solution)/shard_map/all_to_all | solution.py:34
  34.6 10.0 %collective-permute-start = (bf16[1,256,4,128]{3,1,2,0:T(8,128)(2,1)S(1)}, bf16[1,256,4,128]{3,1,2,0:T(8,128)(2,1)S(1)}, u32[]{:S(2)}, u32[]{:S(2)}) collective-permute-start(bf16[1,256,4,128]{3,1,2,0:T(8,128)(2,1)S(1)} %bitcast.59), channel_id=1, source_target_pairs={{0,8},{8,16},{16,24},{1,9},{9,17},{17,25},{2,10},{10,18},{18,26},{... | collective-permute-start | bytes 786440 | tf_op jit(solution)/shard_map/ppermute | solution.py:15
  38.9 10.9 %collective-permute-start.1 = (bf16[1,256,4,128]{1,3,2,0:T(8,128)(2,1)S(1)}, bf16[1,256,4,128]{1,3,2,0:T(8,128)(2,1)S(1)}, u32[]{:S(2)}, u32[]{:S(2)}) collective-permute-start(bf16[1,256,4,128]{1,3,2,0:T(8,128)(2,1)S(1)} %copy.64), channel_id=1, source_target_pairs={{0,8},{8,16},{16,24},{1,9},{9,17},{17,25},{2,10},{10,18},{18,26},{... | collective-permute-start | bytes 786440 | tf_op jit(solution)/shard_map/ppermute | solution.py:15
  49.7 7.0 %copy-start = (f32[50,4096]{1,0:T(8,128)S(1)}, f32[50,4096]{1,0:T(8,128)}, u32[]{:S(2)}) copy-start(f32[50,4096]{1,0:T(8,128)} %param.11) | copy-start | bytes 2457604
  51.3 14.5 %all-to-all-start.3 = ((bf16[1,256,4,128]{3,2,0,1:T(4,128)(2,1)}), bf16[1,256,4,128]{3,2,0,1:T(4,128)(2,1)S(1)}, u32[]{:S(2)}, u32[]{:S(2)}) async-start(bf16[1,256,4,128]{3,2,0,1:T(4,128)(2,1)} %copy.67), calls=%async_computation.3 | async-start | bytes 524288 | tf_op jit(solution)/shard_map/all_to_all | solution.py:96
where the time goes:
time: 68.3 us; the launch traced here: 67.2 us
  waiting for transfers between devices  31.6 us (46%)
  starting transfers between devices  24.7 us (36%)
  local copies, waits for them, and re-layouts  6.5 us (10%)
  other arithmetic  1.85 us (3%)
  between operations  1.47 us (2%)
  matrix products  1.17 us (2%)
    all_to_all x1, waiting for transfers between devices, body(): lax.all_to_all(attended[None], 'seq', split_axis=1, concat_axis=0, tiled=...  8.9 us
    all_to_all x1, waiting for transfers between devices, body(): lax.all_to_all(spread(value_rows[0], groups, per_dev, blocks), 'seq', spl...  8.67 us
    all_to_all x1, waiting for transfers between devices, body(): lax.all_to_all(spread(key_rows[0], groups, per_dev, blocks), 'seq', split...  7.82 us
    ppermute x2, starting transfers between devices, passed_along(): return lax.ppermute(block, axis, route)  6.81 us
    all_to_all x1, starting transfers between devices, body(): lax.all_to_all(spread(key_rows[0], groups, per_dev, blocks), 'seq', split...  6.33 us
    all_to_all x1, starting transfers between devices, body(): lax.all_to_all(attended[None], 'seq', split_axis=1, concat_axis=0, tiled=...  4.74 us
    ppermute x2, waiting for transfers between devices, passed_along(): return lax.ppermute(block, axis, route)  4.39 us
    all_to_all x1, starting transfers between devices, body(): lax.all_to_all(queries, 'seq', split_axis=0, concat_axis=1, tiled=True)  3.41 us
  transfers between devices with their start and end apart: 6, of which 6 were waited for; matrix products, arithmetic and copies ran while one was open for 7% of the time, Pallas kernels for 0%

commit v1 on v0

--- a/solution.py
+++ b/solution.py
@@ -3,10 +3,15 @@
 import jax
 import jax.numpy as jnp
 from jax import lax
+from jax.experimental import pallas as pl
+from jax.experimental.pallas import tpu as pltpu
 from jax.sharding import PartitionSpec as P
 
 HEADS = 32
 HD = 128
+VMEM = pl.BlockSpec(memory_space=pltpu.VMEM)
+SMEM = pl.BlockSpec(memory_space=pltpu.SMEM)
+ANY = pl.BlockSpec(memory_space=pl.ANY)
 
 
 def passed_along(block, axis, distance):
@@ -21,7 +26,7 @@
     return jnp.repeat(arranged, blocks, axis=0)
 
 
-def body(query_rows, key_rows, value_rows, cache_from, time_index, gate_table):
+def general_body(query_rows, key_rows, value_rows, cache_from, time_index, gate_table):
     seq_count = lax.axis_size("seq")
     own_count = query_rows.shape[1]
     blocks = max(seq_count // HEADS, 1)
@@ -102,9 +107,93 @@
     return attn_out
 
 
+def pack_kernel(query_ref, key_ref, value_ref, packed_ref):
+    rows = query_ref.shape[0]
+    for head in range(HEADS):
+        lanes = pl.ds(head * HD, HD)
+        for part, ref in enumerate((query_ref, key_ref, value_ref)):
+            packed_ref[head, pl.ds(part * rows, rows), :] = ref[:, lanes]
+
+
+def attend_kernel(cache_ref, time_ref, got_ref, gate_ref, out_ref, row_ref, sem):
+    fetch = pltpu.make_async_copy(gate_ref.at[pl.ds(time_ref[0], 1)], row_ref, sem)
+    fetch.start()
+    clips = cache_ref.shape[0]
+    devices, triple, _ = got_ref.shape
+    seq, rows = devices // clips, triple // 3
+    tokens = seq * rows
+
+    def part(clip, which):
+        block = got_ref[pl.ds(clip * seq, seq), pl.ds(which * rows, rows), :]
+        return block.reshape(tokens, HD)
+
+    def product(left, right, dims):
+        return lax.dot_general(left, right, (dims, ((), ())), preferred_element_type=jnp.float32)
+
+    scale = HD ** (-0.5)
+    for clip in range(clips):
+        query = part(clip, 0)
+        own = product(query, part(clip, 1), ((1,), (1,))) * scale
+        largest = jnp.max(own, axis=1, keepdims=True)
+        if clip > 0:
+            past = product(query, part(clip - 1, 1), ((1,), (1,))) * scale
+            position = lax.broadcasted_iota(jnp.int32, past.shape, 1)
+            past = jnp.where(position >= cache_ref[clip], past, -1e30)
+            largest = jnp.maximum(largest, jnp.max(past, axis=1, keepdims=True))
+        weights = jnp.exp(own - largest)
+        total = jnp.sum(weights, axis=1, keepdims=True)
+        numer = product(weights.astype(jnp.bfloat16), part(clip, 2), ((1,), (0,)))
+        if clip > 0:
+            weights = jnp.exp(past - largest)
+            total += jnp.sum(weights, axis=1, keepdims=True)
+            numer += product(weights.astype(jnp.bfloat16), part(clip - 1, 2), ((1,), (0,)))
+        attended = (numer / total).astype(jnp.bfloat16)
+        out_ref[pl.ds(clip * seq, seq)] = attended.reshape(seq, rows, HD)
+    fetch.wait()
+
+
+def unpack_kernel(got_ref, row_ref, out_ref):
+    for head in range(HEADS):
+        lanes = pl.ds(head * HD, HD)
+        gated = got_ref[head].astype(jnp.float32) * row_ref[:, lanes]
+        out_ref[:, lanes] = gated.astype(jnp.bfloat16)
+
+
+def head_body(query_rows, key_rows, value_rows, cache_from, time_index, gate_table):
+    axes = ("stretch", "seq")
+    rows = query_rows.shape[1]
+    clips = lax.axis_size("stretch")
+    packed = pl.pallas_call(
+        pack_kernel,
+        out_shape=jax.ShapeDtypeStruct((HEADS, 3 * rows, HD), jnp.bfloat16),
+        in_specs=[VMEM] * 3,
+        out_specs=VMEM,
+    )(query_rows[0], key_rows[0], value_rows[0])
+    cache_all = lax.all_gather(cache_from, "stretch", tiled=True)
+    got = lax.all_to_all(packed, axes, split_axis=0, concat_axis=0, tiled=True)
+    attended, gate_row = pl.pallas_call(
+        attend_kernel,
+        out_shape=(
+            jax.ShapeDtypeStruct((HEADS, rows, HD), jnp.bfloat16),
+            jax.ShapeDtypeStruct((1, HEADS * HD), jnp.float32),
+        ),
+        in_specs=[SMEM, SMEM, VMEM, ANY],
+        out_specs=(VMEM, VMEM),
+        scratch_shapes=[pltpu.SemaphoreType.DMA],
+    )(cache_all, time_index, got, gate_table)
+    back = lax.all_to_all(attended, axes, split_axis=0, concat_axis=0, tiled=True)
+    return pl.pallas_call(
+        unpack_kernel,
+        out_shape=jax.ShapeDtypeStruct((rows, HEADS * HD), jnp.bfloat16),
+        in_specs=[VMEM, VMEM],
+        out_specs=VMEM,
+    )(back, gate_row)[None]
+
+
 def solution(mesh):
+    by_head = mesh.shape["stretch"] * mesh.shape["seq"] == HEADS
     return jax.shard_map(
-        body,
+        head_body if by_head else general_body,
         mesh=mesh,
         in_specs=(
             P("stretch", "seq", None),

time: 68.3 us -> 51.3 us (0.75)
  blocking collectives: 0 us -> 21.9 us
  waiting for transfers between devices: 31.6 us -> 10.5 us
  starting transfers between devices: 24.7 us -> 7.3 us
  Pallas kernels: 0 us -> 7.05 us
  local copies, waits for them, and re-layouts: 6.5 us -> 2.88 us
  other arithmetic: 1.85 us -> 0 us
  matrix products: 1.17 us -> 0 us
    all_to_all x4 -> x1, waiting for transfers between devices: 27.2 us -> 10.5 us  [head_body(): got = lax.all_to_all(packed, axes, split_axis=0, concat_axis=0, tiled=True)]
    all_to_all x0 -> x1, blocking collectives: none -> 13.7 us  [head_body(): lax.all_to_all(attended, axes, split_axis=0, concat_axis=0, tiled=True)]
    all_to_all x4 -> x1, starting transfers between devices: 17.9 us -> 7.3 us  [head_body(): got = lax.all_to_all(packed, axes, split_axis=0, concat_axis=0, tiled=True)]
    unnamed x0 -> x1, blocking collectives: none -> 8.18 us
    pallas_call x0 -> x3, Pallas kernels: none -> 7.05 us  [the longest x1 3.21 us: head_body(): pl.pallas_call(attend_kernel, out_shape=(jax.ShapeDtypeStruct((HEADS, row...]
    ppermute x2 -> x0, starting transfers between devices: 6.81 us -> none  [passed_along(): return lax.ppermute(block, axis, route)]
    ppermute x2 -> x0, waiting for transfers between devices: 4.39 us -> none  [passed_along(): return lax.ppermute(block, axis, route)]
    unnamed x4 -> x7, local copies, waits for them, and re-layouts: 0.01 us -> 2.88 us
  transfers between devices with their start and end apart: 6 -> 1, of which waited for: 6 -> 1; matrix products, arithmetic and copies ran while one was open for 7% -> 3% of each run, Pallas kernels for 0% -> 0%
where the time goes in v1:
time: 51.3 us; the launch traced here: 50.9 us
  blocking collectives  21.9 us (43%)
  waiting for transfers between devices  10.5 us (20%)
  starting transfers between devices  7.3 us (14%)
  Pallas kernels  7.05 us (14%)
  local copies, waits for them, and re-layouts  2.88 us (6%)
  between operations  1.33 us (3%)
    all_to_all x1, blocking collectives, head_body(): lax.all_to_all(attended, axes, split_axis=0, concat_axis=0, tiled=True)  13.7 us
    all_to_all x1, waiting for transfers between devices, head_body(): got = lax.all_to_all(packed, axes, split_axis=0, concat_axis=0, tiled=True)  10.5 us
    unnamed x1, blocking collectives  8.18 us
    all_to_all x1, starting transfers between devices, head_body(): got = lax.all_to_all(packed, axes, split_axis=0, concat_axis=0, tiled=True)  7.3 us
    pallas_call x1, Pallas kernels, head_body(): pl.pallas_call(attend_kernel, out_shape=(jax.ShapeDtypeStruct((HEADS, row...  3.21 us
    unnamed x7, local copies, waits for them, and re-layouts  2.88 us
    pallas_call x1, Pallas kernels, head_body(): pl.pallas_call(pack_kernel, out_shape=jax.ShapeDtypeStruct((HEADS, 3 * ro...  2.14 us
    pallas_call x1, Pallas kernels, head_body(): pl.pallas_call(unpack_kernel, out_shape=jax.ShapeDtypeStruct((rows, HEADS...  1.71 us
  transfers between devices with their start and end apart: 1, of which 1 were waited for; matrix products, arithmetic and copies ran while one was open for 3% of the time, Pallas kernels for 0%

profile of v1, /device:TPU:0, one launch (start us, length us, event | category | flops | bytes accessed | tf_op | source)
XLA Modules:
  0.0 50.9 jit_solution(2136922759974429916)
XLA Ops:
  0.0 2.1 %shard_map.64 = bf16[32,96,128]{2,1,0:T(8,128)(2,1)} custom-call(bf16[32,4096]{1,0:T(8,128)(2,1)} %bitcast.5, bf16[32,4096]{1,0:T(8,128)(2,1)} %bitcast.6, bf16[32,4096]{1,0:T(8,128)(2,1)} %bitcast.7), custom_call_target="tpu_custom_call" | custom-call | tf_op jit(solution)/shard_map/pallas_call | solution.py:166
  2.1 7.3 %all-to-all-start = ((bf16[32,96,128]{2,1,0:T(8,128)(2,1)}), bf16[32,96,128]{2,1,0:T(8,128)(2,1)S(1)}, u32[]{:S(2)}, u32[]{:S(2)}) async-start(bf16[32,96,128]{2,1,0:T(8,128)(2,1)} %shard_map.64), calls=%async_computation | async-start | bytes 1572864 | tf_op jit(solution)/shard_map/all_to_all | solution.py:173
  10.1 0.0 copy-start.1
  10.1 0.6 %copy-done.1 = u32[32]{0:T(128)S(1)} copy-done((u32[32]{0:T(128)S(1)}, u32[32]{0:T(128)}, u32[]{:S(2)}) %copy-start.1) | copy-done | bytes 152
  10.8 0.6 %dynamic-slice = u32[1]{0:T(128)} dynamic-slice(u32[32]{0:T(128)S(1)} %copy-done.1, u32[]{:T(128)S(6)} %add), dynamic_slice_sizes={1} | dynamic-slice | bytes 12
  11.3 0.8 %dynamic-update-slice = s32[4]{0:T(128)S(1)} dynamic-update-slice(s32[4]{0:T(128)S(1)} %broadcast, s32[1]{0:T(128)S(6)} %copy.8, u32[]{:T(128)} %bitcast) | dynamic-update-slice | bytes 12
  12.1 8.2 %all-reduce.cache_ref = s32[4]{0:T(128)} all-reduce(s32[4]{0:T(128)S(1)} %dynamic-update-slice), channel_id=1, replica_groups=mesh['stretch'=4,'seq'=8] {'stretch'}, use_global_device_ids=true, to_apply=%add | all-reduce | flops 4 | bytes 32
  20.9 10.5 %all-to-all-done.got_ref = bf16[32,96,128]{2,1,0:T(8,128)(2,1)S(1)} async-done(((bf16[32,96,128]{2,1,0:T(8,128)(2,1)}), bf16[32,96,128]{2,1,0:T(8,128)(2,1)S(1)}, u32[]{:S(2)}, u32[]{:S(2)}) %all-to-all-start) | async-done | bytes 786464 | tf_op jit(solution)/shard_map/all_to_all | solution.py:173
  31.4 0.0 copy-start
  31.4 0.9 %copy-done = bf16[32,96,128]{2,1,0:T(8,128)(2,1)} copy-done((bf16[32,96,128]{2,1,0:T(8,128)(2,1)}, bf16[32,96,128]{2,1,0:T(8,128)(2,1)S(1)}, u32[]{:S(2)}) %copy-start) | copy-done | bytes 786456
  32.3 3.2 %shard_map.65 = (bf16[32,32,128]{2,1,0:T(8,128)(2,1)}, f32[1,4096]{1,0:T(1,128)}) custom-call(s32[4]{0:T(128)} %all-reduce.cache_ref, s32[1]{0:T(128)S(6)} %copy.9.time_ref, bf16[32,96,128]{2,1,0:T(8,128)(2,1)} %copy-done, f32[50,4096]{1,0:T(8,128)} %gate_ref.1), custom_call_target="tpu_custom_call" | custom-call | tf_op jit(solution)/shard_map/pallas_call | solution.py:174
  35.5 13.7 %all_to_all.10.got_ref = bf16[32,32,128]{2,1,0:T(8,128)(2,1)} all-to-all(bf16[32,32,128]{2,1,0:T(8,128)(2,1)} %get-tuple-element.7), channel_id=1, replica_groups=mesh['stretch'=4,'seq'=8] {'stretch','seq'}, dimensions={0} | all-to-all | bytes 524288 | tf_op jit(solution)/shard_map/all_to_all | solution.py:184
  49.2 1.7 %shard_map.66 = bf16[32,4096]{1,0:T(8,128)(2,1)} custom-call(bf16[32,32,128]{2,1,0:T(8,128)(2,1)} %all_to_all.10.got_ref, f32[1,4096]{1,0:T(1,128)} %get-tuple-element.8.row_ref), custom_call_target="tpu_custom_call" | custom-call | tf_op jit(solution)/shard_map/pallas_call | solution.py:185
  (1 shorter events, 0.0 us)
Async XLA Ops:
  2.1 29.3 %all-to-all-start = ((bf16[32,96,128]{2,1,0:T(8,128)(2,1)}), bf16[32,96,128]{2,1,0:T(8,128)(2,1)S(1)}, u32[]{:S(2)}, u32[]{:S(2)}) async-start(bf16[32,96,128]{2,1,0:T(8,128)(2,1)} %shard_map.64), calls=%async_computation | async-start | bytes 1572864 | tf_op jit(solution)/shard_map/all_to_all | solution.py:173
  10.1 0.7 %copy-start.1 = (u32[32]{0:T(128)S(1)}, u32[32]{0:T(128)}, u32[]{:S(2)}) copy-start(u32[32]{0:T(128)} %constant.7) | copy-start | bytes 388
  31.4 0.9 %copy-start = (bf16[32,96,128]{2,1,0:T(8,128)(2,1)}, bf16[32,96,128]{2,1,0:T(8,128)(2,1)S(1)}, u32[]{:S(2)}) copy-start(bf16[32,96,128]{2,1,0:T(8,128)(2,1)S(1)} %all-to-all-done.got_ref) | copy-start | bytes 2359300

commit v2 on v0

--- a/solution.py
+++ b/solution.py
@@ -3,10 +3,16 @@
 import jax
 import jax.numpy as jnp
 from jax import lax
+from jax.experimental import pallas as pl
+from jax.experimental.pallas import tpu as pltpu
 from jax.sharding import PartitionSpec as P
 
 HEADS = 32
 HD = 128
+VMEM = pl.BlockSpec(memory_space=pltpu.VMEM)
+SMEM = pl.BlockSpec(memory_space=pltpu.SMEM)
+ANY = pl.BlockSpec(memory_space=pl.ANY)
+HBM = pl.BlockSpec(memory_space=pltpu.HBM)
 
 
 def passed_along(block, axis, distance):
@@ -21,7 +27,7 @@
     return jnp.repeat(arranged, blocks, axis=0)
 
 
-def body(query_rows, key_rows, value_rows, cache_from, time_index, gate_table):
+def general_body(query_rows, key_rows, value_rows, cache_from, time_index, gate_table):
     seq_count = lax.axis_size("seq")
     own_count = query_rows.shape[1]
     blocks = max(seq_count // HEADS, 1)
@@ -102,9 +108,227 @@
     return attn_out
 
 
+def chips_of(seq):
+    return seq // 2
+
+
+def steps_of(chips):
+    return [step for step in range(1, chips) if step >= chips // 2] + list(range(1, chips // 2))
+
+
+def span_of(chip, width):
+    return pl.ds(pl.multiple_of(chip * width, width), width)
+
+
+def pack_kernel(*refs):
+    whole, parts, sems = refs[:3], refs[3:-1], refs[-1]
+    chips = len(parts) // 3
+    chip = lax.axis_index("seq") // 2
+    copies = []
+    for index, ref in enumerate(whole):
+        width = ref.shape[1] // chips
+        for place, step in enumerate([0] + steps_of(chips)):
+            copies.append(
+                pltpu.make_async_copy(
+                    ref.at[:, span_of(chip ^ step, width)],
+                    parts[index * chips + place],
+                    sems.at[index * chips + place],
+                )
+            )
+    for copy in copies:
+        copy.start()
+    for copy in copies:
+        copy.wait()
+
+
+def join_kernel(*refs):
+    parts, out_ref = refs[:-1], refs[-1]
+    rows = parts[0].shape[0]
+    for place, part in enumerate(parts):
+        out_ref[pl.ds(place * rows, rows)] = part[...]
+
+
+def product(left, right, dims):
+    return lax.dot_general(left, right, (dims, ((), ())), preferred_element_type=jnp.float32)
+
+
+def weigh_kernel(cache_ref, *refs):
+    chips = len(refs) - 9
+    queries, refs = refs[:chips], refs[chips:]
+    key_refs, value_refs, past_refs = refs[0:2], refs[2:4], refs[4:6]
+    past_weight_ref, total_ref, numer_ref = refs[6:9]
+    rows, width = queries[0].shape
+    half = chips * rows
+    tokens = 2 * half
+    core = lax.rem(lax.axis_index("seq"), 2)
+    chip = lax.axis_index("seq") // 2
+    seen_from = jnp.where(lax.axis_index("stretch") > 0, cache_ref[0], tokens)
+    steps = [0] + steps_of(chips)
+    lane = lax.broadcasted_iota(jnp.int32, (1, rows), 1)
+    position = jnp.concatenate(
+        [
+            lane + ((chip ^ step) * 2 + (core ^ other)) * rows
+            for other in range(2)
+            for step in steps
+        ],
+        axis=1,
+    )
+    visible = position >= seen_from
+    scale = HD ** (-0.5)
+    for head in range(width // HD):
+        lanes = pl.ds(head * HD, HD)
+        query = jnp.concatenate([ref[:, lanes] for ref in queries], axis=0)
+        key = jnp.concatenate([ref[:, lanes] for ref in key_refs], axis=0)
+        value = jnp.concatenate([ref[:, lanes] for ref in value_refs], axis=0)
+        past_key = jnp.concatenate([ref[:, lanes] for ref in past_refs], axis=0)
+        own = product(query, key, ((1,), (1,))) * scale
+        past = product(query, past_key, ((1,), (1,))) * scale
+        past = jnp.where(visible, past, -1e30)
+        largest = jnp.max(jnp.maximum(own, past), axis=1, keepdims=True)
+        own = jnp.exp(own - largest)
+        past = jnp.exp(past - largest)
+        total_ref[head] = jnp.sum(own + past, axis=1, keepdims=True)
+        numer_ref[:, lanes] = product(own.astype(jnp.bfloat16), value, ((1,), (0,)))
+        past_weight_ref[head] = past.astype(jnp.bfloat16)
+
+
+def finish_kernel(time_ref, past_weight_ref, total_ref, numer_ref, *refs):
+    past_refs, gate_ref = refs[0:2], refs[2]
+    outs, gate_row, sem = refs[3:-2], refs[-2], refs[-1]
+    chips = len(outs)
+    width = outs[0].shape[1]
+    rows = outs[0].shape[0]
+    chip = lax.axis_index("seq") // 2
+    fetch = pltpu.make_async_copy(gate_ref.at[pl.ds(time_ref[0], 1), span_of(chip, width)], gate_row, sem)
+    fetch.start()
+    fetch.wait()
+    for head in range(width // HD):
+        lanes = pl.ds(head * HD, HD)
+        past_value = jnp.concatenate([ref[:, lanes] for ref in past_refs], axis=0)
+        numer = numer_ref[:, lanes] + product(past_weight_ref[head], past_value, ((1,), (0,)))
+        attended = (numer / total_ref[head]).astype(jnp.bfloat16)
+        gated = (attended.astype(jnp.float32) * gate_row[:, lanes]).astype(jnp.bfloat16)
+        for place in range(chips):
+            outs[place][:, lanes] = gated[place * rows:(place + 1) * rows]
+
+
+def unpack_kernel(*refs):
+    parts, out_ref, sems = refs[:-2], refs[-2], refs[-1]
+    chips = len(parts)
+    chip = lax.axis_index("seq") // 2
+    width = parts[0].shape[1]
+    copies = [
+        pltpu.make_async_copy(part, out_ref.at[:, span_of(chip ^ step, width)], sems.at[place])
+        for place, (part, step) in enumerate(zip(parts, [0] + steps_of(chips)))
+    ]
+    for copy in copies:
+        copy.start()
+    for copy in copies:
+        copy.wait()
+
+
+def kernel_call(kernel, ins, outs, scratch=(), work=0):
+    many = isinstance(outs, tuple)
+    call = pl.pallas_call(
+        kernel,
+        out_shape=jax.tree.map(lambda out: pltpu.VMEM(out.shape, out.dtype), outs),
+        in_specs=ins,
+        out_specs=(VMEM,) * len(outs) if many else VMEM,
+        scratch_shapes=[*scratch],
+        cost_estimate=pl.CostEstimate(flops=work, bytes_accessed=0, transcendentals=0),
+        compiler_params=pltpu.CompilerParams(vmem_limit_bytes=4 << 20),
+    )
+
+    def run(*operands):
+        return call(
+            *(
+                pltpu.with_memory_space_constraint(operand, spec.memory_space)
+                if spec in (VMEM, HBM)
+                else operand
+                for operand, spec in zip(operands, ins)
+            )
+        )
+
+    return run
+
+
+def chip_body(query_rows, key_rows, value_rows, cache_from, time_index, gate_table):
+    seq = lax.axis_size("seq")
+    chips = chips_of(seq)
+    rows = query_rows.shape[1]
+    width = HEADS * HD // chips
+    half = chips * rows
+    steps = steps_of(chips)
+    block = jax.ShapeDtypeStruct((rows, width), jnp.bfloat16)
+    joined = jax.ShapeDtypeStruct((half, width), jnp.bfloat16)
+
+    def between_chips(parts):
+        return [parts[0]] + [
+            lax.ppermute(part, "seq", [(i, i ^ (2 * step)) for i in range(seq)])
+            for part, step in zip(parts[1:], steps)
+        ]
+
+    def between_cores(part):
+        return lax.ppermute(part, "seq", [(i, i ^ 1) for i in range(seq)])
+
+    def join(parts):
+        return kernel_call(join_kernel, [VMEM] * chips, joined)(*parts)
+
+    parts = kernel_call(
+        pack_kernel,
+        [HBM] * 3,
+        (block,) * (3 * chips),
+        scratch=[pltpu.SemaphoreType.DMA((3 * chips,))],
+    )(
+        key_rows[0], value_rows[0], query_rows[0]
+    )
+    keys = join(between_chips(parts[:chips]))
+    past_keys = passed_along(keys, "stretch", 1)
+    values = join(between_chips(parts[chips:2 * chips]))
+    past_values = passed_along(values, "stretch", 1)
+    queries = between_chips(parts[2 * chips:])
+    queries, keys, values = lax.optimization_barrier((queries, keys, values))
+    per_dev = width // HD
+    past_weight, total, numer = kernel_call(
+        weigh_kernel,
+        [SMEM] + [VMEM] * (chips + 6),
+        (
+            jax.ShapeDtypeStruct((per_dev, half, 2 * half), jnp.bfloat16),
+            jax.ShapeDtypeStruct((per_dev, half, 1), jnp.float32),
+            jax.ShapeDtypeStruct((half, width), jnp.float32),
+        ),
+    )(
+        cache_from,
+        *queries,
+        keys,
+        between_cores(keys),
+        values,
+        between_cores(values),
+        past_keys,
+        between_cores(past_keys),
+    )
+    outs = kernel_call(
+        finish_kernel,
+        [SMEM] + [VMEM] * 5 + [ANY],
+        (block,) * chips,
+        scratch=[pltpu.VMEM((1, width), jnp.float32), pltpu.SemaphoreType.DMA],
+    )(time_index, past_weight, total, numer, past_values, between_cores(past_values), gate_table)
+    returned = between_chips(outs)
+    out = pl.pallas_call(
+        unpack_kernel,
+        out_shape=jax.ShapeDtypeStruct((rows, HEADS * HD), jnp.bfloat16),
+        in_specs=[VMEM] * chips,
+        out_specs=ANY,
+        scratch_shapes=[pltpu.SemaphoreType.DMA((chips,))],
+    )(*(pltpu.with_memory_space_constraint(part, pltpu.VMEM) for part in returned))
+    return out[None]
+
+
 def solution(mesh):
+    chips = chips_of(mesh.shape["seq"])
+    by_chip = HEADS % chips == 0 and chips & (chips - 1) == 0
     return jax.shard_map(
-        body,
+        chip_body if by_chip else general_body,
         mesh=mesh,
         in_specs=(
             P("stretch", "seq", None),

time: 68.3 us -> 45.1 us (0.66); the launches traced: 67.2 us -> 44.9 us
  waiting for transfers between devices: 31.6 us -> 12.1 us
  local copies, waits for them, and re-layouts: 6.5 us -> 0.01 us
  Pallas kernels: 0 us -> 4.52 us
  starting transfers between devices: 24.7 us -> 26.9 us
  other arithmetic: 1.85 us -> 0 us
  matrix products: 1.17 us -> 0 us
    all_to_all x4 -> x0, waiting for transfers between devices: 27.2 us -> none  [the longest x1 8.9 us: body(): lax.all_to_all(attended[None], 'seq', split_axis=1, concat_axis=0, tiled=...]
    ppermute x0 -> x16, starting transfers between devices: none -> 19.8 us  [the longest x12 18.8 us: between_chips(): lax.ppermute(part, 'seq', [(i, i ^ 2 * step) for i in range(seq)])]
    all_to_all x4 -> x0, starting transfers between devices: 17.9 us -> none  [the longest x1 6.33 us: body(): lax.all_to_all(spread(key_rows[0], groups, per_dev, blocks), 'seq', split...]
    ppermute x0 -> x16, waiting for transfers between devices: none -> 12.1 us  [the longest x12 12.1 us: between_chips(): lax.ppermute(part, 'seq', [(i, i ^ 2 * step) for i in range(seq)])]
    pallas_call x0 -> x6, Pallas kernels: none -> 4.52 us  [the longest x5 3.79 us: run(): call(*(pltpu.with_memory_space_constraint(operand, spec.memory_space) if...]
    ppermute x2, waiting for transfers between devices: 4.39 us -> 0.01 us  [passed_along(): return lax.ppermute(block, axis, route)]
    another operation x3 -> x0, local copies, waits for them, and re-layouts: 2.44 us -> none  [the longest x2 2.27 us: spread(): arranged = rows.reshape(count, groups, per_dev, HD).transpose(1, 0, 2, 3)]
    transpose x2 -> x0, local copies, waits for them, and re-layouts: 1.61 us -> none  [spread(): arranged = rows.reshape(count, groups, per_dev, HD).transpose(1, 0, 2, 3)]
  transfers between devices with their start and end apart: 6 -> 18, of which waited for: 6 -> 8; matrix products, arithmetic and copies ran while one was open for 7% -> 0% of each run, Pallas kernels for 0% -> 5%
where the time goes in v2:
time: 45.1 us; the launch traced here: 44.9 us
  starting transfers between devices  26.9 us (60%)
  waiting for transfers between devices  12.1 us (27%)
  Pallas kernels  4.52 us (10%)
  between operations  1.41 us (3%)
    ppermute x12, starting transfers between devices, between_chips(): lax.ppermute(part, 'seq', [(i, i ^ 2 * step) for i in range(seq)])  18.8 us
    ppermute x12, waiting for transfers between devices, between_chips(): lax.ppermute(part, 'seq', [(i, i ^ 2 * step) for i in range(seq)])  12.1 us
    ppermute x2, starting transfers between devices, passed_along(): return lax.ppermute(block, axis, route)  7.03 us
    pallas_call x5, Pallas kernels, run(): call(*(pltpu.with_memory_space_constraint(operand, spec.memory_space) if...  3.79 us
    ppermute x4, starting transfers between devices, between_cores(): return lax.ppermute(part, 'seq', [(i, i ^ 1) for i in range(seq)])  1.02 us
  transfers between devices with their start and end apart: 18, of which 8 were waited for; matrix products, arithmetic and copies ran while one was open for 0% of the time, Pallas kernels for 5%

profile of v2, /device:TPU:0, one launch (start us, length us, event | category | flops | bytes accessed | tf_op | source)
XLA Modules:
  0.0 44.9 jit_solution(8474959696137189140)
XLA Ops:
  0.0 1.3 %shard_map.64 = (bf16[32,1024]{1,0:T(8,128)(2,1)S(1)}, bf16[32,1024]{1,0:T(8,128)(2,1)S(1)}, bf16[32,1024]{1,0:T(8,128)(2,1)S(1)}, bf16[32,1024]{1,0:T(8,128)(2,...) custom-call(bf16[32,4096]{1,0:T(8,128)(2,1)} %bitcast.4, ...), custom_call_target="tpu_custom_call" | custom-call | tf_op jit(solution)/shard_map/pallas_call | solution.py:243
  1.3 4.1 %collective-permute-start.3 = (bf16[32,1024]{1,0:T(8,128)(2,1)S(1)}, bf16[32,1024]{1,0:T(8,128)(2,1)S(1)}, u32[]{:S(2)}, u32[]{:S(2)}) collective-permute-start(bf16[32,1024]{1,0:T(8,128)(2,1)S(1)} %get-tuple-element.35), channel_id=1, source_target_pairs={{0,4},{1,5},{2,6},{3,7},{4,0},{5,1},{6,2},{7,3},{8,12},{9,13},{10,... | collective-permute-start | bytes 196616 | tf_op jit(solution)/shard_map/ppermute | solution.py:267
  5.4 1.3 %collective-permute-start.4 = (bf16[32,1024]{1,0:T(8,128)(2,1)S(1)}, bf16[32,1024]{1,0:T(8,128)(2,1)S(1)}, u32[]{:S(2)}, u32[]{:S(2)}) collective-permute-start(bf16[32,1024]{1,0:T(8,128)(2,1)S(1)} %get-tuple-element.36), channel_id=1, source_target_pairs={{0,6},{1,7},{2,4},{3,5},{4,2},{5,3},{6,0},{7,1},{8,14},{9,15},{10,... | collective-permute-start | bytes 196616 | tf_op jit(solution)/shard_map/ppermute | solution.py:267
  6.7 0.2 collective-permute-start.5
  7.0 2.8 %collective-permute-start.6 = (bf16[32,1024]{1,0:T(8,128)(2,1)S(1)}, bf16[32,1024]{1,0:T(8,128)(2,1)S(1)}, u32[]{:S(2)}, u32[]{:S(2)}) collective-permute-start(bf16[32,1024]{1,0:T(8,128)(2,1)S(1)} %get-tuple-element.39), channel_id=1, source_target_pairs={{0,4},{1,5},{2,6},{3,7},{4,0},{5,1},{6,2},{7,3},{8,12},{9,13},{10,... | collective-permute-start | bytes 196616 | tf_op jit(solution)/shard_map/ppermute | solution.py:267
  9.8 1.3 %collective-permute-start.7 = (bf16[32,1024]{1,0:T(8,128)(2,1)S(1)}, bf16[32,1024]{1,0:T(8,128)(2,1)S(1)}, u32[]{:S(2)}, u32[]{:S(2)}) collective-permute-start(bf16[32,1024]{1,0:T(8,128)(2,1)S(1)} %get-tuple-element.40), channel_id=1, source_target_pairs={{0,6},{1,7},{2,4},{3,5},{4,2},{5,3},{6,0},{7,1},{8,14},{9,15},{10,... | collective-permute-start | bytes 196616 | tf_op jit(solution)/shard_map/ppermute | solution.py:267
  11.1 0.0 collective-permute-done.3.refs_1_
  11.1 0.6 %collective-permute-start.8 = (bf16[32,1024]{1,0:T(8,128)(2,1)S(1)}, bf16[32,1024]{1,0:T(8,128)(2,1)S(1)}, u32[]{:S(2)}, u32[]{:S(2)}) collective-permute-start(bf16[32,1024]{1,0:T(8,128)(2,1)S(1)} %get-tuple-element.41), channel_id=1, source_target_pairs={{0,2},{1,3},{2,0},{3,1},{4,6},{5,7},{6,4},{7,5},{8,10},{9,11},{10,... | collective-permute-start | bytes 196616 | tf_op jit(solution)/shard_map/ppermute | solution.py:267
  11.7 0.6 %collective-permute-done.4.refs_2_ = bf16[32,1024]{1,0:T(8,128)(2,1)S(1)} collective-permute-done((bf16[32,1024]{1,0:T(8,128)(2,1)S(1)}, bf16[32,1024]{1,0:T(8,128)(2,1)S(1)}, u32[]{:S(2)}, u32[]{:S(2)}) %collective-permute-start.4) | collective-permute-done | bytes 65568 | tf_op jit(solution)/shard_map/ppermute | solution.py:267
  12.3 0.0 collective-permute-done.5.refs_3_
  12.4 3.4 %collective-permute-start.11 = (bf16[128,1024]{1,0:T(8,128)(2,1)S(1)}, bf16[128,1024]{1,0:T(8,128)(2,1)S(1)}, u32[]{:S(2)}, u32[]{:S(2)}) collective-permute-start(bf16[128,1024]{1,0:T(8,128)(2,1)S(1)} %shard_map.65.refs_4_), channel_id=1, source_target_pairs={{0,8},{8,16},{16,24},{1,9},{9,17},{17,25},{2,10},{10,18},{18,26},{... | collective-permute-start | bytes 786440 | tf_op jit(solution)/shard_map/ppermute | solution.py:21
  15.8 0.7 %collective-permute-done.6.refs_1_ = bf16[32,1024]{1,0:T(8,128)(2,1)S(1)} collective-permute-done((bf16[32,1024]{1,0:T(8,128)(2,1)S(1)}, bf16[32,1024]{1,0:T(8,128)(2,1)S(1)}, u32[]{:S(2)}, u32[]{:S(2)}) %collective-permute-start.6) | collective-permute-done | bytes 65568 | tf_op jit(solution)/shard_map/ppermute | solution.py:267
  16.4 0.0 collective-permute-done.7.refs_2_
  16.4 0.3 collective-permute-done.8.refs_3_
  16.8 3.6 %collective-permute-start.13 = (bf16[128,1024]{1,0:T(8,128)(2,1)S(1)}, bf16[128,1024]{1,0:T(8,128)(2,1)S(1)}, u32[]{:S(2)}, u32[]{:S(2)}) collective-permute-start(bf16[128,1024]{1,0:T(8,128)(2,1)S(1)} %shard_map.66.refs_6_), channel_id=1, source_target_pairs={{0,8},{8,16},{16,24},{1,9},{9,17},{17,25},{2,10},{10,18},{18,26},{... | collective-permute-start | bytes 786440 | tf_op jit(solution)/shard_map/ppermute | solution.py:21
  20.4 4.2 %collective-permute-start = (bf16[32,1024]{1,0:T(8,128)(2,1)S(1)}, bf16[32,1024]{1,0:T(8,128)(2,1)S(1)}, u32[]{:S(2)}, u32[]{:S(2)}) collective-permute-start(bf16[32,1024]{1,0:T(8,128)(2,1)S(1)} %get-tuple-element.31), channel_id=1, source_target_pairs={{0,4},{1,5},{2,6},{3,7},{4,0},{5,1},{6,2},{7,3},{8,12},{9,13},{10,... | collective-permute-start | bytes 196616 | tf_op jit(solution)/shard_map/ppermute | solution.py:267
  24.5 0.3 collective-permute-start.1
  24.9 0.3 collective-permute-start.2
  25.2 3.0 %collective-permute-done.refs_1_ = bf16[32,1024]{1,0:T(8,128)(2,1)S(1)} collective-permute-done((bf16[32,1024]{1,0:T(8,128)(2,1)S(1)}, bf16[32,1024]{1,0:T(8,128)(2,1)S(1)}, u32[]{:S(2)}, u32[]{:S(2)}) %collective-permute-start) | collective-permute-done | bytes 65568 | tf_op jit(solution)/shard_map/ppermute | solution.py:267
  28.2 2.4 %collective-permute-done.1.refs_2_ = bf16[32,1024]{1,0:T(8,128)(2,1)S(1)} collective-permute-done((bf16[32,1024]{1,0:T(8,128)(2,1)S(1)}, bf16[32,1024]{1,0:T(8,128)(2,1)S(1)}, u32[]{:S(2)}, u32[]{:S(2)}) %collective-permute-start.1) | collective-permute-done | bytes 65568 | tf_op jit(solution)/shard_map/ppermute | solution.py:267
  30.6 0.0 collective-permute-done.2.refs_3_
  30.6 0.0 collective-permute-start.10
  30.6 0.5 %collective-permute-start.9 = (bf16[128,1024]{1,0:T(8,128)(2,1)S(1)}, bf16[128,1024]{1,0:T(8,128)(2,1)S(1)}, u32[]{:S(2)}, u32[]{:S(2)}) collective-permute-start(bf16[128,1024]{1,0:T(8,128)(2,1)S(1)} %shard_map.65.refs_4_), channel_id=1, source_target_pairs={{0,1},{1,0},{2,3},{3,2},{4,5},{5,4},{6,7},{7,6},{8,9},{9,8},{10,11... | collective-permute-start | bytes 786440 | tf_op jit(solution)/shard_map/ppermute | solution.py:272
  31.1 0.0 collective-permute-done.11.refs_8_
  31.1 0.0 collective-permute-start.12
  31.1 0.0 collective-permute-done.13.refs_0_
  31.1 0.5 %collective-permute-start.14 = (bf16[128,1024]{1,0:T(8,128)(2,1)S(1)}, bf16[128,1024]{1,0:T(8,128)(2,1)S(1)}, u32[]{:S(2)}, u32[]{:S(2)}) collective-permute-start(bf16[128,1024]{1,0:T(8,128)(2,1)S(1)} %collective-permute-done.13.refs_0_), channel_id=1, source_target_pairs={{0,1},{1,0},{2,3},{3,2},{4,5},{5,4},{6,7},{7,6},{8,9},{9,8},{10,11... | collective-permute-start | bytes 786440 | tf_op jit(solution)/shard_map/ppermute | solution.py:272
  32.9 0.0 copy-start
  33.0 0.0 collective-permute-done.10.refs_7_
  33.0 0.0 collective-permute-done.9.refs_5_
  33.0 0.0 collective-permute-done.12.refs_9_
  33.0 2.1 %shard_map.67 = (bf16[8,128,256]{2,1,0:T(8,128)(2,1)S(1)}, f32[8,128,1]{2,1,0:T(8,128)S(1)}, f32[128,1024]{1,0:T(8,128)S(1)}) custom-call(s32[1]{0:T(128)S(6)} %copy.7.cache_ref, bf16[32,1024]{1,0:T(8,128)(2,1)S(1)} %get-tuple-element.42.refs_0_, bf16[32,1024]{1,0:T(8,128)(2,1)S(1)} %collective-permute-done.refs_1_, ...), custom_call_target="tpu_custom_call" | custom-call | tf_op jit(solution)/shard_map/pallas_call | solution.py:243
  35.1 0.0 collective-permute-done.14.refs_1_
  35.2 0.0 copy-done
  35.2 0.3 shard_map.68
  35.5 1.3 %collective-permute-start.15 = (bf16[32,1024]{1,0:T(8,128)(2,1)S(1)}, bf16[32,1024]{1,0:T(8,128)(2,1)S(1)}, u32[]{:S(2)}, u32[]{:S(2)}) collective-permute-start(bf16[32,1024]{1,0:T(8,128)(2,1)S(1)} %get-tuple-element.52), channel_id=1, source_target_pairs={{0,4},{1,5},{2,6},{3,7},{4,0},{5,1},{6,2},{7,3},{8,12},{9,13},{10,... | collective-permute-start | bytes 196616 | tf_op jit(solution)/shard_map/ppermute | solution.py:267
  36.8 0.8 %collective-permute-start.16 = (bf16[32,1024]{1,0:T(8,128)(2,1)S(1)}, bf16[32,1024]{1,0:T(8,128)(2,1)S(1)}, u32[]{:S(2)}, u32[]{:S(2)}) collective-permute-start(bf16[32,1024]{1,0:T(8,128)(2,1)S(1)} %get-tuple-element.53), channel_id=1, source_target_pairs={{0,6},{1,7},{2,4},{3,5},{4,2},{5,3},{6,0},{7,1},{8,14},{9,15},{10,... | collective-permute-start | bytes 196616 | tf_op jit(solution)/shard_map/ppermute | solution.py:267
  37.7 1.4 %collective-permute-start.17 = (bf16[32,1024]{1,0:T(8,128)(2,1)S(1)}, bf16[32,1024]{1,0:T(8,128)(2,1)S(1)}, u32[]{:S(2)}, u32[]{:S(2)}) collective-permute-start(bf16[32,1024]{1,0:T(8,128)(2,1)S(1)} %get-tuple-element.54), channel_id=1, source_target_pairs={{0,2},{1,3},{2,0},{3,1},{4,6},{5,7},{6,4},{7,5},{8,10},{9,11},{10,... | collective-permute-start | bytes 196616 | tf_op jit(solution)/shard_map/ppermute | solution.py:267
  39.1 3.1 %collective-permute-done.15.refs_1_ = bf16[32,1024]{1,0:T(8,128)(2,1)S(1)} collective-permute-done((bf16[32,1024]{1,0:T(8,128)(2,1)S(1)}, bf16[32,1024]{1,0:T(8,128)(2,1)S(1)}, u32[]{:S(2)}, u32[]{:S(2)}) %collective-permute-start.15) | collective-permute-done | bytes 65568 | tf_op jit(solution)/shard_map/ppermute | solution.py:267
  42.2 1.0 %collective-permute-done.16.refs_2_ = bf16[32,1024]{1,0:T(8,128)(2,1)S(1)} collective-permute-done((bf16[32,1024]{1,0:T(8,128)(2,1)S(1)}, bf16[32,1024]{1,0:T(8,128)(2,1)S(1)}, u32[]{:S(2)}, u32[]{:S(2)}) %collective-permute-start.16) | collective-permute-done | bytes 65568 | tf_op jit(solution)/shard_map/ppermute | solution.py:267
  43.2 1.0 %collective-permute-done.17.refs_3_ = bf16[32,1024]{1,0:T(8,128)(2,1)S(1)} collective-permute-done((bf16[32,1024]{1,0:T(8,128)(2,1)S(1)}, bf16[32,1024]{1,0:T(8,128)(2,1)S(1)}, u32[]{:S(2)}, u32[]{:S(2)}) %collective-permute-start.17) | collective-permute-done | bytes 65568 | tf_op jit(solution)/shard_map/ppermute | solution.py:267
  44.2 0.7 %shard_map.69 = bf16[32,4096]{1,0:T(8,128)(2,1)} custom-call(bf16[32,1024]{1,0:T(8,128)(2,1)S(1)} %get-tuple-element.51.refs_0_, bf16[32,1024]{1,0:T(8,128)(2,1)S(1)} %collective-permute-done.15.refs_1_, bf16[32,1024]{1,0:T(8,128)(2,1)S(1)} %collective-permute-done.16.refs_2_, bf16[32,1024]{1,0:T(8,128)(2,1)S(1)} %collective-permute-done.17.refs_3_), custom_call_target="tpu_custom_call" | custom-call | tf_op jit(solution)/shard_map/pallas_call | solution.py:317
  (2 shorter events, 0.0 us)
Async XLA Ops:
  1.3 9.8 %collective-permute-start.3 = (bf16[32,1024]{1,0:T(8,128)(2,1)S(1)}, bf16[32,1024]{1,0:T(8,128)(2,1)S(1)}, u32[]{:S(2)}, u32[]{:S(2)}) collective-permute-start(bf16[32,1024]{1,0:T(8,128)(2,1)S(1)} %get-tuple-element.35), channel_id=1, source_target_pairs={{0,4},{1,5},{2,6},{3,7},{4,0},{5,1},{6,2},{7,3},{8,12},{9,13},{10,... | collective-permute-start | bytes 196616 | tf_op jit(solution)/shard_map/ppermute | solution.py:267
  5.4 7.0 %collective-permute-start.4 = (bf16[32,1024]{1,0:T(8,128)(2,1)S(1)}, bf16[32,1024]{1,0:T(8,128)(2,1)S(1)}, u32[]{:S(2)}, u32[]{:S(2)}) collective-permute-start(bf16[32,1024]{1,0:T(8,128)(2,1)S(1)} %get-tuple-element.36), channel_id=1, source_target_pairs={{0,6},{1,7},{2,4},{3,5},{4,2},{5,3},{6,0},{7,1},{8,14},{9,15},{10,... | collective-permute-start | bytes 196616 | tf_op jit(solution)/shard_map/ppermute | solution.py:267
  6.7 5.6 %collective-permute-start.5 = (bf16[32,1024]{1,0:T(8,128)(2,1)S(1)}, bf16[32,1024]{1,0:T(8,128)(2,1)S(1)}, u32[]{:S(2)}, u32[]{:S(2)}) collective-permute-start(bf16[32,1024]{1,0:T(8,128)(2,1)S(1)} %get-tuple-element.37), channel_id=1, source_target_pairs={{0,2},{1,3},{2,0},{3,1},{4,6},{5,7},{6,4},{7,5},{8,10},{9,11},{10,... | collective-permute-start | bytes 196616 | tf_op jit(solution)/shard_map/ppermute | solution.py:267
  7.0 9.5 %collective-permute-start.6 = (bf16[32,1024]{1,0:T(8,128)(2,1)S(1)}, bf16[32,1024]{1,0:T(8,128)(2,1)S(1)}, u32[]{:S(2)}, u32[]{:S(2)}) collective-permute-start(bf16[32,1024]{1,0:T(8,128)(2,1)S(1)} %get-tuple-element.39), channel_id=1, source_target_pairs={{0,4},{1,5},{2,6},{3,7},{4,0},{5,1},{6,2},{7,3},{8,12},{9,13},{10,... | collective-permute-start | bytes 196616 | tf_op jit(solution)/shard_map/ppermute | solution.py:267
  9.8 6.7 %collective-permute-start.7 = (bf16[32,1024]{1,0:T(8,128)(2,1)S(1)}, bf16[32,1024]{1,0:T(8,128)(2,1)S(1)}, u32[]{:S(2)}, u32[]{:S(2)}) collective-permute-start(bf16[32,1024]{1,0:T(8,128)(2,1)S(1)} %get-tuple-element.40), channel_id=1, source_target_pairs={{0,6},{1,7},{2,4},{3,5},{4,2},{5,3},{6,0},{7,1},{8,14},{9,15},{10,... | collective-permute-start | bytes 196616 | tf_op jit(solution)/shard_map/ppermute | solution.py:267
  11.1 5.6 %collective-permute-start.8 = (bf16[32,1024]{1,0:T(8,128)(2,1)S(1)}, bf16[32,1024]{1,0:T(8,128)(2,1)S(1)}, u32[]{:S(2)}, u32[]{:S(2)}) collective-permute-start(bf16[32,1024]{1,0:T(8,128)(2,1)S(1)} %get-tuple-element.41), channel_id=1, source_target_pairs={{0,2},{1,3},{2,0},{3,1},{4,6},{5,7},{6,4},{7,5},{8,10},{9,11},{10,... | collective-permute-start | bytes 196616 | tf_op jit(solution)/shard_map/ppermute | solution.py:267
  12.4 18.8 %collective-permute-start.11 = (bf16[128,1024]{1,0:T(8,128)(2,1)S(1)}, bf16[128,1024]{1,0:T(8,128)(2,1)S(1)}, u32[]{:S(2)}, u32[]{:S(2)}) collective-permute-start(bf16[128,1024]{1,0:T(8,128)(2,1)S(1)} %shard_map.65.refs_4_), channel_id=1, source_target_pairs={{0,8},{8,16},{16,24},{1,9},{9,17},{17,25},{2,10},{10,18},{18,26},{... | collective-permute-start | bytes 786440 | tf_op jit(solution)/shard_map/ppermute | solution.py:21
  16.8 14.4 %collective-permute-start.13 = (bf16[128,1024]{1,0:T(8,128)(2,1)S(1)}, bf16[128,1024]{1,0:T(8,128)(2,1)S(1)}, u32[]{:S(2)}, u32[]{:S(2)}) collective-permute-start(bf16[128,1024]{1,0:T(8,128)(2,1)S(1)} %shard_map.66.refs_6_), channel_id=1, source_target_pairs={{0,8},{8,16},{16,24},{1,9},{9,17},{17,25},{2,10},{10,18},{18,26},{... | collective-permute-start | bytes 786440 | tf_op jit(solution)/shard_map/ppermute | solution.py:21
  20.4 7.8 %collective-permute-start = (bf16[32,1024]{1,0:T(8,128)(2,1)S(1)}, bf16[32,1024]{1,0:T(8,128)(2,1)S(1)}, u32[]{:S(2)}, u32[]{:S(2)}) collective-permute-start(bf16[32,1024]{1,0:T(8,128)(2,1)S(1)} %get-tuple-element.31), channel_id=1, source_target_pairs={{0,4},{1,5},{2,6},{3,7},{4,0},{5,1},{6,2},{7,3},{8,12},{9,13},{10,... | collective-permute-start | bytes 196616 | tf_op jit(solution)/shard_map/ppermute | solution.py:267
  24.5 6.1 %collective-permute-start.1 = (bf16[32,1024]{1,0:T(8,128)(2,1)S(1)}, bf16[32,1024]{1,0:T(8,128)(2,1)S(1)}, u32[]{:S(2)}, u32[]{:S(2)}) collective-permute-start(bf16[32,1024]{1,0:T(8,128)(2,1)S(1)} %get-tuple-element.32), channel_id=1, source_target_pairs={{0,6},{1,7},{2,4},{3,5},{4,2},{5,3},{6,0},{7,1},{8,14},{9,15},{10,... | collective-permute-start | bytes 196616 | tf_op jit(solution)/shard_map/ppermute | solution.py:267
  24.9 5.8 %collective-permute-start.2 = (bf16[32,1024]{1,0:T(8,128)(2,1)S(1)}, bf16[32,1024]{1,0:T(8,128)(2,1)S(1)}, u32[]{:S(2)}, u32[]{:S(2)}) collective-permute-start(bf16[32,1024]{1,0:T(8,128)(2,1)S(1)} %get-tuple-element.33), channel_id=1, source_target_pairs={{0,2},{1,3},{2,0},{3,1},{4,6},{5,7},{6,4},{7,5},{8,10},{9,11},{10,... | collective-permute-start | bytes 196616 | tf_op jit(solution)/shard_map/ppermute | solution.py:267
  30.6 2.3 %collective-permute-start.10 = (bf16[128,1024]{1,0:T(8,128)(2,1)S(1)}, bf16[128,1024]{1,0:T(8,128)(2,1)S(1)}, u32[]{:S(2)}, u32[]{:S(2)}) collective-permute-start(bf16[128,1024]{1,0:T(8,128)(2,1)S(1)} %shard_map.66.refs_6_), channel_id=1, source_target_pairs={{0,1},{1,0},{2,3},{3,2},{4,5},{5,4},{6,7},{7,6},{8,9},{9,8},{10,11... | collective-permute-start | bytes 786440 | tf_op jit(solution)/shard_map/ppermute | solution.py:272
  30.6 2.4 %collective-permute-start.9 = (bf16[128,1024]{1,0:T(8,128)(2,1)S(1)}, bf16[128,1024]{1,0:T(8,128)(2,1)S(1)}, u32[]{:S(2)}, u32[]{:S(2)}) collective-permute-start(bf16[128,1024]{1,0:T(8,128)(2,1)S(1)} %shard_map.65.refs_4_), channel_id=1, source_target_pairs={{0,1},{1,0},{2,3},{3,2},{4,5},{5,4},{6,7},{7,6},{8,9},{9,8},{10,11... | collective-permute-start | bytes 786440 | tf_op jit(solution)/shard_map/ppermute | solution.py:272
  31.1 1.8 %collective-permute-start.12 = (bf16[128,1024]{1,0:T(8,128)(2,1)S(1)}, bf16[128,1024]{1,0:T(8,128)(2,1)S(1)}, u32[]{:S(2)}, u32[]{:S(2)}) collective-permute-start(bf16[128,1024]{1,0:T(8,128)(2,1)S(1)} %collective-permute-done.11.refs_8_), channel_id=1, source_target_pairs={{0,1},{1,0},{2,3},{3,2},{4,5},{5,4},{6,7},{7,6},{8,9},{9,8},{10,11... | collective-permute-start | bytes 786440 | tf_op jit(solution)/shard_map/ppermute | solution.py:272
  31.1 4.0 %collective-permute-start.14 = (bf16[128,1024]{1,0:T(8,128)(2,1)S(1)}, bf16[128,1024]{1,0:T(8,128)(2,1)S(1)}, u32[]{:S(2)}, u32[]{:S(2)}) collective-permute-start(bf16[128,1024]{1,0:T(8,128)(2,1)S(1)} %collective-permute-done.13.refs_0_), channel_id=1, source_target_pairs={{0,1},{1,0},{2,3},{3,2},{4,5},{5,4},{6,7},{7,6},{8,9},{9,8},{10,11... | collective-permute-start | bytes 786440 | tf_op jit(solution)/shard_map/ppermute | solution.py:272
  32.9 2.2 %copy-start = (f32[50,4096]{1,0:T(8,128)S(1)}, f32[50,4096]{1,0:T(8,128)}, u32[]{:S(2)}) copy-start(f32[50,4096]{1,0:T(8,128)} %refs_2_.1) | copy-start | bytes 2457604
  35.5 6.7 %collective-permute-start.15 = (bf16[32,1024]{1,0:T(8,128)(2,1)S(1)}, bf16[32,1024]{1,0:T(8,128)(2,1)S(1)}, u32[]{:S(2)}, u32[]{:S(2)}) collective-permute-start(bf16[32,1024]{1,0:T(8,128)(2,1)S(1)} %get-tuple-element.52), channel_id=1, source_target_pairs={{0,4},{1,5},{2,6},{3,7},{4,0},{5,1},{6,2},{7,3},{8,12},{9,13},{10,... | collective-permute-start | bytes 196616 | tf_op jit(solution)/shard_map/ppermute | solution.py:267
  36.8 6.3 %collective-permute-start.16 = (bf16[32,1024]{1,0:T(8,128)(2,1)S(1)}, bf16[32,1024]{1,0:T(8,128)(2,1)S(1)}, u32[]{:S(2)}, u32[]{:S(2)}) collective-permute-start(bf16[32,1024]{1,0:T(8,128)(2,1)S(1)} %get-tuple-element.53), channel_id=1, source_target_pairs={{0,6},{1,7},{2,4},{3,5},{4,2},{5,3},{6,0},{7,1},{8,14},{9,15},{10,... | collective-permute-start | bytes 196616 | tf_op jit(solution)/shard_map/ppermute | solution.py:267
  37.7 6.5 %collective-permute-start.17 = (bf16[32,1024]{1,0:T(8,128)(2,1)S(1)}, bf16[32,1024]{1,0:T(8,128)(2,1)S(1)}, u32[]{:S(2)}, u32[]{:S(2)}) collective-permute-start(bf16[32,1024]{1,0:T(8,128)(2,1)S(1)} %get-tuple-element.54), channel_id=1, source_target_pairs={{0,2},{1,3},{2,0},{3,1},{4,6},{5,7},{6,4},{7,5},{8,10},{9,11},{10,... | collective-permute-start | bytes 196616 | tf_op jit(solution)/shard_map/ppermute | solution.py:267

commit v3 on v2

--- a/solution.py
+++ b/solution.py
@@ -1,3 +1,4 @@
+import functools
 import math
 
 import jax
@@ -108,44 +109,46 @@
     return attn_out
 
 
-def chips_of(seq):
-    return seq // 2
-
-
-def steps_of(chips):
-    return [step for step in range(1, chips) if step >= chips // 2] + list(range(1, chips // 2))
+CHIPS = 4
+STEPS_IN = (3, 1, 2)
+STEPS_OUT = (3, 2, 1)
+QUERY_SHARES = ((2,), (1, 3))
 
 
 def span_of(chip, width):
     return pl.ds(pl.multiple_of(chip * width, width), width)
 
 
-def pack_kernel(*refs):
-    whole, parts, sems = refs[:3], refs[3:-1], refs[-1]
-    chips = len(parts) // 3
-    chip = lax.axis_index("seq") // 2
-    copies = []
-    for index, ref in enumerate(whole):
-        width = ref.shape[1] // chips
-        for place, step in enumerate([0] + steps_of(chips)):
-            copies.append(
-                pltpu.make_async_copy(
-                    ref.at[:, span_of(chip ^ step, width)],
-                    parts[index * chips + place],
-                    sems.at[index * chips + place],
-                )
-            )
+def run_copies(copies):
     for copy in copies:
         copy.start()
     for copy in copies:
         copy.wait()
 
 
-def join_kernel(*refs):
+def pack_kernel(cuts, *refs):
+    whole, parts, sems = refs[:3], refs[3:-1], refs[-1]
+    rows = whole[0].shape[0]
+    width = parts[0].shape[1]
+    chip = lax.axis_index("seq") // 2
+    copies = []
+    for part, (index, steps) in zip(parts, cuts):
+        for place, step in enumerate(steps):
+            copies.append(
+                pltpu.make_async_copy(
+                    whole[index].at[:, span_of(chip ^ step, width)],
+                    part.at[pl.ds(place * rows, rows)],
+                    sems.at[len(copies)],
+                )
+            )
+    run_copies(copies)
+
+
+def join_kernel(places, *refs):
     parts, out_ref = refs[:-1], refs[-1]
-    rows = parts[0].shape[0]
-    for place, part in enumerate(parts):
-        out_ref[pl.ds(place * rows, rows)] = part[...]
+    rows = out_ref.shape[0] // len(parts)
+    for part, (to, place) in zip(parts, places):
+        out_ref[pl.ds(to * rows, rows)] = part[pl.ds(place * rows, rows)]
 
 
 def product(left, right, dims):
@@ -153,17 +156,17 @@
 
 
 def weigh_kernel(cache_ref, *refs):
-    chips = len(refs) - 9
-    queries, refs = refs[:chips], refs[chips:]
+    queries, refs = refs[0], refs[1:]
+    chips = CHIPS
     key_refs, value_refs, past_refs = refs[0:2], refs[2:4], refs[4:6]
     past_weight_ref, total_ref, numer_ref = refs[6:9]
-    rows, width = queries[0].shape
-    half = chips * rows
+    half, width = queries.shape
+    rows = half // chips
     tokens = 2 * half
     core = lax.rem(lax.axis_index("seq"), 2)
     chip = lax.axis_index("seq") // 2
     seen_from = jnp.where(lax.axis_index("stretch") > 0, cache_ref[0], tokens)
-    steps = [0] + steps_of(chips)
+    steps = range(chips)
     lane = lax.broadcasted_iota(jnp.int32, (1, rows), 1)
     position = jnp.concatenate(
         [
@@ -174,22 +177,37 @@
         axis=1,
     )
     visible = position >= seen_from
-    scale = HD ** (-0.5)
-    for head in range(width // HD):
+    scale = HD ** (-0.5) * math.log2(math.e)
+
+    def scores(head):
         lanes = pl.ds(head * HD, HD)
-        query = jnp.concatenate([ref[:, lanes] for ref in queries], axis=0)
+        query = queries[:, lanes]
         key = jnp.concatenate([ref[:, lanes] for ref in key_refs], axis=0)
         value = jnp.concatenate([ref[:, lanes] for ref in value_refs], axis=0)
         past_key = jnp.concatenate([ref[:, lanes] for ref in past_refs], axis=0)
-        own = product(query, key, ((1,), (1,))) * scale
-        past = product(query, past_key, ((1,), (1,))) * scale
+        own = product(query, key, ((1,), (1,)))
+        past = product(query, past_key, ((1,), (1,)))
+        return own, past, value
+
+    def mix(head, own, value):
+        numer_ref[:, pl.ds(head * HD, HD)] = product(own, value, ((1,), (0,)))
+
+    heads = width // HD
+    ready, weighed = scores(0), None
+    for head in range(heads):
+        own, past, value = ready
+        if head + 1 < heads:
+            ready = scores(head + 1)
+        if weighed is not None:
+            mix(*weighed)
         past = jnp.where(visible, past, -1e30)
         largest = jnp.max(jnp.maximum(own, past), axis=1, keepdims=True)
-        own = jnp.exp(own - largest)
-        past = jnp.exp(past - largest)
+        own = jnp.exp2((own - largest) * scale)
+        past = jnp.exp2((past - largest) * scale)
         total_ref[head] = jnp.sum(own + past, axis=1, keepdims=True)
-        numer_ref[:, lanes] = product(own.astype(jnp.bfloat16), value, ((1,), (0,)))
         past_weight_ref[head] = past.astype(jnp.bfloat16)
+        weighed = (head, own.astype(jnp.bfloat16), value)
+    mix(*weighed)
 
 
 def finish_kernel(time_ref, past_weight_ref, total_ref, numer_ref, *refs):
@@ -214,17 +232,14 @@
 
 def unpack_kernel(*refs):
     parts, out_ref, sems = refs[:-2], refs[-2], refs[-1]
-    chips = len(parts)
     chip = lax.axis_index("seq") // 2
     width = parts[0].shape[1]
-    copies = [
-        pltpu.make_async_copy(part, out_ref.at[:, span_of(chip ^ step, width)], sems.at[place])
-        for place, (part, step) in enumerate(zip(parts, [0] + steps_of(chips)))
-    ]
-    for copy in copies:
-        copy.start()
-    for copy in copies:
-        copy.wait()
+    run_copies(
+        [
+            pltpu.make_async_copy(part, out_ref.at[:, span_of(chip ^ step, width)], sems.at[place])
+            for place, (part, step) in enumerate(zip(parts, (0, *STEPS_OUT)))
+        ]
+    )
 
 
 def kernel_call(kernel, ins, outs, scratch=(), work=0):
@@ -252,46 +267,55 @@
     return run
 
 
+def after(value, *others):
+    return lax.optimization_barrier((value, others))[0]
+
+
 def chip_body(query_rows, key_rows, value_rows, cache_from, time_index, gate_table):
     seq = lax.axis_size("seq")
-    chips = chips_of(seq)
     rows = query_rows.shape[1]
-    width = HEADS * HD // chips
-    half = chips * rows
-    steps = steps_of(chips)
-    block = jax.ShapeDtypeStruct((rows, width), jnp.bfloat16)
-    joined = jax.ShapeDtypeStruct((half, width), jnp.bfloat16)
-
-    def between_chips(parts):
-        return [parts[0]] + [
-            lax.ppermute(part, "seq", [(i, i ^ (2 * step)) for i in range(seq)])
-            for part, step in zip(parts[1:], steps)
-        ]
-
-    def between_cores(part):
+    width = HEADS * HD // CHIPS
+    half = CHIPS * rows
+    per_dev = width // HD
+
+    def block(count):
+        return jax.ShapeDtypeStruct((count * rows, width), jnp.bfloat16)
+
+    def with_chip(part, step):
+        return lax.ppermute(part, "seq", [(i, i ^ (2 * step)) for i in range(seq)])
+
+    def with_core(part):
         return lax.ppermute(part, "seq", [(i, i ^ 1) for i in range(seq)])
 
-    def join(parts):
-        return kernel_call(join_kernel, [VMEM] * chips, joined)(*parts)
-
+    def join(parts, places, work=0):
+        kernel = functools.partial(join_kernel, places)
+        return kernel_call(kernel, [VMEM] * len(parts), block(len(parts)), work=work)(*parts)
+
+    cuts = [(index, (step,)) for index in range(2) for step in (0, *STEPS_IN)]
+    cuts += [(2, (0,))] + [(2, steps) for steps in QUERY_SHARES]
     parts = kernel_call(
-        pack_kernel,
+        functools.partial(pack_kernel, cuts),
         [HBM] * 3,
-        (block,) * (3 * chips),
-        scratch=[pltpu.SemaphoreType.DMA((3 * chips,))],
-    )(
-        key_rows[0], value_rows[0], query_rows[0]
-    )
-    keys = join(between_chips(parts[:chips]))
+        tuple(block(len(steps)) for _, steps in cuts),
+        scratch=[pltpu.SemaphoreType.DMA((3 * CHIPS,))],
+    )(key_rows[0], value_rows[0], query_rows[0])
+    key_parts, value_parts, query_parts = parts[:CHIPS], parts[CHIPS:2 * CHIPS], parts[2 * CHIPS:]
+
+    def gathered(parts, work=0):
+        got = [parts[0]] + [with_chip(part, step) for part, step in zip(parts[1:], STEPS_IN)]
+        return join(got, [(step, 0) for step in (0, *STEPS_IN)], work)
+
+    keys = gathered(key_parts)
+    values = gathered(value_parts)
     past_keys = passed_along(keys, "stretch", 1)
-    values = join(between_chips(parts[chips:2 * chips]))
     past_values = passed_along(values, "stretch", 1)
-    queries = between_chips(parts[2 * chips:])
-    queries, keys, values = lax.optimization_barrier((queries, keys, values))
-    per_dev = width // HD
+    own_query, two_on, near = query_parts
+    near = with_chip(near, 1)
+    far = with_chip(join([after(two_on, values), near], [(0, 0), (1, 1)]), 2)
+    queries = join([own_query, near, far, far], [(0, 0), (1, 0), (2, 0), (3, 1)])
     past_weight, total, numer = kernel_call(
         weigh_kernel,
-        [SMEM] + [VMEM] * (chips + 6),
+        [SMEM] + [VMEM] * 7,
         (
             jax.ShapeDtypeStruct((per_dev, half, 2 * half), jnp.bfloat16),
             jax.ShapeDtypeStruct((per_dev, half, 1), jnp.float32),
@@ -299,34 +323,41 @@
         ),
     )(
         cache_from,
-        *queries,
+        queries,
         keys,
-        between_cores(keys),
+        with_core(keys),
         values,
-        between_cores(values),
+        with_core(values),
         past_keys,
-        between_cores(past_keys),
+        with_core(after(past_keys, far)),
     )
     outs = kernel_call(
         finish_kernel,
         [SMEM] + [VMEM] * 5 + [ANY],
-        (block,) * chips,
+        (block(1),) * CHIPS,
         scratch=[pltpu.VMEM((1, width), jnp.float32), pltpu.SemaphoreType.DMA],
-    )(time_index, past_weight, total, numer, past_values, between_cores(past_values), gate_table)
-    returned = between_chips(outs)
+    )(
+        time_index,
+        past_weight,
+        total,
+        numer,
+        past_values,
+        with_core(after(past_values, far)),
+        gate_table,
+    )
+    returned = [outs[0]] + [with_chip(outs[step], step) for step in STEPS_OUT]
     out = pl.pallas_call(
         unpack_kernel,
         out_shape=jax.ShapeDtypeStruct((rows, HEADS * HD), jnp.bfloat16),
-        in_specs=[VMEM] * chips,
+        in_specs=[VMEM] * CHIPS,
         out_specs=ANY,
-        scratch_shapes=[pltpu.SemaphoreType.DMA((chips,))],
+        scratch_shapes=[pltpu.SemaphoreType.DMA((CHIPS,))],
     )(*(pltpu.with_memory_space_constraint(part, pltpu.VMEM) for part in returned))
     return out[None]
 
 
 def solution(mesh):
-    chips = chips_of(mesh.shape["seq"])
-    by_chip = HEADS % chips == 0 and chips & (chips - 1) == 0
+    by_chip = mesh.shape["seq"] == 2 * CHIPS
     return jax.shard_map(
         chip_body if by_chip else general_body,
         mesh=mesh,

time: 45.1 us -> 41.7 us (0.925)
  waiting for transfers between devices: 12.1 us -> 10.4 us
  Pallas kernels: 4.52 us -> 3.42 us
  starting transfers between devices: 26.9 us -> 26 us
    ppermute x16 -> x15, waiting for transfers between devices: 12.1 us -> 10.4 us  [the longest x11 10.4 us: with_chip(): return lax.ppermute(part, 'seq', [(i, i ^ 2 * step) for i in range(seq)])]
    pallas_call x5 -> x7, Pallas kernels: 3.79 us -> 2.69 us  [run(): call(*(pltpu.with_memory_space_constraint(operand, spec.memory_space) if...]
    ppermute x16 -> x15, starting transfers between devices: 19.8 us -> 19.2 us  [the longest x11 18.2 us: with_chip(): return lax.ppermute(part, 'seq', [(i, i ^ 2 * step) for i in range(seq)])]
  transfers between devices with their start and end apart: 18 -> 17, of which waited for: 8 -> 4; matrix products, arithmetic and copies ran while one was open for 0% -> 0% of each run, Pallas kernels for 5% -> 3%
where the time goes in v3:
time: 41.7 us; the launch traced here: 41.4 us
  starting transfers between devices  26 us (62%)
  waiting for transfers between devices  10.4 us (25%)
  Pallas kernels  3.42 us (8%)
  between operations  1.45 us (3%)
    ppermute x11, starting transfers between devices, with_chip(): return lax.ppermute(part, 'seq', [(i, i ^ 2 * step) for i in range(seq)])  18.2 us
    ppermute x11, waiting for transfers between devices, with_chip(): return lax.ppermute(part, 'seq', [(i, i ^ 2 * step) for i in range(seq)])  10.4 us
    ppermute x2, starting transfers between devices, passed_along(): return lax.ppermute(block, axis, route)  6.81 us
    pallas_call x7, Pallas kernels, run(): call(*(pltpu.with_memory_space_constraint(operand, spec.memory_space) if...  2.69 us
    ppermute x4, starting transfers between devices, with_core(): return lax.ppermute(part, 'seq', [(i, i ^ 1) for i in range(seq)])  1.02 us
  transfers between devices with their start and end apart: 17, of which 4 were waited for; matrix products, arithmetic and copies ran while one was open for 0% of the time, Pallas kernels for 3%

profile of v3, /device:TPU:0, one launch (start us, length us, event | category | flops | bytes accessed | tf_op | source)
XLA Modules:
  0.0 41.4 jit_solution(8919864802594765993)
XLA Ops:
  0.0 1.3 %shard_map.64 = (bf16[32,1024]{1,0:T(8,128)(2,1)S(1)}, bf16[32,1024]{1,0:T(8,128)(2,1)S(1)}, bf16[32,1024]{1,0:T(8,128)(2,1)S(1)}, bf16[32,1024]{1,0:T(8,128)(2,...) custom-call(bf16[32,4096]{1,0:T(8,128)(2,1)} %bitcast.4, ...), custom_call_target="tpu_custom_call" | custom-call | tf_op jit(solution)/shard_map/pallas_call | solution.py:258
  1.3 5.1 %collective-permute-start.5 = (bf16[32,1024]{1,0:T(8,128)(2,1)S(1)}, bf16[32,1024]{1,0:T(8,128)(2,1)S(1)}, u32[]{:S(2)}, u32[]{:S(2)}) collective-permute-start(bf16[32,1024]{1,0:T(8,128)(2,1)S(1)} %get-tuple-element.35), channel_id=1, source_target_pairs={{0,6},{1,7},{2,4},{3,5},{4,2},{5,3},{6,0},{7,1},{8,14},{9,15},{10,... | collective-permute-start | bytes 196616 | tf_op jit(solution)/shard_map/ppermute | solution.py:285
  6.4 0.0 collective-permute-start.6
  6.4 0.6 %collective-permute-start.7 = (bf16[32,1024]{1,0:T(8,128)(2,1)S(1)}, bf16[32,1024]{1,0:T(8,128)(2,1)S(1)}, u32[]{:S(2)}, u32[]{:S(2)}) collective-permute-start(bf16[32,1024]{1,0:T(8,128)(2,1)S(1)} %get-tuple-element.37), channel_id=1, source_target_pairs={{0,4},{1,5},{2,6},{3,7},{4,0},{5,1},{6,2},{7,3},{8,12},{9,13},{10,... | collective-permute-start | bytes 196616 | tf_op jit(solution)/shard_map/ppermute | solution.py:285
  7.0 3.7 %collective-permute-start.1 = (bf16[32,1024]{1,0:T(8,128)(2,1)S(1)}, bf16[32,1024]{1,0:T(8,128)(2,1)S(1)}, u32[]{:S(2)}, u32[]{:S(2)}) collective-permute-start(bf16[32,1024]{1,0:T(8,128)(2,1)S(1)} %get-tuple-element.30), channel_id=1, source_target_pairs={{0,6},{1,7},{2,4},{3,5},{4,2},{5,3},{6,0},{7,1},{8,14},{9,15},{10,... | collective-permute-start | bytes 196616 | tf_op jit(solution)/shard_map/ppermute | solution.py:285
  10.8 0.0 collective-permute-start.2
  10.8 0.0 collective-permute-done.5.refs_1_
  10.8 0.6 %collective-permute-start.3 = (bf16[32,1024]{1,0:T(8,128)(2,1)S(1)}, bf16[32,1024]{1,0:T(8,128)(2,1)S(1)}, u32[]{:S(2)}, u32[]{:S(2)}) collective-permute-start(bf16[32,1024]{1,0:T(8,128)(2,1)S(1)} %get-tuple-element.32), channel_id=1, source_target_pairs={{0,4},{1,5},{2,6},{3,7},{4,0},{5,1},{6,2},{7,3},{8,12},{9,13},{10,... | collective-permute-start | bytes 196616 | tf_op jit(solution)/shard_map/ppermute | solution.py:285
  11.4 0.0 collective-permute-done.6.refs_2_
  11.4 2.3 %collective-permute-start = (bf16[64,1024]{1,0:T(8,128)(2,1)S(1)}, bf16[64,1024]{1,0:T(8,128)(2,1)S(1)}, u32[]{:S(2)}, u32[]{:S(2)}) collective-permute-start(bf16[64,1024]{1,0:T(8,128)(2,1)S(1)} %get-tuple-element.27), channel_id=1, source_target_pairs={{0,2},{1,3},{2,0},{3,1},{4,6},{5,7},{6,4},{7,5},{8,10},{9,11},{10,... | collective-permute-start | bytes 393224 | tf_op jit(solution)/shard_map/ppermute | solution.py:285
  13.7 1.1 %collective-permute-done.7.refs_3_ = bf16[32,1024]{1,0:T(8,128)(2,1)S(1)} collective-permute-done((bf16[32,1024]{1,0:T(8,128)(2,1)S(1)}, bf16[32,1024]{1,0:T(8,128)(2,1)S(1)}, u32[]{:S(2)}, u32[]{:S(2)}) %collective-permute-start.7) | collective-permute-done | bytes 65568 | tf_op jit(solution)/shard_map/ppermute | solution.py:285
  14.9 3.4 %collective-permute-start.10 = (bf16[128,1024]{1,0:T(8,128)(2,1)S(1)}, bf16[128,1024]{1,0:T(8,128)(2,1)S(1)}, u32[]{:S(2)}, u32[]{:S(2)}) collective-permute-start(bf16[128,1024]{1,0:T(8,128)(2,1)S(1)} %shard_map.68.refs_1_), channel_id=1, source_target_pairs={{0,8},{8,16},{16,24},{1,9},{9,17},{17,25},{2,10},{10,18},{18,26},{... | collective-permute-start | bytes 786440 | tf_op jit(solution)/shard_map/ppermute | solution.py:22
  18.3 0.0 collective-permute-done.1.refs_1_
  18.3 0.0 collective-permute-done.2.refs_2_
  18.3 0.0 collective-permute-done.3.refs_3_
  18.4 3.4 %collective-permute-start.12 = (bf16[128,1024]{1,0:T(8,128)(2,1)S(1)}, bf16[128,1024]{1,0:T(8,128)(2,1)S(1)}, u32[]{:S(2)}, u32[]{:S(2)}) collective-permute-start(bf16[128,1024]{1,0:T(8,128)(2,1)S(1)} %shard_map.65.refs_3_), channel_id=1, source_target_pairs={{0,8},{8,16},{16,24},{1,9},{9,17},{17,25},{2,10},{10,18},{18,26},{... | collective-permute-start | bytes 786440 | tf_op jit(solution)/shard_map/ppermute | solution.py:22
  21.8 0.0 collective-permute-done.refs_1_
  21.8 1.3 %collective-permute-start.4 = (bf16[64,1024]{1,0:T(8,128)(2,1)S(1)}, bf16[64,1024]{1,0:T(8,128)(2,1)S(1)}, u32[]{:S(2)}, u32[]{:S(2)}) collective-permute-start(bf16[64,1024]{1,0:T(8,128)(2,1)S(1)} %shard_map.66), channel_id=1, source_target_pairs={{0,4},{1,5},{2,6},{3,7},{4,0},{5,1},{6,2},{7,3},{8,12},{9,13},{10,... | collective-permute-start | bytes 393224 | tf_op jit(solution)/shard_map/ppermute | solution.py:285
  23.1 0.0 collective-permute-start.9
  23.1 0.5 %collective-permute-start.8 = (bf16[128,1024]{1,0:T(8,128)(2,1)S(1)}, bf16[128,1024]{1,0:T(8,128)(2,1)S(1)}, u32[]{:S(2)}, u32[]{:S(2)}) collective-permute-start(bf16[128,1024]{1,0:T(8,128)(2,1)S(1)} %shard_map.68.refs_1_), channel_id=1, source_target_pairs={{0,1},{1,0},{2,3},{3,2},{4,5},{5,4},{6,7},{7,6},{8,9},{9,8},{10,11... | collective-permute-start | bytes 786440 | tf_op jit(solution)/shard_map/ppermute | solution.py:288
  23.6 5.0 %collective-permute-done.4.refs_2_.refs_3_ = bf16[64,1024]{1,0:T(8,128)(2,1)S(1)} collective-permute-done((bf16[64,1024]{1,0:T(8,128)(2,1)S(1)}, bf16[64,1024]{1,0:T(8,128)(2,1)S(1)}, u32[]{:S(2)}, u32[]{:S(2)}) %collective-permute-start.4) | collective-permute-done | bytes 131104 | tf_op jit(solution)/shard_map/ppermute | solution.py:285
  28.6 0.0 collective-permute-done.10.refs_5_
  28.6 0.0 collective-permute-start.11
  28.6 0.0 collective-permute-done.12.refs_0_
  28.6 0.5 %collective-permute-start.13 = (bf16[128,1024]{1,0:T(8,128)(2,1)S(1)}, bf16[128,1024]{1,0:T(8,128)(2,1)S(1)}, u32[]{:S(2)}, u32[]{:S(2)}) collective-permute-start(bf16[128,1024]{1,0:T(8,128)(2,1)S(1)} %collective-permute-done.12.refs_0_), channel_id=1, source_target_pairs={{0,1},{1,0},{2,3},{3,2},{4,5},{5,4},{6,7},{7,6},{8,9},{9,8},{10,11... | collective-permute-start | bytes 786440 | tf_op jit(solution)/shard_map/ppermute | solution.py:288
  30.4 0.0 copy-start
  30.4 0.0 collective-permute-done.9.refs_4_
  30.5 0.0 collective-permute-done.8.refs_2_
  30.5 0.0 collective-permute-done.11.refs_6_
  30.5 1.0 %shard_map.69 = (bf16[8,128,256]{2,1,0:T(8,128)(2,1)S(1)}, f32[8,128,1]{2,1,0:T(8,128)S(1)}, f32[128,1024]{1,0:T(8,128)S(1)}) custom-call(s32[1]{0:T(128)S(6)} %copy.7.cache_ref, bf16[128,1024]{1,0:T(8,128)(2,1)S(1)} %shard_map.67.refs_0_, bf16[128,1024]{1,0:T(8,128)(2,1)S(1)} %shard_map.68.refs_1_, bf16[128,1024]{1,0:T(8,128)(2,1)S(1)} %collective-permute-done.8.refs_2_, ...), custom_call_target="tpu_custom_call" | custom-call | tf_op jit(solution)/shard_map/pallas_call | solution.py:258
  31.5 0.0 collective-permute-done.13.refs_1_
  31.5 0.1 copy-done
  31.6 0.3 shard_map.70
  32.0 2.7 %collective-permute-start.14 = (bf16[32,1024]{1,0:T(8,128)(2,1)S(1)}, bf16[32,1024]{1,0:T(8,128)(2,1)S(1)}, u32[]{:S(2)}, u32[]{:S(2)}) collective-permute-start(bf16[32,1024]{1,0:T(8,128)(2,1)S(1)} %get-tuple-element.44), channel_id=1, source_target_pairs={{0,6},{1,7},{2,4},{3,5},{4,2},{5,3},{6,0},{7,1},{8,14},{9,15},{10,... | collective-permute-start | bytes 196616 | tf_op jit(solution)/shard_map/ppermute | solution.py:285
  34.7 0.0 collective-permute-start.15
  34.7 1.7 %collective-permute-start.16 = (bf16[32,1024]{1,0:T(8,128)(2,1)S(1)}, bf16[32,1024]{1,0:T(8,128)(2,1)S(1)}, u32[]{:S(2)}, u32[]{:S(2)}) collective-permute-start(bf16[32,1024]{1,0:T(8,128)(2,1)S(1)} %get-tuple-element.46), channel_id=1, source_target_pairs={{0,2},{1,3},{2,0},{3,1},{4,6},{5,7},{6,4},{7,5},{8,10},{9,11},{10,... | collective-permute-start | bytes 196616 | tf_op jit(solution)/shard_map/ppermute | solution.py:285
  36.4 2.3 %collective-permute-done.14.refs_1_ = bf16[32,1024]{1,0:T(8,128)(2,1)S(1)} collective-permute-done((bf16[32,1024]{1,0:T(8,128)(2,1)S(1)}, bf16[32,1024]{1,0:T(8,128)(2,1)S(1)}, u32[]{:S(2)}, u32[]{:S(2)}) %collective-permute-start.14) | collective-permute-done | bytes 65568 | tf_op jit(solution)/shard_map/ppermute | solution.py:285
  38.7 2.0 %collective-permute-done.15.refs_2_ = bf16[32,1024]{1,0:T(8,128)(2,1)S(1)} collective-permute-done((bf16[32,1024]{1,0:T(8,128)(2,1)S(1)}, bf16[32,1024]{1,0:T(8,128)(2,1)S(1)}, u32[]{:S(2)}, u32[]{:S(2)}) %collective-permute-start.15) | collective-permute-done | bytes 65568 | tf_op jit(solution)/shard_map/ppermute | solution.py:285
  40.7 0.0 collective-permute-done.16.refs_3_
  40.7 0.7 %shard_map.71 = bf16[32,4096]{1,0:T(8,128)(2,1)} custom-call(bf16[32,1024]{1,0:T(8,128)(2,1)S(1)} %get-tuple-element.43.refs_0_, bf16[32,1024]{1,0:T(8,128)(2,1)S(1)} %collective-permute-done.14.refs_1_, bf16[32,1024]{1,0:T(8,128)(2,1)S(1)} %collective-permute-done.15.refs_2_, bf16[32,1024]{1,0:T(8,128)(2,1)S(1)} %collective-permute-done.16.refs_3_), custom_call_target="tpu_custom_call" | custom-call | tf_op jit(solution)/shard_map/pallas_call | solution.py:349
  (4 shorter events, 0.1 us)
Async XLA Ops:
  1.3 9.5 %collective-permute-start.5 = (bf16[32,1024]{1,0:T(8,128)(2,1)S(1)}, bf16[32,1024]{1,0:T(8,128)(2,1)S(1)}, u32[]{:S(2)}, u32[]{:S(2)}) collective-permute-start(bf16[32,1024]{1,0:T(8,128)(2,1)S(1)} %get-tuple-element.35), channel_id=1, source_target_pairs={{0,6},{1,7},{2,4},{3,5},{4,2},{5,3},{6,0},{7,1},{8,14},{9,15},{10,... | collective-permute-start | bytes 196616 | tf_op jit(solution)/shard_map/ppermute | solution.py:285
  6.4 5.0 %collective-permute-start.6 = (bf16[32,1024]{1,0:T(8,128)(2,1)S(1)}, bf16[32,1024]{1,0:T(8,128)(2,1)S(1)}, u32[]{:S(2)}, u32[]{:S(2)}) collective-permute-start(bf16[32,1024]{1,0:T(8,128)(2,1)S(1)} %get-tuple-element.36), channel_id=1, source_target_pairs={{0,2},{1,3},{2,0},{3,1},{4,6},{5,7},{6,4},{7,5},{8,10},{9,11},{10,... | collective-permute-start | bytes 196616 | tf_op jit(solution)/shard_map/ppermute | solution.py:285
  6.4 8.5 %collective-permute-start.7 = (bf16[32,1024]{1,0:T(8,128)(2,1)S(1)}, bf16[32,1024]{1,0:T(8,128)(2,1)S(1)}, u32[]{:S(2)}, u32[]{:S(2)}) collective-permute-start(bf16[32,1024]{1,0:T(8,128)(2,1)S(1)} %get-tuple-element.37), channel_id=1, source_target_pairs={{0,4},{1,5},{2,6},{3,7},{4,0},{5,1},{6,2},{7,3},{8,12},{9,13},{10,... | collective-permute-start | bytes 196616 | tf_op jit(solution)/shard_map/ppermute | solution.py:285
  7.0 11.3 %collective-permute-start.1 = (bf16[32,1024]{1,0:T(8,128)(2,1)S(1)}, bf16[32,1024]{1,0:T(8,128)(2,1)S(1)}, u32[]{:S(2)}, u32[]{:S(2)}) collective-permute-start(bf16[32,1024]{1,0:T(8,128)(2,1)S(1)} %get-tuple-element.30), channel_id=1, source_target_pairs={{0,6},{1,7},{2,4},{3,5},{4,2},{5,3},{6,0},{7,1},{8,14},{9,15},{10,... | collective-permute-start | bytes 196616 | tf_op jit(solution)/shard_map/ppermute | solution.py:285
  10.8 7.5 %collective-permute-start.2 = (bf16[32,1024]{1,0:T(8,128)(2,1)S(1)}, bf16[32,1024]{1,0:T(8,128)(2,1)S(1)}, u32[]{:S(2)}, u32[]{:S(2)}) collective-permute-start(bf16[32,1024]{1,0:T(8,128)(2,1)S(1)} %get-tuple-element.31), channel_id=1, source_target_pairs={{0,2},{1,3},{2,0},{3,1},{4,6},{5,7},{6,4},{7,5},{8,10},{9,11},{10,... | collective-permute-start | bytes 196616 | tf_op jit(solution)/shard_map/ppermute | solution.py:285
  10.8 7.5 %collective-permute-start.3 = (bf16[32,1024]{1,0:T(8,128)(2,1)S(1)}, bf16[32,1024]{1,0:T(8,128)(2,1)S(1)}, u32[]{:S(2)}, u32[]{:S(2)}) collective-permute-start(bf16[32,1024]{1,0:T(8,128)(2,1)S(1)} %get-tuple-element.32), channel_id=1, source_target_pairs={{0,4},{1,5},{2,6},{3,7},{4,0},{5,1},{6,2},{7,3},{8,12},{9,13},{10,... | collective-permute-start | bytes 196616 | tf_op jit(solution)/shard_map/ppermute | solution.py:285
  11.4 10.3 %collective-permute-start = (bf16[64,1024]{1,0:T(8,128)(2,1)S(1)}, bf16[64,1024]{1,0:T(8,128)(2,1)S(1)}, u32[]{:S(2)}, u32[]{:S(2)}) collective-permute-start(bf16[64,1024]{1,0:T(8,128)(2,1)S(1)} %get-tuple-element.27), channel_id=1, source_target_pairs={{0,2},{1,3},{2,0},{3,1},{4,6},{5,7},{6,4},{7,5},{8,10},{9,11},{10,... | collective-permute-start | bytes 393224 | tf_op jit(solution)/shard_map/ppermute | solution.py:285
  14.9 13.7 %collective-permute-start.10 = (bf16[128,1024]{1,0:T(8,128)(2,1)S(1)}, bf16[128,1024]{1,0:T(8,128)(2,1)S(1)}, u32[]{:S(2)}, u32[]{:S(2)}) collective-permute-start(bf16[128,1024]{1,0:T(8,128)(2,1)S(1)} %shard_map.68.refs_1_), channel_id=1, source_target_pairs={{0,8},{8,16},{16,24},{1,9},{9,17},{17,25},{2,10},{10,18},{18,26},{... | collective-permute-start | bytes 786440 | tf_op jit(solution)/shard_map/ppermute | solution.py:22
  18.4 10.2 %collective-permute-start.12 = (bf16[128,1024]{1,0:T(8,128)(2,1)S(1)}, bf16[128,1024]{1,0:T(8,128)(2,1)S(1)}, u32[]{:S(2)}, u32[]{:S(2)}) collective-permute-start(bf16[128,1024]{1,0:T(8,128)(2,1)S(1)} %shard_map.65.refs_3_), channel_id=1, source_target_pairs={{0,8},{8,16},{16,24},{1,9},{9,17},{17,25},{2,10},{10,18},{18,26},{... | collective-permute-start | bytes 786440 | tf_op jit(solution)/shard_map/ppermute | solution.py:22
  21.8 6.8 %collective-permute-start.4 = (bf16[64,1024]{1,0:T(8,128)(2,1)S(1)}, bf16[64,1024]{1,0:T(8,128)(2,1)S(1)}, u32[]{:S(2)}, u32[]{:S(2)}) collective-permute-start(bf16[64,1024]{1,0:T(8,128)(2,1)S(1)} %shard_map.66), channel_id=1, source_target_pairs={{0,4},{1,5},{2,6},{3,7},{4,0},{5,1},{6,2},{7,3},{8,12},{9,13},{10,... | collective-permute-start | bytes 393224 | tf_op jit(solution)/shard_map/ppermute | solution.py:285
  23.1 7.4 %collective-permute-start.9 = (bf16[128,1024]{1,0:T(8,128)(2,1)S(1)}, bf16[128,1024]{1,0:T(8,128)(2,1)S(1)}, u32[]{:S(2)}, u32[]{:S(2)}) collective-permute-start(bf16[128,1024]{1,0:T(8,128)(2,1)S(1)} %shard_map.65.refs_3_), channel_id=1, source_target_pairs={{0,1},{1,0},{2,3},{3,2},{4,5},{5,4},{6,7},{7,6},{8,9},{9,8},{10,11... | collective-permute-start | bytes 786440 | tf_op jit(solution)/shard_map/ppermute | solution.py:288
  23.1 7.4 %collective-permute-start.8 = (bf16[128,1024]{1,0:T(8,128)(2,1)S(1)}, bf16[128,1024]{1,0:T(8,128)(2,1)S(1)}, u32[]{:S(2)}, u32[]{:S(2)}) collective-permute-start(bf16[128,1024]{1,0:T(8,128)(2,1)S(1)} %shard_map.68.refs_1_), channel_id=1, source_target_pairs={{0,1},{1,0},{2,3},{3,2},{4,5},{5,4},{6,7},{7,6},{8,9},{9,8},{10,11... | collective-permute-start | bytes 786440 | tf_op jit(solution)/shard_map/ppermute | solution.py:288
  28.6 1.9 %collective-permute-start.11 = (bf16[128,1024]{1,0:T(8,128)(2,1)S(1)}, bf16[128,1024]{1,0:T(8,128)(2,1)S(1)}, u32[]{:S(2)}, u32[]{:S(2)}) collective-permute-start(bf16[128,1024]{1,0:T(8,128)(2,1)S(1)} %collective-permute-done.10.refs_5_), channel_id=1, source_target_pairs={{0,1},{1,0},{2,3},{3,2},{4,5},{5,4},{6,7},{7,6},{8,9},{9,8},{10,11... | collective-permute-start | bytes 786440 | tf_op jit(solution)/shard_map/ppermute | solution.py:288
  28.6 2.9 %collective-permute-start.13 = (bf16[128,1024]{1,0:T(8,128)(2,1)S(1)}, bf16[128,1024]{1,0:T(8,128)(2,1)S(1)}, u32[]{:S(2)}, u32[]{:S(2)}) collective-permute-start(bf16[128,1024]{1,0:T(8,128)(2,1)S(1)} %collective-permute-done.12.refs_0_), channel_id=1, source_target_pairs={{0,1},{1,0},{2,3},{3,2},{4,5},{5,4},{6,7},{7,6},{8,9},{9,8},{10,11... | collective-permute-start | bytes 786440 | tf_op jit(solution)/shard_map/ppermute | solution.py:288
  30.4 1.2 %copy-start = (f32[50,4096]{1,0:T(8,128)S(1)}, f32[50,4096]{1,0:T(8,128)}, u32[]{:S(2)}) copy-start(f32[50,4096]{1,0:T(8,128)} %refs_2_.1) | copy-start | bytes 2457604
  32.0 6.7 %collective-permute-start.14 = (bf16[32,1024]{1,0:T(8,128)(2,1)S(1)}, bf16[32,1024]{1,0:T(8,128)(2,1)S(1)}, u32[]{:S(2)}, u32[]{:S(2)}) collective-permute-start(bf16[32,1024]{1,0:T(8,128)(2,1)S(1)} %get-tuple-element.44), channel_id=1, source_target_pairs={{0,6},{1,7},{2,4},{3,5},{4,2},{5,3},{6,0},{7,1},{8,14},{9,15},{10,... | collective-permute-start | bytes 196616 | tf_op jit(solution)/shard_map/ppermute | solution.py:285
  34.7 6.0 %collective-permute-start.15 = (bf16[32,1024]{1,0:T(8,128)(2,1)S(1)}, bf16[32,1024]{1,0:T(8,128)(2,1)S(1)}, u32[]{:S(2)}, u32[]{:S(2)}) collective-permute-start(bf16[32,1024]{1,0:T(8,128)(2,1)S(1)} %get-tuple-element.45), channel_id=1, source_target_pairs={{0,4},{1,5},{2,6},{3,7},{4,0},{5,1},{6,2},{7,3},{8,12},{9,13},{10,... | collective-permute-start | bytes 196616 | tf_op jit(solution)/shard_map/ppermute | solution.py:285
  34.7 6.0 %collective-permute-start.16 = (bf16[32,1024]{1,0:T(8,128)(2,1)S(1)}, bf16[32,1024]{1,0:T(8,128)(2,1)S(1)}, u32[]{:S(2)}, u32[]{:S(2)}) collective-permute-start(bf16[32,1024]{1,0:T(8,128)(2,1)S(1)} %get-tuple-element.46), channel_id=1, source_target_pairs={{0,2},{1,3},{2,0},{3,1},{4,6},{5,7},{6,4},{7,5},{8,10},{9,11},{10,... | collective-permute-start | bytes 196616 | tf_op jit(solution)/shard_map/ppermute | solution.py:285

commit v4 on v3

--- a/solution.py
+++ b/solution.py
@@ -110,9 +110,24 @@
 
 
 CHIPS = 4
-STEPS_IN = (3, 1, 2)
-STEPS_OUT = (3, 2, 1)
-QUERY_SHARES = ((2,), (1, 3))
+
+
+def following(chip):
+    return 2 * (chip & 1) + 1 - (chip >> 1)
+
+
+def preceding(chip):
+    return 2 - 2 * (chip & 1) + (chip >> 1)
+
+
+def facing(chip):
+    return CHIPS - 1 - chip
+
+
+ROUTES = ((following, preceding), (facing, facing), (preceding, following))
+OUT_ORDER = (0, 1, 2)
+KEY_ORDER = (1, 0, 2)
+VALUE_ORDER = (0, 1, 2)
 
 
 def span_of(chip, width):
@@ -130,13 +145,13 @@
     whole, parts, sems = refs[:3], refs[3:-1], refs[-1]
     rows = whole[0].shape[0]
     width = parts[0].shape[1]
-    chip = lax.axis_index("seq") // 2
+    here = lax.axis_index("seq") // 2
     copies = []
-    for part, (index, steps) in zip(parts, cuts):
-        for place, step in enumerate(steps):
+    for part, (index, chips) in zip(parts, cuts):
+        for place, chip in enumerate(chips):
             copies.append(
                 pltpu.make_async_copy(
-                    whole[index].at[:, span_of(chip ^ step, width)],
+                    whole[index].at[:, span_of(chip(here), width)],
                     part.at[pl.ds(place * rows, rows)],
                     sems.at[len(copies)],
                 )
@@ -149,6 +164,16 @@
     rows = out_ref.shape[0] // len(parts)
     for part, (to, place) in zip(parts, places):
         out_ref[pl.ds(to * rows, rows)] = part[pl.ds(place * rows, rows)]
+
+
+def query_kernel(own_ref, near_ref, far_ref, out_ref):
+    rows = own_ref.shape[0]
+    chip = lax.axis_index("seq") // 2
+    near_place = jnp.where((chip ^ 1) == following(chip), 1, 3)
+    out_ref[pl.ds(0, rows)] = own_ref[...]
+    out_ref[pl.ds(2 * rows, rows)] = far_ref[pl.ds(rows, rows)]
+    out_ref[pl.ds(pl.multiple_of(near_place * rows, rows), rows)] = near_ref[pl.ds(0, rows)]
+    out_ref[pl.ds(pl.multiple_of((4 - near_place) * rows, rows), rows)] = far_ref[pl.ds(0, rows)]
 
 
 def product(left, right, dims):
@@ -166,13 +191,13 @@
     core = lax.rem(lax.axis_index("seq"), 2)
     chip = lax.axis_index("seq") // 2
     seen_from = jnp.where(lax.axis_index("stretch") > 0, cache_ref[0], tokens)
-    steps = range(chips)
+    sources = [chip] + [source(chip) for _, source in ROUTES]
     lane = lax.broadcasted_iota(jnp.int32, (1, rows), 1)
     position = jnp.concatenate(
         [
-            lane + ((chip ^ step) * 2 + (core ^ other)) * rows
+            lane + (source * 2 + (core ^ other)) * rows
             for other in range(2)
-            for step in steps
+            for source in sources
         ],
         axis=1,
     )
@@ -234,10 +259,11 @@
     parts, out_ref, sems = refs[:-2], refs[-2], refs[-1]
     chip = lax.axis_index("seq") // 2
     width = parts[0].shape[1]
+    sources = [chip] + [ROUTES[route][1](chip) for route in OUT_ORDER]
     run_copies(
         [
-            pltpu.make_async_copy(part, out_ref.at[:, span_of(chip ^ step, width)], sems.at[place])
-            for place, (part, step) in enumerate(zip(parts, (0, *STEPS_OUT)))
+            pltpu.make_async_copy(part, out_ref.at[:, span_of(source, width)], sems.at[place])
+            for place, (part, source) in enumerate(zip(parts, sources))
         ]
     )
 
@@ -281,8 +307,8 @@
     def block(count):
         return jax.ShapeDtypeStruct((count * rows, width), jnp.bfloat16)
 
-    def with_chip(part, step):
-        return lax.ppermute(part, "seq", [(i, i ^ (2 * step)) for i in range(seq)])
+    def to_chip(part, target):
+        return lax.ppermute(part, "seq", [(i, 2 * target(i // 2) + i % 2) for i in range(seq)])
 
     def with_core(part):
         return lax.ppermute(part, "seq", [(i, i ^ 1) for i in range(seq)])
@@ -291,28 +317,34 @@
         kernel = functools.partial(join_kernel, places)
         return kernel_call(kernel, [VMEM] * len(parts), block(len(parts)), work=work)(*parts)
 
-    cuts = [(index, (step,)) for index in range(2) for step in (0, *STEPS_IN)]
-    cuts += [(2, (0,))] + [(2, steps) for steps in QUERY_SHARES]
+    def stay(chip):
+        return chip
+
+    def away(step):
+        return lambda chip: chip ^ step
+
+    cuts = [(index, (chip,)) for index in range(2) for chip in (stay, *(to for to, _ in ROUTES))]
+    cuts += [(2, (stay,)), (2, (away(2),)), (2, (away(1), away(3)))]
     parts = kernel_call(
         functools.partial(pack_kernel, cuts),
         [HBM] * 3,
-        tuple(block(len(steps)) for _, steps in cuts),
+        tuple(block(len(chips)) for _, chips in cuts),
         scratch=[pltpu.SemaphoreType.DMA((3 * CHIPS,))],
     )(key_rows[0], value_rows[0], query_rows[0])
     key_parts, value_parts, query_parts = parts[:CHIPS], parts[CHIPS:2 * CHIPS], parts[2 * CHIPS:]
 
-    def gathered(parts, work=0):
-        got = [parts[0]] + [with_chip(part, step) for part, step in zip(parts[1:], STEPS_IN)]
-        return join(got, [(step, 0) for step in (0, *STEPS_IN)], work)
-
-    keys = gathered(key_parts)
-    values = gathered(value_parts)
+    def gathered(parts, order, work=0):
+        got = [parts[0]] + [to_chip(parts[1 + route], ROUTES[route][0]) for route in order]
+        return join(got, [(0, 0)] + [(1 + route, 0) for route in order], work)
+
+    keys = gathered(key_parts, KEY_ORDER)
+    values = gathered(value_parts, VALUE_ORDER)
     past_keys = passed_along(keys, "stretch", 1)
     past_values = passed_along(values, "stretch", 1)
     own_query, two_on, near = query_parts
-    near = with_chip(near, 1)
-    far = with_chip(join([after(two_on, values), near], [(0, 0), (1, 1)]), 2)
-    queries = join([own_query, near, far, far], [(0, 0), (1, 0), (2, 0), (3, 1)])
+    near = to_chip(near, away(1))
+    far = to_chip(join([after(two_on, values), near], [(0, 0), (1, 1)]), away(2))
+    queries = kernel_call(query_kernel, [VMEM] * 3, block(CHIPS))(own_query, near, far)
     past_weight, total, numer = kernel_call(
         weigh_kernel,
         [SMEM] + [VMEM] * 7,
@@ -345,7 +377,7 @@
         with_core(after(past_values, far)),
         gate_table,
     )
-    returned = [outs[0]] + [with_chip(outs[step], step) for step in STEPS_OUT]
+    returned = [outs[0]] + [to_chip(outs[1 + route], ROUTES[route][0]) for route in OUT_ORDER]
     out = pl.pallas_call(
         unpack_kernel,
         out_shape=jax.ShapeDtypeStruct((rows, HEADS * HD), jnp.bfloat16),

time: 41.7 us -> 40.8 us (0.978)
  waiting for transfers between devices: 10.4 us -> 9.15 us
    ppermute x11, waiting for transfers between devices: 10.4 us -> 9.14 us  [to_chip(): lax.ppermute(part, 'seq', [(i, 2 * target(i // 2) + i % 2) for i in range...]
  transfers between devices with their start and end apart: 17 -> 17, of which waited for: 4 -> 5; matrix products, arithmetic and copies ran while one was open for 0% -> 0% of each run, Pallas kernels for 3% -> 3%
where the time goes in v4:
time: 40.8 us; the launch traced here: 40.5 us
  starting transfers between devices  26.4 us (65%)
  waiting for transfers between devices  9.15 us (22%)
  Pallas kernels  3.42 us (8%)
  between operations  1.43 us (4%)
    ppermute x11, starting transfers between devices, to_chip(): lax.ppermute(part, 'seq', [(i, 2 * target(i // 2) + i % 2) for i in range...  18.6 us
    ppermute x11, waiting for transfers between devices, to_chip(): lax.ppermute(part, 'seq', [(i, 2 * target(i // 2) + i % 2) for i in range...  9.14 us
    ppermute x2, starting transfers between devices, passed_along(): return lax.ppermute(block, axis, route)  6.82 us
    pallas_call x7, Pallas kernels, run(): call(*(pltpu.with_memory_space_constraint(operand, spec.memory_space) if...  2.69 us
    ppermute x4, starting transfers between devices, with_core(): return lax.ppermute(part, 'seq', [(i, i ^ 1) for i in range(seq)])  1.02 us
  transfers between devices with their start and end apart: 17, of which 5 were waited for; matrix products, arithmetic and copies ran while one was open for 0% of the time, Pallas kernels for 3%

profile of v4, /device:TPU:0, one launch (start us, length us, event | category | flops | bytes accessed | tf_op | source)
XLA Modules:
  0.0 40.5 jit_solution(17202428864418233312)
XLA Ops:
  0.0 1.3 %shard_map.64 = (bf16[32,1024]{1,0:T(8,128)(2,1)S(1)}, bf16[32,1024]{1,0:T(8,128)(2,1)S(1)}, bf16[32,1024]{1,0:T(8,128)(2,1)S(1)}, bf16[32,1024]{1,0:T(8,128)(2,...) custom-call(bf16[32,4096]{1,0:T(8,128)(2,1)} %bitcast.4, ...), custom_call_target="tpu_custom_call" | custom-call | tf_op jit(solution)/shard_map/pallas_call | solution.py:284
  1.3 5.1 %collective-permute-start.5 = (bf16[32,1024]{1,0:T(8,128)(2,1)S(1)}, bf16[32,1024]{1,0:T(8,128)(2,1)S(1)}, u32[]{:S(2)}, u32[]{:S(2)}) collective-permute-start(bf16[32,1024]{1,0:T(8,128)(2,1)S(1)} %get-tuple-element.35), channel_id=1, source_target_pairs={{0,6},{1,7},{2,4},{3,5},{4,2},{5,3},{6,0},{7,1},{8,14},{9,15},{10,... | collective-permute-start | bytes 196616 | tf_op jit(solution)/shard_map/ppermute | solution.py:311
  6.4 0.0 collective-permute-start.6
  6.4 2.9 %collective-permute-start.7 = (bf16[32,1024]{1,0:T(8,128)(2,1)S(1)}, bf16[32,1024]{1,0:T(8,128)(2,1)S(1)}, u32[]{:S(2)}, u32[]{:S(2)}) collective-permute-start(bf16[32,1024]{1,0:T(8,128)(2,1)S(1)} %get-tuple-element.37), channel_id=1, source_target_pairs={{0,4},{1,5},{2,0},{3,1},{4,6},{5,7},{6,2},{7,3},{8,12},{9,13},{10,... | collective-permute-start | bytes 196616 | tf_op jit(solution)/shard_map/ppermute | solution.py:311
  9.3 0.0 collective-permute-start.1
  9.3 1.5 %collective-permute-start.2 = (bf16[32,1024]{1,0:T(8,128)(2,1)S(1)}, bf16[32,1024]{1,0:T(8,128)(2,1)S(1)}, u32[]{:S(2)}, u32[]{:S(2)}) collective-permute-start(bf16[32,1024]{1,0:T(8,128)(2,1)S(1)} %get-tuple-element.31), channel_id=1, source_target_pairs={{0,6},{1,7},{2,4},{3,5},{4,2},{5,3},{6,0},{7,1},{8,14},{9,15},{10,... | collective-permute-start | bytes 196616 | tf_op jit(solution)/shard_map/ppermute | solution.py:311
  10.8 0.0 collective-permute-done.5.refs_1_
  10.8 1.5 %collective-permute-start.3 = (bf16[32,1024]{1,0:T(8,128)(2,1)S(1)}, bf16[32,1024]{1,0:T(8,128)(2,1)S(1)}, u32[]{:S(2)}, u32[]{:S(2)}) collective-permute-start(bf16[32,1024]{1,0:T(8,128)(2,1)S(1)} %get-tuple-element.32), channel_id=1, source_target_pairs={{0,4},{1,5},{2,0},{3,1},{4,6},{5,7},{6,2},{7,3},{8,12},{9,13},{10,... | collective-permute-start | bytes 196616 | tf_op jit(solution)/shard_map/ppermute | solution.py:311
  12.2 0.3 collective-permute-done.6.refs_2_
  12.5 0.3 collective-permute-start
  12.9 0.0 collective-permute-done.7.refs_3_
  12.9 3.4 %collective-permute-start.10 = (bf16[128,1024]{1,0:T(8,128)(2,1)S(1)}, bf16[128,1024]{1,0:T(8,128)(2,1)S(1)}, u32[]{:S(2)}, u32[]{:S(2)}) collective-permute-start(bf16[128,1024]{1,0:T(8,128)(2,1)S(1)} %shard_map.68.refs_1_), channel_id=1, source_target_pairs={{0,8},{8,16},{16,24},{1,9},{9,17},{17,25},{2,10},{10,18},{18,26},{... | collective-permute-start | bytes 786440 | tf_op jit(solution)/shard_map/ppermute | solution.py:22
  16.3 0.2 collective-permute-done.1.refs_1_
  16.5 0.0 collective-permute-done.2.refs_2_
  16.5 0.6 %collective-permute-done.3.refs_3_ = bf16[32,1024]{1,0:T(8,128)(2,1)S(1)} collective-permute-done((bf16[32,1024]{1,0:T(8,128)(2,1)S(1)}, bf16[32,1024]{1,0:T(8,128)(2,1)S(1)}, u32[]{:S(2)}, u32[]{:S(2)}) %collective-permute-start.3) | collective-permute-done | bytes 65568 | tf_op jit(solution)/shard_map/ppermute | solution.py:311
  17.1 3.4 %collective-permute-start.12 = (bf16[128,1024]{1,0:T(8,128)(2,1)S(1)}, bf16[128,1024]{1,0:T(8,128)(2,1)S(1)}, u32[]{:S(2)}, u32[]{:S(2)}) collective-permute-start(bf16[128,1024]{1,0:T(8,128)(2,1)S(1)} %shard_map.65.refs_3_), channel_id=1, source_target_pairs={{0,8},{8,16},{16,24},{1,9},{9,17},{17,25},{2,10},{10,18},{18,26},{... | collective-permute-start | bytes 786440 | tf_op jit(solution)/shard_map/ppermute | solution.py:22
  20.5 0.0 collective-permute-done.refs_1_.near_ref
  20.5 2.5 %collective-permute-start.4 = (bf16[64,1024]{1,0:T(8,128)(2,1)S(1)}, bf16[64,1024]{1,0:T(8,128)(2,1)S(1)}, u32[]{:S(2)}, u32[]{:S(2)}) collective-permute-start(bf16[64,1024]{1,0:T(8,128)(2,1)S(1)} %shard_map.66), channel_id=1, source_target_pairs={{0,4},{1,5},{2,6},{3,7},{4,0},{5,1},{6,2},{7,3},{8,12},{9,13},{10,... | collective-permute-start | bytes 393224 | tf_op jit(solution)/shard_map/ppermute | solution.py:311
  23.0 0.0 collective-permute-start.9
  23.0 0.5 %collective-permute-start.8 = (bf16[128,1024]{1,0:T(8,128)(2,1)S(1)}, bf16[128,1024]{1,0:T(8,128)(2,1)S(1)}, u32[]{:S(2)}, u32[]{:S(2)}) collective-permute-start(bf16[128,1024]{1,0:T(8,128)(2,1)S(1)} %shard_map.68.refs_1_), channel_id=1, source_target_pairs={{0,1},{1,0},{2,3},{3,2},{4,5},{5,4},{6,7},{7,6},{8,9},{9,8},{10,11... | collective-permute-start | bytes 786440 | tf_op jit(solution)/shard_map/ppermute | solution.py:314
  23.5 4.5 %collective-permute-done.4.far_ref = bf16[64,1024]{1,0:T(8,128)(2,1)S(1)} collective-permute-done((bf16[64,1024]{1,0:T(8,128)(2,1)S(1)}, bf16[64,1024]{1,0:T(8,128)(2,1)S(1)}, u32[]{:S(2)}, u32[]{:S(2)}) %collective-permute-start.4) | collective-permute-done | bytes 131104 | tf_op jit(solution)/shard_map/ppermute | solution.py:311
  28.0 0.0 collective-permute-done.10.refs_5_
  28.0 0.0 collective-permute-start.11
  28.0 0.0 collective-permute-done.12.refs_0_
  28.0 0.5 %collective-permute-start.13 = (bf16[128,1024]{1,0:T(8,128)(2,1)S(1)}, bf16[128,1024]{1,0:T(8,128)(2,1)S(1)}, u32[]{:S(2)}, u32[]{:S(2)}) collective-permute-start(bf16[128,1024]{1,0:T(8,128)(2,1)S(1)} %collective-permute-done.12.refs_0_), channel_id=1, source_target_pairs={{0,1},{1,0},{2,3},{3,2},{4,5},{5,4},{6,7},{7,6},{8,9},{9,8},{10,11... | collective-permute-start | bytes 786440 | tf_op jit(solution)/shard_map/ppermute | solution.py:314
  29.9 0.0 copy-start
  29.9 0.0 collective-permute-done.9.refs_4_
  29.9 0.0 collective-permute-done.8.refs_2_
  29.9 0.0 collective-permute-done.11.refs_6_
  29.9 1.0 %shard_map.69 = (bf16[8,128,256]{2,1,0:T(8,128)(2,1)S(1)}, f32[8,128,1]{2,1,0:T(8,128)S(1)}, f32[128,1024]{1,0:T(8,128)S(1)}) custom-call(s32[1]{0:T(128)S(6)} %copy.7.cache_ref, bf16[128,1024]{1,0:T(8,128)(2,1)S(1)} %shard_map.67.refs_0_, bf16[128,1024]{1,0:T(8,128)(2,1)S(1)} %shard_map.68.refs_1_, bf16[128,1024]{1,0:T(8,128)(2,1)S(1)} %collective-permute-done.8.refs_2_, ...), custom_call_target="tpu_custom_call" | custom-call | tf_op jit(solution)/shard_map/pallas_call | solution.py:284
  31.0 0.0 collective-permute-done.13.refs_1_
  31.0 0.1 copy-done
  31.1 0.3 shard_map.70
  31.4 0.1 collective-permute-start.14
  31.5 2.7 %collective-permute-start.15 = (bf16[32,1024]{1,0:T(8,128)(2,1)S(1)}, bf16[32,1024]{1,0:T(8,128)(2,1)S(1)}, u32[]{:S(2)}, u32[]{:S(2)}) collective-permute-start(bf16[32,1024]{1,0:T(8,128)(2,1)S(1)} %get-tuple-element.45), channel_id=1, source_target_pairs={{0,6},{1,7},{2,4},{3,5},{4,2},{5,3},{6,0},{7,1},{8,14},{9,15},{10,... | collective-permute-start | bytes 196616 | tf_op jit(solution)/shard_map/ppermute | solution.py:311
  34.2 1.9 %collective-permute-start.16 = (bf16[32,1024]{1,0:T(8,128)(2,1)S(1)}, bf16[32,1024]{1,0:T(8,128)(2,1)S(1)}, u32[]{:S(2)}, u32[]{:S(2)}) collective-permute-start(bf16[32,1024]{1,0:T(8,128)(2,1)S(1)} %get-tuple-element.46), channel_id=1, source_target_pairs={{0,4},{1,5},{2,0},{3,1},{4,6},{5,7},{6,2},{7,3},{8,12},{9,13},{10,... | collective-permute-start | bytes 196616 | tf_op jit(solution)/shard_map/ppermute | solution.py:311
  36.2 3.6 %collective-permute-done.14.refs_1_ = bf16[32,1024]{1,0:T(8,128)(2,1)S(1)} collective-permute-done((bf16[32,1024]{1,0:T(8,128)(2,1)S(1)}, bf16[32,1024]{1,0:T(8,128)(2,1)S(1)}, u32[]{:S(2)}, u32[]{:S(2)}) %collective-permute-start.14) | collective-permute-done | bytes 65568 | tf_op jit(solution)/shard_map/ppermute | solution.py:311
  39.8 0.0 collective-permute-done.15.refs_2_
  39.8 0.0 collective-permute-done.16.refs_3_
  39.8 0.7 %shard_map.71 = bf16[32,4096]{1,0:T(8,128)(2,1)} custom-call(bf16[32,1024]{1,0:T(8,128)(2,1)S(1)} %get-tuple-element.43.refs_0_, bf16[32,1024]{1,0:T(8,128)(2,1)S(1)} %collective-permute-done.14.refs_1_, bf16[32,1024]{1,0:T(8,128)(2,1)S(1)} %collective-permute-done.15.refs_2_, bf16[32,1024]{1,0:T(8,128)(2,1)S(1)} %collective-permute-done.16.refs_3_), custom_call_target="tpu_custom_call" | custom-call | tf_op jit(solution)/shard_map/pallas_call | solution.py:381
  (4 shorter events, 0.1 us)
Async XLA Ops:
  1.3 9.5 %collective-permute-start.5 = (bf16[32,1024]{1,0:T(8,128)(2,1)S(1)}, bf16[32,1024]{1,0:T(8,128)(2,1)S(1)}, u32[]{:S(2)}, u32[]{:S(2)}) collective-permute-start(bf16[32,1024]{1,0:T(8,128)(2,1)S(1)} %get-tuple-element.35), channel_id=1, source_target_pairs={{0,6},{1,7},{2,4},{3,5},{4,2},{5,3},{6,0},{7,1},{8,14},{9,15},{10,... | collective-permute-start | bytes 196616 | tf_op jit(solution)/shard_map/ppermute | solution.py:311
  6.4 6.1 %collective-permute-start.6 = (bf16[32,1024]{1,0:T(8,128)(2,1)S(1)}, bf16[32,1024]{1,0:T(8,128)(2,1)S(1)}, u32[]{:S(2)}, u32[]{:S(2)}) collective-permute-start(bf16[32,1024]{1,0:T(8,128)(2,1)S(1)} %get-tuple-element.36), channel_id=1, source_target_pairs={{0,2},{1,3},{2,6},{3,7},{4,0},{5,1},{6,4},{7,5},{8,10},{9,11},{10,... | collective-permute-start | bytes 196616 | tf_op jit(solution)/shard_map/ppermute | solution.py:311
  6.4 6.5 %collective-permute-start.7 = (bf16[32,1024]{1,0:T(8,128)(2,1)S(1)}, bf16[32,1024]{1,0:T(8,128)(2,1)S(1)}, u32[]{:S(2)}, u32[]{:S(2)}) collective-permute-start(bf16[32,1024]{1,0:T(8,128)(2,1)S(1)} %get-tuple-element.37), channel_id=1, source_target_pairs={{0,4},{1,5},{2,0},{3,1},{4,6},{5,7},{6,2},{7,3},{8,12},{9,13},{10,... | collective-permute-start | bytes 196616 | tf_op jit(solution)/shard_map/ppermute | solution.py:311
  9.3 7.2 %collective-permute-start.1 = (bf16[32,1024]{1,0:T(8,128)(2,1)S(1)}, bf16[32,1024]{1,0:T(8,128)(2,1)S(1)}, u32[]{:S(2)}, u32[]{:S(2)}) collective-permute-start(bf16[32,1024]{1,0:T(8,128)(2,1)S(1)} %get-tuple-element.30), channel_id=1, source_target_pairs={{0,2},{1,3},{2,6},{3,7},{4,0},{5,1},{6,4},{7,5},{8,10},{9,11},{10,... | collective-permute-start | bytes 196616 | tf_op jit(solution)/shard_map/ppermute | solution.py:311
  9.3 7.2 %collective-permute-start.2 = (bf16[32,1024]{1,0:T(8,128)(2,1)S(1)}, bf16[32,1024]{1,0:T(8,128)(2,1)S(1)}, u32[]{:S(2)}, u32[]{:S(2)}) collective-permute-start(bf16[32,1024]{1,0:T(8,128)(2,1)S(1)} %get-tuple-element.31), channel_id=1, source_target_pairs={{0,6},{1,7},{2,4},{3,5},{4,2},{5,3},{6,0},{7,1},{8,14},{9,15},{10,... | collective-permute-start | bytes 196616 | tf_op jit(solution)/shard_map/ppermute | solution.py:311
  10.8 6.3 %collective-permute-start.3 = (bf16[32,1024]{1,0:T(8,128)(2,1)S(1)}, bf16[32,1024]{1,0:T(8,128)(2,1)S(1)}, u32[]{:S(2)}, u32[]{:S(2)}) collective-permute-start(bf16[32,1024]{1,0:T(8,128)(2,1)S(1)} %get-tuple-element.32), channel_id=1, source_target_pairs={{0,4},{1,5},{2,0},{3,1},{4,6},{5,7},{6,2},{7,3},{8,12},{9,13},{10,... | collective-permute-start | bytes 196616 | tf_op jit(solution)/shard_map/ppermute | solution.py:311
  12.5 8.0 %collective-permute-start = (bf16[64,1024]{1,0:T(8,128)(2,1)S(1)}, bf16[64,1024]{1,0:T(8,128)(2,1)S(1)}, u32[]{:S(2)}, u32[]{:S(2)}) collective-permute-start(bf16[64,1024]{1,0:T(8,128)(2,1)S(1)} %get-tuple-element.27), channel_id=1, source_target_pairs={{0,2},{1,3},{2,0},{3,1},{4,6},{5,7},{6,4},{7,5},{8,10},{9,11},{10,... | collective-permute-start | bytes 393224 | tf_op jit(solution)/shard_map/ppermute | solution.py:311
  12.9 15.1 %collective-permute-start.10 = (bf16[128,1024]{1,0:T(8,128)(2,1)S(1)}, bf16[128,1024]{1,0:T(8,128)(2,1)S(1)}, u32[]{:S(2)}, u32[]{:S(2)}) collective-permute-start(bf16[128,1024]{1,0:T(8,128)(2,1)S(1)} %shard_map.68.refs_1_), channel_id=1, source_target_pairs={{0,8},{8,16},{16,24},{1,9},{9,17},{17,25},{2,10},{10,18},{18,26},{... | collective-permute-start | bytes 786440 | tf_op jit(solution)/shard_map/ppermute | solution.py:22
  17.1 11.0 %collective-permute-start.12 = (bf16[128,1024]{1,0:T(8,128)(2,1)S(1)}, bf16[128,1024]{1,0:T(8,128)(2,1)S(1)}, u32[]{:S(2)}, u32[]{:S(2)}) collective-permute-start(bf16[128,1024]{1,0:T(8,128)(2,1)S(1)} %shard_map.65.refs_3_), channel_id=1, source_target_pairs={{0,8},{8,16},{16,24},{1,9},{9,17},{17,25},{2,10},{10,18},{18,26},{... | collective-permute-start | bytes 786440 | tf_op jit(solution)/shard_map/ppermute | solution.py:22
  20.5 7.5 %collective-permute-start.4 = (bf16[64,1024]{1,0:T(8,128)(2,1)S(1)}, bf16[64,1024]{1,0:T(8,128)(2,1)S(1)}, u32[]{:S(2)}, u32[]{:S(2)}) collective-permute-start(bf16[64,1024]{1,0:T(8,128)(2,1)S(1)} %shard_map.66), channel_id=1, source_target_pairs={{0,4},{1,5},{2,6},{3,7},{4,0},{5,1},{6,2},{7,3},{8,12},{9,13},{10,... | collective-permute-start | bytes 393224 | tf_op jit(solution)/shard_map/ppermute | solution.py:311
  23.0 6.9 %collective-permute-start.9 = (bf16[128,1024]{1,0:T(8,128)(2,1)S(1)}, bf16[128,1024]{1,0:T(8,128)(2,1)S(1)}, u32[]{:S(2)}, u32[]{:S(2)}) collective-permute-start(bf16[128,1024]{1,0:T(8,128)(2,1)S(1)} %shard_map.65.refs_3_), channel_id=1, source_target_pairs={{0,1},{1,0},{2,3},{3,2},{4,5},{5,4},{6,7},{7,6},{8,9},{9,8},{10,11... | collective-permute-start | bytes 786440 | tf_op jit(solution)/shard_map/ppermute | solution.py:314
  23.0 6.9 %collective-permute-start.8 = (bf16[128,1024]{1,0:T(8,128)(2,1)S(1)}, bf16[128,1024]{1,0:T(8,128)(2,1)S(1)}, u32[]{:S(2)}, u32[]{:S(2)}) collective-permute-start(bf16[128,1024]{1,0:T(8,128)(2,1)S(1)} %shard_map.68.refs_1_), channel_id=1, source_target_pairs={{0,1},{1,0},{2,3},{3,2},{4,5},{5,4},{6,7},{7,6},{8,9},{9,8},{10,11... | collective-permute-start | bytes 786440 | tf_op jit(solution)/shard_map/ppermute | solution.py:314
  28.0 1.9 %collective-permute-start.11 = (bf16[128,1024]{1,0:T(8,128)(2,1)S(1)}, bf16[128,1024]{1,0:T(8,128)(2,1)S(1)}, u32[]{:S(2)}, u32[]{:S(2)}) collective-permute-start(bf16[128,1024]{1,0:T(8,128)(2,1)S(1)} %collective-permute-done.10.refs_5_), channel_id=1, source_target_pairs={{0,1},{1,0},{2,3},{3,2},{4,5},{5,4},{6,7},{7,6},{8,9},{9,8},{10,11... | collective-permute-start | bytes 786440 | tf_op jit(solution)/shard_map/ppermute | solution.py:314
  28.0 2.9 %collective-permute-start.13 = (bf16[128,1024]{1,0:T(8,128)(2,1)S(1)}, bf16[128,1024]{1,0:T(8,128)(2,1)S(1)}, u32[]{:S(2)}, u32[]{:S(2)}) collective-permute-start(bf16[128,1024]{1,0:T(8,128)(2,1)S(1)} %collective-permute-done.12.refs_0_), channel_id=1, source_target_pairs={{0,1},{1,0},{2,3},{3,2},{4,5},{5,4},{6,7},{7,6},{8,9},{9,8},{10,11... | collective-permute-start | bytes 786440 | tf_op jit(solution)/shard_map/ppermute | solution.py:314
  29.9 1.2 %copy-start = (f32[50,4096]{1,0:T(8,128)S(1)}, f32[50,4096]{1,0:T(8,128)}, u32[]{:S(2)}) copy-start(f32[50,4096]{1,0:T(8,128)} %refs_2_.1) | copy-start | bytes 2457604
  31.4 8.4 %collective-permute-start.14 = (bf16[32,1024]{1,0:T(8,128)(2,1)S(1)}, bf16[32,1024]{1,0:T(8,128)(2,1)S(1)}, u32[]{:S(2)}, u32[]{:S(2)}) collective-permute-start(bf16[32,1024]{1,0:T(8,128)(2,1)S(1)} %get-tuple-element.44), channel_id=1, source_target_pairs={{0,2},{1,3},{2,6},{3,7},{4,0},{5,1},{6,4},{7,5},{8,10},{9,11},{10,... | collective-permute-start | bytes 196616 | tf_op jit(solution)/shard_map/ppermute | solution.py:311
  31.5 8.3 %collective-permute-start.15 = (bf16[32,1024]{1,0:T(8,128)(2,1)S(1)}, bf16[32,1024]{1,0:T(8,128)(2,1)S(1)}, u32[]{:S(2)}, u32[]{:S(2)}) collective-permute-start(bf16[32,1024]{1,0:T(8,128)(2,1)S(1)} %get-tuple-element.45), channel_id=1, source_target_pairs={{0,6},{1,7},{2,4},{3,5},{4,2},{5,3},{6,0},{7,1},{8,14},{9,15},{10,... | collective-permute-start | bytes 196616 | tf_op jit(solution)/shard_map/ppermute | solution.py:311
  34.2 5.6 %collective-permute-start.16 = (bf16[32,1024]{1,0:T(8,128)(2,1)S(1)}, bf16[32,1024]{1,0:T(8,128)(2,1)S(1)}, u32[]{:S(2)}, u32[]{:S(2)}) collective-permute-start(bf16[32,1024]{1,0:T(8,128)(2,1)S(1)} %get-tuple-element.46), channel_id=1, source_target_pairs={{0,4},{1,5},{2,0},{3,1},{4,6},{5,7},{6,2},{7,3},{8,12},{9,13},{10,... | collective-permute-start | bytes 196616 | tf_op jit(solution)/shard_map/ppermute | solution.py:311

commit v5 on v4

--- a/solution.py
+++ b/solution.py
@@ -180,17 +180,27 @@
     return lax.dot_general(left, right, (dims, ((), ())), preferred_element_type=jnp.float32)
 
 
-def weigh_kernel(cache_ref, *refs):
+def prepare_kernel(cache_ref, time_ref, gate_ref, from_ref, row_ref, sem):
+    chip = lax.axis_index("seq") // 2
+    copy = pltpu.make_async_copy(
+        gate_ref.at[pl.ds(time_ref[0], 1), span_of(chip, row_ref.shape[1])], row_ref, sem
+    )
+    copy.start()
+    tokens = from_ref.shape[1]
+    seen_from = jnp.where(lax.axis_index("stretch") > 0, cache_ref[0], tokens)
+    from_ref[...] = jnp.full(from_ref.shape, seen_from, jnp.int32)
+    copy.wait()
+
+
+def weigh_kernel(from_ref, *refs):
     queries, refs = refs[0], refs[1:]
     chips = CHIPS
     key_refs, value_refs, past_refs = refs[0:2], refs[2:4], refs[4:6]
     past_weight_ref, total_ref, numer_ref = refs[6:9]
     half, width = queries.shape
     rows = half // chips
-    tokens = 2 * half
     core = lax.rem(lax.axis_index("seq"), 2)
     chip = lax.axis_index("seq") // 2
-    seen_from = jnp.where(lax.axis_index("stretch") > 0, cache_ref[0], tokens)
     sources = [chip] + [source(chip) for _, source in ROUTES]
     lane = lax.broadcasted_iota(jnp.int32, (1, rows), 1)
     position = jnp.concatenate(
@@ -201,7 +211,7 @@
         ],
         axis=1,
     )
-    visible = position >= seen_from
+    visible = position >= from_ref[...]
     scale = HD ** (-0.5) * math.log2(math.e)
 
     def scores(head):
@@ -235,23 +245,16 @@
     mix(*weighed)
 
 
-def finish_kernel(time_ref, past_weight_ref, total_ref, numer_ref, *refs):
-    past_refs, gate_ref = refs[0:2], refs[2]
-    outs, gate_row, sem = refs[3:-2], refs[-2], refs[-1]
-    chips = len(outs)
-    width = outs[0].shape[1]
-    rows = outs[0].shape[0]
-    chip = lax.axis_index("seq") // 2
-    fetch = pltpu.make_async_copy(gate_ref.at[pl.ds(time_ref[0], 1), span_of(chip, width)], gate_row, sem)
-    fetch.start()
-    fetch.wait()
+def finish_kernel(past_weight_ref, total_ref, numer_ref, gate_row, *refs):
+    past_refs, outs = refs[:2], refs[2:]
+    rows, width = outs[0].shape
     for head in range(width // HD):
         lanes = pl.ds(head * HD, HD)
         past_value = jnp.concatenate([ref[:, lanes] for ref in past_refs], axis=0)
         numer = numer_ref[:, lanes] + product(past_weight_ref[head], past_value, ((1,), (0,)))
         attended = (numer / total_ref[head]).astype(jnp.bfloat16)
         gated = (attended.astype(jnp.float32) * gate_row[:, lanes]).astype(jnp.bfloat16)
-        for place in range(chips):
+        for place in range(CHIPS):
             outs[place][:, lanes] = gated[place * rows:(place + 1) * rows]
 
 
@@ -344,38 +347,48 @@
     own_query, two_on, near = query_parts
     near = to_chip(near, away(1))
     far = to_chip(join([after(two_on, values), near], [(0, 0), (1, 1)]), away(2))
-    queries = kernel_call(query_kernel, [VMEM] * 3, block(CHIPS))(own_query, near, far)
+    past_keys_too = with_core(past_keys)
+    queries = kernel_call(query_kernel, [VMEM] * 3, block(CHIPS))(
+        after(own_query, past_keys_too), near, far
+    )
+    seen_from, gate_row = kernel_call(
+        prepare_kernel,
+        [SMEM, SMEM, HBM],
+        (
+            jax.ShapeDtypeStruct((1, 2 * half), jnp.int32),
+            jax.ShapeDtypeStruct((1, width), jnp.float32),
+        ),
+        scratch=[pltpu.SemaphoreType.DMA],
+    )(cache_from, time_index, gate_table)
     past_weight, total, numer = kernel_call(
         weigh_kernel,
-        [SMEM] + [VMEM] * 7,
+        [VMEM] * 8,
         (
             jax.ShapeDtypeStruct((per_dev, half, 2 * half), jnp.bfloat16),
             jax.ShapeDtypeStruct((per_dev, half, 1), jnp.float32),
             jax.ShapeDtypeStruct((half, width), jnp.float32),
         ),
     )(
-        cache_from,
+        seen_from,
         queries,
         keys,
-        with_core(keys),
+        with_core(after(keys, seen_from, gate_row)),
         values,
         with_core(values),
         past_keys,
-        with_core(after(past_keys, far)),
+        past_keys_too,
     )
     outs = kernel_call(
         finish_kernel,
-        [SMEM] + [VMEM] * 5 + [ANY],
+        [VMEM] * 6,
         (block(1),) * CHIPS,
-        scratch=[pltpu.VMEM((1, width), jnp.float32), pltpu.SemaphoreType.DMA],
     )(
-        time_index,
         past_weight,
         total,
         numer,
+        gate_row,
         past_values,
         with_core(after(past_values, far)),
-        gate_table,
     )
     returned = [outs[0]] + [to_chip(outs[1 + route], ROUTES[route][0]) for route in OUT_ORDER]
     out = pl.pallas_call(

time: 40.8 us -> 39.3 us (0.963)
  waiting for transfers between devices: 9.15 us -> 7.39 us
  Pallas kernels: 3.42 us -> 4.13 us
    ppermute x11, waiting for transfers between devices: 9.14 us -> 6.95 us  [to_chip(): lax.ppermute(part, 'seq', [(i, 2 * target(i // 2) + i % 2) for i in range...]
    pallas_call x7 -> x8, Pallas kernels: 2.69 us -> 3.4 us  [run(): call(*(pltpu.with_memory_space_constraint(operand, spec.memory_space) if...]
    ppermute x4, waiting for transfers between devices: 0.01 us -> 0.44 us  [with_core(): return lax.ppermute(part, 'seq', [(i, i ^ 1) for i in range(seq)])]
  transfers between devices with their start and end apart: 17 -> 17, of which waited for: 5 -> 6; matrix products, arithmetic and copies ran while one was open for 0% -> 0% of each run, Pallas kernels for 3% -> 5%
where the time goes in v5:
time: 39.3 us; the launch traced here: 39 us
  starting transfers between devices  26 us (66%)
  waiting for transfers between devices  7.39 us (19%)
  Pallas kernels  4.13 us (11%)
  between operations  1.43 us (4%)
    ppermute x11, starting transfers between devices, to_chip(): lax.ppermute(part, 'seq', [(i, 2 * target(i // 2) + i % 2) for i in range...  18.6 us
    ppermute x11, waiting for transfers between devices, to_chip(): lax.ppermute(part, 'seq', [(i, 2 * target(i // 2) + i % 2) for i in range...  6.95 us
    ppermute x2, starting transfers between devices, passed_along(): return lax.ppermute(block, axis, route)  6.82 us
    pallas_call x8, Pallas kernels, run(): call(*(pltpu.with_memory_space_constraint(operand, spec.memory_space) if...  3.4 us
  transfers between devices with their start and end apart: 17, of which 6 were waited for; matrix products, arithmetic and copies ran while one was open for 0% of the time, Pallas kernels for 5%

profile of v5, /device:TPU:0, one launch (start us, length us, event | category | flops | bytes accessed | tf_op | source)
XLA Modules:
  0.0 39.0 jit_solution(10920803559109879377)
XLA Ops:
  0.0 1.3 %shard_map.65 = (bf16[32,1024]{1,0:T(8,128)(2,1)S(1)}, bf16[32,1024]{1,0:T(8,128)(2,1)S(1)}, bf16[32,1024]{1,0:T(8,128)(2,1)S(1)}, bf16[32,1024]{1,0:T(8,128)(2,...) custom-call(bf16[32,4096]{1,0:T(8,128)(2,1)} %bitcast.4, ...), custom_call_target="tpu_custom_call" | custom-call | tf_op jit(solution)/shard_map/pallas_call | solution.py:287
  1.3 5.1 %collective-permute-start = (bf16[32,1024]{1,0:T(8,128)(2,1)S(1)}, bf16[32,1024]{1,0:T(8,128)(2,1)S(1)}, u32[]{:S(2)}, u32[]{:S(2)}) collective-permute-start(bf16[32,1024]{1,0:T(8,128)(2,1)S(1)} %get-tuple-element.32), channel_id=1, source_target_pairs={{0,6},{1,7},{2,4},{3,5},{4,2},{5,3},{6,0},{7,1},{8,14},{9,15},{10,... | collective-permute-start | bytes 196616 | tf_op jit(solution)/shard_map/ppermute | solution.py:314
  6.4 0.0 collective-permute-start.1
  6.4 2.9 %collective-permute-start.2 = (bf16[32,1024]{1,0:T(8,128)(2,1)S(1)}, bf16[32,1024]{1,0:T(8,128)(2,1)S(1)}, u32[]{:S(2)}, u32[]{:S(2)}) collective-permute-start(bf16[32,1024]{1,0:T(8,128)(2,1)S(1)} %get-tuple-element.34), channel_id=1, source_target_pairs={{0,4},{1,5},{2,0},{3,1},{4,6},{5,7},{6,2},{7,3},{8,12},{9,13},{10,... | collective-permute-start | bytes 196616 | tf_op jit(solution)/shard_map/ppermute | solution.py:314
  9.3 0.0 collective-permute-start.6
  9.3 1.5 %collective-permute-start.7 = (bf16[32,1024]{1,0:T(8,128)(2,1)S(1)}, bf16[32,1024]{1,0:T(8,128)(2,1)S(1)}, u32[]{:S(2)}, u32[]{:S(2)}) collective-permute-start(bf16[32,1024]{1,0:T(8,128)(2,1)S(1)} %get-tuple-element.40), channel_id=1, source_target_pairs={{0,6},{1,7},{2,4},{3,5},{4,2},{5,3},{6,0},{7,1},{8,14},{9,15},{10,... | collective-permute-start | bytes 196616 | tf_op jit(solution)/shard_map/ppermute | solution.py:314
  10.8 0.0 collective-permute-done.refs_1_
  10.8 1.5 %collective-permute-start.8 = (bf16[32,1024]{1,0:T(8,128)(2,1)S(1)}, bf16[32,1024]{1,0:T(8,128)(2,1)S(1)}, u32[]{:S(2)}, u32[]{:S(2)}) collective-permute-start(bf16[32,1024]{1,0:T(8,128)(2,1)S(1)} %get-tuple-element.41), channel_id=1, source_target_pairs={{0,4},{1,5},{2,0},{3,1},{4,6},{5,7},{6,2},{7,3},{8,12},{9,13},{10,... | collective-permute-start | bytes 196616 | tf_op jit(solution)/shard_map/ppermute | solution.py:314
  12.2 0.3 collective-permute-done.1.refs_2_
  12.5 0.3 collective-permute-start.5
  12.9 0.0 collective-permute-done.2.refs_3_
  12.9 3.4 %collective-permute-start.3 = (bf16[128,1024]{1,0:T(8,128)(2,1)S(1)}, bf16[128,1024]{1,0:T(8,128)(2,1)S(1)}, u32[]{:S(2)}, u32[]{:S(2)}) collective-permute-start(bf16[128,1024]{1,0:T(8,128)(2,1)S(1)} %shard_map.66.refs_1_), channel_id=1, source_target_pairs={{0,8},{8,16},{16,24},{1,9},{9,17},{17,25},{2,10},{10,18},{18,26},{... | collective-permute-start | bytes 786440 | tf_op jit(solution)/shard_map/ppermute | solution.py:22
  16.3 0.2 collective-permute-done.6.refs_1_
  16.5 0.0 collective-permute-done.7.refs_2_
  16.5 0.6 %collective-permute-done.8.refs_3_ = bf16[32,1024]{1,0:T(8,128)(2,1)S(1)} collective-permute-done((bf16[32,1024]{1,0:T(8,128)(2,1)S(1)}, bf16[32,1024]{1,0:T(8,128)(2,1)S(1)}, u32[]{:S(2)}, u32[]{:S(2)}) %collective-permute-start.8) | collective-permute-done | bytes 65568 | tf_op jit(solution)/shard_map/ppermute | solution.py:314
  17.1 3.4 %collective-permute-start.12 = (bf16[128,1024]{1,0:T(8,128)(2,1)S(1)}, bf16[128,1024]{1,0:T(8,128)(2,1)S(1)}, u32[]{:S(2)}, u32[]{:S(2)}) collective-permute-start(bf16[128,1024]{1,0:T(8,128)(2,1)S(1)} %shard_map.67.refs_3_), channel_id=1, source_target_pairs={{0,8},{8,16},{16,24},{1,9},{9,17},{17,25},{2,10},{10,18},{18,26},{... | collective-permute-start | bytes 786440 | tf_op jit(solution)/shard_map/ppermute | solution.py:22
  20.5 0.0 collective-permute-done.5.refs_1_.near_ref
  20.5 2.5 %collective-permute-start.9 = (bf16[64,1024]{1,0:T(8,128)(2,1)S(1)}, bf16[64,1024]{1,0:T(8,128)(2,1)S(1)}, u32[]{:S(2)}, u32[]{:S(2)}) collective-permute-start(bf16[64,1024]{1,0:T(8,128)(2,1)S(1)} %shard_map.68), channel_id=1, source_target_pairs={{0,4},{1,5},{2,6},{3,7},{4,0},{5,1},{6,2},{7,3},{8,12},{9,13},{10,... | collective-permute-start | bytes 393224 | tf_op jit(solution)/shard_map/ppermute | solution.py:314
  24.3 0.7 %shard_map.64 = (s32[1,256]{1,0:T(1,128)S(1)}, f32[1,1024]{1,0:T(1,128)S(1)}) custom-call(s32[1]{0:T(128)S(6)} %copy.7.cache_ref, s32[1]{0:T(128)S(6)} %copy.8.time_ref, f32[50,4096]{1,0:T(8,128)} %gate_ref.1), custom_call_target="tpu_custom_call" | custom-call | tf_op jit(solution)/shard_map/pallas_call | solution.py:287
  25.1 0.1 collective-permute-start.11
  25.1 0.0 collective-permute-done.3.refs_5_
  25.1 0.5 %collective-permute-start.4 = (bf16[128,1024]{1,0:T(8,128)(2,1)S(1)}, bf16[128,1024]{1,0:T(8,128)(2,1)S(1)}, u32[]{:S(2)}, u32[]{:S(2)}) collective-permute-start(bf16[128,1024]{1,0:T(8,128)(2,1)S(1)} %collective-permute-done.3.refs_5_), channel_id=1, source_target_pairs={{0,1},{1,0},{2,3},{3,2},{4,5},{5,4},{6,7},{7,6},{8,9},{9,8},{10,11... | collective-permute-start | bytes 786440 | tf_op jit(solution)/shard_map/ppermute | solution.py:317
  25.6 0.1 collective-permute-start.10
  25.7 2.3 %collective-permute-done.9.far_ref = bf16[64,1024]{1,0:T(8,128)(2,1)S(1)} collective-permute-done((bf16[64,1024]{1,0:T(8,128)(2,1)S(1)}, bf16[64,1024]{1,0:T(8,128)(2,1)S(1)}, u32[]{:S(2)}, u32[]{:S(2)}) %collective-permute-start.9) | collective-permute-done | bytes 131104 | tf_op jit(solution)/shard_map/ppermute | solution.py:314
  28.0 0.0 collective-permute-done.12.refs_0_
  28.0 0.0 collective-permute-start.13
  28.0 0.0 collective-permute-done.4.refs_6_
  28.1 0.0 collective-permute-done.10.refs_2_
  28.1 0.0 collective-permute-done.11.refs_4_
  28.1 1.0 %shard_map.70 = (bf16[8,128,256]{2,1,0:T(8,128)(2,1)S(1)}, f32[8,128,1]{2,1,0:T(8,128)S(1)}, f32[128,1024]{1,0:T(8,128)S(1)}) custom-call(s32[1,256]{1,0:T(1,128)S(1)} %get-tuple-element.29.from_ref, bf16[128,1024]{1,0:T(8,128)(2,1)S(1)} %shard_map.69.refs_0_, bf16[128,1024]{1,0:T(8,128)(2,1)S(1)} %shard_map.66.refs_1_, ...), custom_call_target="tpu_custom_call" | custom-call | tf_op jit(solution)/shard_map/pallas_call | solution.py:287
  29.1 0.4 %collective-permute-done.13.refs_1_ = bf16[128,1024]{1,0:T(8,128)(2,1)S(1)} collective-permute-done((bf16[128,1024]{1,0:T(8,128)(2,1)S(1)}, bf16[128,1024]{1,0:T(8,128)(2,1)S(1)}, u32[]{:S(2)}, u32[]{:S(2)}) %collective-permute-start.13) | collective-permute-done | bytes 262176 | tf_op jit(solution)/shard_map/ppermute | solution.py:317
  29.6 0.3 shard_map.71
  29.9 0.1 collective-permute-start.14
  30.0 2.7 %collective-permute-start.15 = (bf16[32,1024]{1,0:T(8,128)(2,1)S(1)}, bf16[32,1024]{1,0:T(8,128)(2,1)S(1)}, u32[]{:S(2)}, u32[]{:S(2)}) collective-permute-start(bf16[32,1024]{1,0:T(8,128)(2,1)S(1)} %get-tuple-element.51), channel_id=1, source_target_pairs={{0,6},{1,7},{2,4},{3,5},{4,2},{5,3},{6,0},{7,1},{8,14},{9,15},{10,... | collective-permute-start | bytes 196616 | tf_op jit(solution)/shard_map/ppermute | solution.py:314
  32.7 1.9 %collective-permute-start.16 = (bf16[32,1024]{1,0:T(8,128)(2,1)S(1)}, bf16[32,1024]{1,0:T(8,128)(2,1)S(1)}, u32[]{:S(2)}, u32[]{:S(2)}) collective-permute-start(bf16[32,1024]{1,0:T(8,128)(2,1)S(1)} %get-tuple-element.52), channel_id=1, source_target_pairs={{0,4},{1,5},{2,0},{3,1},{4,6},{5,7},{6,2},{7,3},{8,12},{9,13},{10,... | collective-permute-start | bytes 196616 | tf_op jit(solution)/shard_map/ppermute | solution.py:314
  34.6 3.6 %collective-permute-done.14.refs_1_ = bf16[32,1024]{1,0:T(8,128)(2,1)S(1)} collective-permute-done((bf16[32,1024]{1,0:T(8,128)(2,1)S(1)}, bf16[32,1024]{1,0:T(8,128)(2,1)S(1)}, u32[]{:S(2)}, u32[]{:S(2)}) %collective-permute-start.14) | collective-permute-done | bytes 65568 | tf_op jit(solution)/shard_map/ppermute | solution.py:314
  38.3 0.0 collective-permute-done.15.refs_2_
  38.3 0.0 collective-permute-done.16.refs_3_
  38.3 0.7 %shard_map.72 = bf16[32,4096]{1,0:T(8,128)(2,1)} custom-call(bf16[32,1024]{1,0:T(8,128)(2,1)S(1)} %get-tuple-element.49.refs_0_, bf16[32,1024]{1,0:T(8,128)(2,1)S(1)} %collective-permute-done.14.refs_1_, bf16[32,1024]{1,0:T(8,128)(2,1)S(1)} %collective-permute-done.15.refs_2_, bf16[32,1024]{1,0:T(8,128)(2,1)S(1)} %collective-permute-done.16.refs_3_), custom_call_target="tpu_custom_call" | custom-call | tf_op jit(solution)/shard_map/pallas_call | solution.py:394
  (4 shorter events, 0.1 us)
Async XLA Ops:
  1.3 9.5 %collective-permute-start = (bf16[32,1024]{1,0:T(8,128)(2,1)S(1)}, bf16[32,1024]{1,0:T(8,128)(2,1)S(1)}, u32[]{:S(2)}, u32[]{:S(2)}) collective-permute-start(bf16[32,1024]{1,0:T(8,128)(2,1)S(1)} %get-tuple-element.32), channel_id=1, source_target_pairs={{0,6},{1,7},{2,4},{3,5},{4,2},{5,3},{6,0},{7,1},{8,14},{9,15},{10,... | collective-permute-start | bytes 196616 | tf_op jit(solution)/shard_map/ppermute | solution.py:314
  6.4 6.1 %collective-permute-start.1 = (bf16[32,1024]{1,0:T(8,128)(2,1)S(1)}, bf16[32,1024]{1,0:T(8,128)(2,1)S(1)}, u32[]{:S(2)}, u32[]{:S(2)}) collective-permute-start(bf16[32,1024]{1,0:T(8,128)(2,1)S(1)} %get-tuple-element.33), channel_id=1, source_target_pairs={{0,2},{1,3},{2,6},{3,7},{4,0},{5,1},{6,4},{7,5},{8,10},{9,11},{10,... | collective-permute-start | bytes 196616 | tf_op jit(solution)/shard_map/ppermute | solution.py:314
  6.4 6.5 %collective-permute-start.2 = (bf16[32,1024]{1,0:T(8,128)(2,1)S(1)}, bf16[32,1024]{1,0:T(8,128)(2,1)S(1)}, u32[]{:S(2)}, u32[]{:S(2)}) collective-permute-start(bf16[32,1024]{1,0:T(8,128)(2,1)S(1)} %get-tuple-element.34), channel_id=1, source_target_pairs={{0,4},{1,5},{2,0},{3,1},{4,6},{5,7},{6,2},{7,3},{8,12},{9,13},{10,... | collective-permute-start | bytes 196616 | tf_op jit(solution)/shard_map/ppermute | solution.py:314
  9.3 7.2 %collective-permute-start.6 = (bf16[32,1024]{1,0:T(8,128)(2,1)S(1)}, bf16[32,1024]{1,0:T(8,128)(2,1)S(1)}, u32[]{:S(2)}, u32[]{:S(2)}) collective-permute-start(bf16[32,1024]{1,0:T(8,128)(2,1)S(1)} %get-tuple-element.39), channel_id=1, source_target_pairs={{0,2},{1,3},{2,6},{3,7},{4,0},{5,1},{6,4},{7,5},{8,10},{9,11},{10,... | collective-permute-start | bytes 196616 | tf_op jit(solution)/shard_map/ppermute | solution.py:314
  9.3 7.2 %collective-permute-start.7 = (bf16[32,1024]{1,0:T(8,128)(2,1)S(1)}, bf16[32,1024]{1,0:T(8,128)(2,1)S(1)}, u32[]{:S(2)}, u32[]{:S(2)}) collective-permute-start(bf16[32,1024]{1,0:T(8,128)(2,1)S(1)} %get-tuple-element.40), channel_id=1, source_target_pairs={{0,6},{1,7},{2,4},{3,5},{4,2},{5,3},{6,0},{7,1},{8,14},{9,15},{10,... | collective-permute-start | bytes 196616 | tf_op jit(solution)/shard_map/ppermute | solution.py:314
  10.8 6.3 %collective-permute-start.8 = (bf16[32,1024]{1,0:T(8,128)(2,1)S(1)}, bf16[32,1024]{1,0:T(8,128)(2,1)S(1)}, u32[]{:S(2)}, u32[]{:S(2)}) collective-permute-start(bf16[32,1024]{1,0:T(8,128)(2,1)S(1)} %get-tuple-element.41), channel_id=1, source_target_pairs={{0,4},{1,5},{2,0},{3,1},{4,6},{5,7},{6,2},{7,3},{8,12},{9,13},{10,... | collective-permute-start | bytes 196616 | tf_op jit(solution)/shard_map/ppermute | solution.py:314
  12.5 8.0 %collective-permute-start.5 = (bf16[64,1024]{1,0:T(8,128)(2,1)S(1)}, bf16[64,1024]{1,0:T(8,128)(2,1)S(1)}, u32[]{:S(2)}, u32[]{:S(2)}) collective-permute-start(bf16[64,1024]{1,0:T(8,128)(2,1)S(1)} %get-tuple-element.36), channel_id=1, source_target_pairs={{0,2},{1,3},{2,0},{3,1},{4,6},{5,7},{6,4},{7,5},{8,10},{9,11},{10,... | collective-permute-start | bytes 393224 | tf_op jit(solution)/shard_map/ppermute | solution.py:314
  12.9 12.2 %collective-permute-start.3 = (bf16[128,1024]{1,0:T(8,128)(2,1)S(1)}, bf16[128,1024]{1,0:T(8,128)(2,1)S(1)}, u32[]{:S(2)}, u32[]{:S(2)}) collective-permute-start(bf16[128,1024]{1,0:T(8,128)(2,1)S(1)} %shard_map.66.refs_1_), channel_id=1, source_target_pairs={{0,8},{8,16},{16,24},{1,9},{9,17},{17,25},{2,10},{10,18},{18,26},{... | collective-permute-start | bytes 786440 | tf_op jit(solution)/shard_map/ppermute | solution.py:22
  17.1 11.0 %collective-permute-start.12 = (bf16[128,1024]{1,0:T(8,128)(2,1)S(1)}, bf16[128,1024]{1,0:T(8,128)(2,1)S(1)}, u32[]{:S(2)}, u32[]{:S(2)}) collective-permute-start(bf16[128,1024]{1,0:T(8,128)(2,1)S(1)} %shard_map.67.refs_3_), channel_id=1, source_target_pairs={{0,8},{8,16},{16,24},{1,9},{9,17},{17,25},{2,10},{10,18},{18,26},{... | collective-permute-start | bytes 786440 | tf_op jit(solution)/shard_map/ppermute | solution.py:22
  20.5 7.5 %collective-permute-start.9 = (bf16[64,1024]{1,0:T(8,128)(2,1)S(1)}, bf16[64,1024]{1,0:T(8,128)(2,1)S(1)}, u32[]{:S(2)}, u32[]{:S(2)}) collective-permute-start(bf16[64,1024]{1,0:T(8,128)(2,1)S(1)} %shard_map.68), channel_id=1, source_target_pairs={{0,4},{1,5},{2,6},{3,7},{4,0},{5,1},{6,2},{7,3},{8,12},{9,13},{10,... | collective-permute-start | bytes 393224 | tf_op jit(solution)/shard_map/ppermute | solution.py:314
  25.1 3.0 %collective-permute-start.11 = (bf16[128,1024]{1,0:T(8,128)(2,1)S(1)}, bf16[128,1024]{1,0:T(8,128)(2,1)S(1)}, u32[]{:S(2)}, u32[]{:S(2)}) collective-permute-start(bf16[128,1024]{1,0:T(8,128)(2,1)S(1)} %shard_map.67.refs_3_), channel_id=1, source_target_pairs={{0,1},{1,0},{2,3},{3,2},{4,5},{5,4},{6,7},{7,6},{8,9},{9,8},{10,11... | collective-permute-start | bytes 786440 | tf_op jit(solution)/shard_map/ppermute | solution.py:317
  25.1 2.9 %collective-permute-start.4 = (bf16[128,1024]{1,0:T(8,128)(2,1)S(1)}, bf16[128,1024]{1,0:T(8,128)(2,1)S(1)}, u32[]{:S(2)}, u32[]{:S(2)}) collective-permute-start(bf16[128,1024]{1,0:T(8,128)(2,1)S(1)} %collective-permute-done.3.refs_5_), channel_id=1, source_target_pairs={{0,1},{1,0},{2,3},{3,2},{4,5},{5,4},{6,7},{7,6},{8,9},{9,8},{10,11... | collective-permute-start | bytes 786440 | tf_op jit(solution)/shard_map/ppermute | solution.py:317
  25.6 2.4 %collective-permute-start.10 = (bf16[128,1024]{1,0:T(8,128)(2,1)S(1)}, bf16[128,1024]{1,0:T(8,128)(2,1)S(1)}, u32[]{:S(2)}, u32[]{:S(2)}) collective-permute-start(bf16[128,1024]{1,0:T(8,128)(2,1)S(1)} %shard_map.66.refs_1_), channel_id=1, source_target_pairs={{0,1},{1,0},{2,3},{3,2},{4,5},{5,4},{6,7},{7,6},{8,9},{9,8},{10,11... | collective-permute-start | bytes 786440 | tf_op jit(solution)/shard_map/ppermute | solution.py:317
  28.0 1.5 %collective-permute-start.13 = (bf16[128,1024]{1,0:T(8,128)(2,1)S(1)}, bf16[128,1024]{1,0:T(8,128)(2,1)S(1)}, u32[]{:S(2)}, u32[]{:S(2)}) collective-permute-start(bf16[128,1024]{1,0:T(8,128)(2,1)S(1)} %collective-permute-done.12.refs_0_), channel_id=1, source_target_pairs={{0,1},{1,0},{2,3},{3,2},{4,5},{5,4},{6,7},{7,6},{8,9},{9,8},{10,11... | collective-permute-start | bytes 786440 | tf_op jit(solution)/shard_map/ppermute | solution.py:317
  29.9 8.4 %collective-permute-start.14 = (bf16[32,1024]{1,0:T(8,128)(2,1)S(1)}, bf16[32,1024]{1,0:T(8,128)(2,1)S(1)}, u32[]{:S(2)}, u32[]{:S(2)}) collective-permute-start(bf16[32,1024]{1,0:T(8,128)(2,1)S(1)} %get-tuple-element.50), channel_id=1, source_target_pairs={{0,2},{1,3},{2,6},{3,7},{4,0},{5,1},{6,4},{7,5},{8,10},{9,11},{10,... | collective-permute-start | bytes 196616 | tf_op jit(solution)/shard_map/ppermute | solution.py:314
  30.0 8.3 %collective-permute-start.15 = (bf16[32,1024]{1,0:T(8,128)(2,1)S(1)}, bf16[32,1024]{1,0:T(8,128)(2,1)S(1)}, u32[]{:S(2)}, u32[]{:S(2)}) collective-permute-start(bf16[32,1024]{1,0:T(8,128)(2,1)S(1)} %get-tuple-element.51), channel_id=1, source_target_pairs={{0,6},{1,7},{2,4},{3,5},{4,2},{5,3},{6,0},{7,1},{8,14},{9,15},{10,... | collective-permute-start | bytes 196616 | tf_op jit(solution)/shard_map/ppermute | solution.py:314
  32.7 5.6 %collective-permute-start.16 = (bf16[32,1024]{1,0:T(8,128)(2,1)S(1)}, bf16[32,1024]{1,0:T(8,128)(2,1)S(1)}, u32[]{:S(2)}, u32[]{:S(2)}) collective-permute-start(bf16[32,1024]{1,0:T(8,128)(2,1)S(1)} %get-tuple-element.52), channel_id=1, source_target_pairs={{0,4},{1,5},{2,0},{3,1},{4,6},{5,7},{6,2},{7,3},{8,12},{9,13},{10,... | collective-permute-start | bytes 196616 | tf_op jit(solution)/shard_map/ppermute | solution.py:314

commit v6 on v5

--- a/solution.py
+++ b/solution.py
@@ -196,7 +196,7 @@
     queries, refs = refs[0], refs[1:]
     chips = CHIPS
     key_refs, value_refs, past_refs = refs[0:2], refs[2:4], refs[4:6]
-    past_weight_ref, total_ref, numer_ref = refs[6:9]
+    past_value_ref, past_weight_ref, total_ref, numer_ref = refs[6:10]
     half, width = queries.shape
     rows = half // chips
     core = lax.rem(lax.axis_index("seq"), 2)
@@ -224,8 +224,10 @@
         past = product(query, past_key, ((1,), (1,)))
         return own, past, value
 
-    def mix(head, own, value):
-        numer_ref[:, pl.ds(head * HD, HD)] = product(own, value, ((1,), (0,)))
+    def mix(head, own, value, past):
+        lanes = pl.ds(head * HD, HD)
+        here = product(past, past_value_ref[:, lanes], ((1,), (0,)))
+        numer_ref[:, lanes] = product(own, value, ((1,), (0,))) + here
 
     heads = width // HD
     ready, weighed = scores(0), None
@@ -240,18 +242,18 @@
         own = jnp.exp2((own - largest) * scale)
         past = jnp.exp2((past - largest) * scale)
         total_ref[head] = jnp.sum(own + past, axis=1, keepdims=True)
-        past_weight_ref[head] = past.astype(jnp.bfloat16)
-        weighed = (head, own.astype(jnp.bfloat16), value)
+        past = past.astype(jnp.bfloat16)
+        past_weight_ref[head] = past[:, half:]
+        weighed = (head, own.astype(jnp.bfloat16), value, past[:, :half])
     mix(*weighed)
 
 
 def finish_kernel(past_weight_ref, total_ref, numer_ref, gate_row, *refs):
-    past_refs, outs = refs[:2], refs[2:]
+    past_ref, outs = refs[0], refs[1:]
     rows, width = outs[0].shape
     for head in range(width // HD):
         lanes = pl.ds(head * HD, HD)
-        past_value = jnp.concatenate([ref[:, lanes] for ref in past_refs], axis=0)
-        numer = numer_ref[:, lanes] + product(past_weight_ref[head], past_value, ((1,), (0,)))
+        numer = numer_ref[:, lanes] + product(past_weight_ref[head], past_ref[:, lanes], ((1,), (0,)))
         attended = (numer / total_ref[head]).astype(jnp.bfloat16)
         gated = (attended.astype(jnp.float32) * gate_row[:, lanes]).astype(jnp.bfloat16)
         for place in range(CHIPS):
@@ -362,9 +364,9 @@
     )(cache_from, time_index, gate_table)
     past_weight, total, numer = kernel_call(
         weigh_kernel,
-        [VMEM] * 8,
+        [VMEM] * 9,
         (
-            jax.ShapeDtypeStruct((per_dev, half, 2 * half), jnp.bfloat16),
+            jax.ShapeDtypeStruct((per_dev, half, half), jnp.bfloat16),
             jax.ShapeDtypeStruct((per_dev, half, 1), jnp.float32),
             jax.ShapeDtypeStruct((half, width), jnp.float32),
         ),
@@ -377,17 +379,17 @@
         with_core(values),
         past_keys,
         past_keys_too,
+        past_values,
     )
     outs = kernel_call(
         finish_kernel,
-        [VMEM] * 6,
+        [VMEM] * 5,
         (block(1),) * CHIPS,
     )(
         past_weight,
         total,
         numer,
         gate_row,
-        past_values,
         with_core(after(past_values, far)),
     )
     returned = [outs[0]] + [to_chip(outs[1 + route], ROUTES[route][0]) for route in OUT_ORDER]

time: 39.3 us -> 39.1 us (level)
  no operation moved by 1% of the time
where the time goes in v6:
time: 39.1 us; the launch traced here: 38.9 us
  starting transfers between devices  26 us (66%)
  waiting for transfers between devices  7.2 us (18%)
  Pallas kernels  4.19 us (11%)
  between operations  1.43 us (4%)
    ppermute x11, starting transfers between devices, to_chip(): lax.ppermute(part, 'seq', [(i, 2 * target(i // 2) + i % 2) for i in range...  18.6 us
    ppermute x11, waiting for transfers between devices, to_chip(): lax.ppermute(part, 'seq', [(i, 2 * target(i // 2) + i % 2) for i in range...  6.87 us
    ppermute x2, starting transfers between devices, passed_along(): return lax.ppermute(block, axis, route)  6.82 us
    pallas_call x8, Pallas kernels, run(): call(*(pltpu.with_memory_space_constraint(operand, spec.memory_space) if...  3.46 us
  transfers between devices with their start and end apart: 17, of which 6 were waited for; matrix products, arithmetic and copies ran while one was open for 0% of the time, Pallas kernels for 5%

profile of v6, /device:TPU:0, one launch (start us, length us, event | category | flops | bytes accessed | tf_op | source)
XLA Modules:
  0.0 38.9 jit_solution(2213016784648886926)
XLA Ops:
  0.0 1.3 %shard_map.65 = (bf16[32,1024]{1,0:T(8,128)(2,1)S(1)}, bf16[32,1024]{1,0:T(8,128)(2,1)S(1)}, bf16[32,1024]{1,0:T(8,128)(2,1)S(1)}, bf16[32,1024]{1,0:T(8,128)(2,...) custom-call(bf16[32,4096]{1,0:T(8,128)(2,1)} %bitcast.4, ...), custom_call_target="tpu_custom_call" | custom-call | tf_op jit(solution)/shard_map/pallas_call | solution.py:289
  1.3 5.1 %collective-permute-start = (bf16[32,1024]{1,0:T(8,128)(2,1)S(1)}, bf16[32,1024]{1,0:T(8,128)(2,1)S(1)}, u32[]{:S(2)}, u32[]{:S(2)}) collective-permute-start(bf16[32,1024]{1,0:T(8,128)(2,1)S(1)} %get-tuple-element.32), channel_id=1, source_target_pairs={{0,6},{1,7},{2,4},{3,5},{4,2},{5,3},{6,0},{7,1},{8,14},{9,15},{10,... | collective-permute-start | bytes 196616 | tf_op jit(solution)/shard_map/ppermute | solution.py:316
  6.4 0.0 collective-permute-start.1
  6.4 2.9 %collective-permute-start.2 = (bf16[32,1024]{1,0:T(8,128)(2,1)S(1)}, bf16[32,1024]{1,0:T(8,128)(2,1)S(1)}, u32[]{:S(2)}, u32[]{:S(2)}) collective-permute-start(bf16[32,1024]{1,0:T(8,128)(2,1)S(1)} %get-tuple-element.34), channel_id=1, source_target_pairs={{0,4},{1,5},{2,0},{3,1},{4,6},{5,7},{6,2},{7,3},{8,12},{9,13},{10,... | collective-permute-start | bytes 196616 | tf_op jit(solution)/shard_map/ppermute | solution.py:316
  9.3 0.0 collective-permute-start.6
  9.3 1.5 %collective-permute-start.7 = (bf16[32,1024]{1,0:T(8,128)(2,1)S(1)}, bf16[32,1024]{1,0:T(8,128)(2,1)S(1)}, u32[]{:S(2)}, u32[]{:S(2)}) collective-permute-start(bf16[32,1024]{1,0:T(8,128)(2,1)S(1)} %get-tuple-element.40), channel_id=1, source_target_pairs={{0,6},{1,7},{2,4},{3,5},{4,2},{5,3},{6,0},{7,1},{8,14},{9,15},{10,... | collective-permute-start | bytes 196616 | tf_op jit(solution)/shard_map/ppermute | solution.py:316
  10.8 0.0 collective-permute-done.refs_1_
  10.8 1.5 %collective-permute-start.8 = (bf16[32,1024]{1,0:T(8,128)(2,1)S(1)}, bf16[32,1024]{1,0:T(8,128)(2,1)S(1)}, u32[]{:S(2)}, u32[]{:S(2)}) collective-permute-start(bf16[32,1024]{1,0:T(8,128)(2,1)S(1)} %get-tuple-element.41), channel_id=1, source_target_pairs={{0,4},{1,5},{2,0},{3,1},{4,6},{5,7},{6,2},{7,3},{8,12},{9,13},{10,... | collective-permute-start | bytes 196616 | tf_op jit(solution)/shard_map/ppermute | solution.py:316
  12.2 0.3 collective-permute-done.1.refs_2_
  12.5 0.3 collective-permute-start.5
  12.9 0.0 collective-permute-done.2.refs_3_
  12.9 3.4 %collective-permute-start.3 = (bf16[128,1024]{1,0:T(8,128)(2,1)S(1)}, bf16[128,1024]{1,0:T(8,128)(2,1)S(1)}, u32[]{:S(2)}, u32[]{:S(2)}) collective-permute-start(bf16[128,1024]{1,0:T(8,128)(2,1)S(1)} %shard_map.66.refs_1_), channel_id=1, source_target_pairs={{0,8},{8,16},{16,24},{1,9},{9,17},{17,25},{2,10},{10,18},{18,26},{... | collective-permute-start | bytes 786440 | tf_op jit(solution)/shard_map/ppermute | solution.py:22
  16.3 0.2 collective-permute-done.6.refs_1_
  16.5 0.0 collective-permute-done.7.refs_2_
  16.5 0.6 %collective-permute-done.8.refs_3_ = bf16[32,1024]{1,0:T(8,128)(2,1)S(1)} collective-permute-done((bf16[32,1024]{1,0:T(8,128)(2,1)S(1)}, bf16[32,1024]{1,0:T(8,128)(2,1)S(1)}, u32[]{:S(2)}, u32[]{:S(2)}) %collective-permute-start.8) | collective-permute-done | bytes 65568 | tf_op jit(solution)/shard_map/ppermute | solution.py:316
  17.1 3.4 %collective-permute-start.12 = (bf16[128,1024]{1,0:T(8,128)(2,1)S(1)}, bf16[128,1024]{1,0:T(8,128)(2,1)S(1)}, u32[]{:S(2)}, u32[]{:S(2)}) collective-permute-start(bf16[128,1024]{1,0:T(8,128)(2,1)S(1)} %shard_map.67.refs_3_), channel_id=1, source_target_pairs={{0,8},{8,16},{16,24},{1,9},{9,17},{17,25},{2,10},{10,18},{18,26},{... | collective-permute-start | bytes 786440 | tf_op jit(solution)/shard_map/ppermute | solution.py:22
  20.5 0.0 collective-permute-done.5.refs_1_.near_ref
  20.5 2.5 %collective-permute-start.9 = (bf16[64,1024]{1,0:T(8,128)(2,1)S(1)}, bf16[64,1024]{1,0:T(8,128)(2,1)S(1)}, u32[]{:S(2)}, u32[]{:S(2)}) collective-permute-start(bf16[64,1024]{1,0:T(8,128)(2,1)S(1)} %shard_map.68), channel_id=1, source_target_pairs={{0,4},{1,5},{2,6},{3,7},{4,0},{5,1},{6,2},{7,3},{8,12},{9,13},{10,... | collective-permute-start | bytes 393224 | tf_op jit(solution)/shard_map/ppermute | solution.py:316
  24.3 0.7 %shard_map.64 = (s32[1,256]{1,0:T(1,128)S(1)}, f32[1,1024]{1,0:T(1,128)S(1)}) custom-call(s32[1]{0:T(128)S(6)} %copy.7.cache_ref, s32[1]{0:T(128)S(6)} %copy.8.time_ref, f32[50,4096]{1,0:T(8,128)} %gate_ref.1), custom_call_target="tpu_custom_call" | custom-call | tf_op jit(solution)/shard_map/pallas_call | solution.py:289
  25.1 0.1 collective-permute-start.11
  25.1 0.0 collective-permute-done.3.refs_5_
  25.1 0.5 %collective-permute-start.4 = (bf16[128,1024]{1,0:T(8,128)(2,1)S(1)}, bf16[128,1024]{1,0:T(8,128)(2,1)S(1)}, u32[]{:S(2)}, u32[]{:S(2)}) collective-permute-start(bf16[128,1024]{1,0:T(8,128)(2,1)S(1)} %collective-permute-done.3.refs_5_), channel_id=1, source_target_pairs={{0,1},{1,0},{2,3},{3,2},{4,5},{5,4},{6,7},{7,6},{8,9},{9,8},{10,11... | collective-permute-start | bytes 786440 | tf_op jit(solution)/shard_map/ppermute | solution.py:319
  25.6 0.1 collective-permute-start.10
  25.7 2.3 %collective-permute-done.9.far_ref = bf16[64,1024]{1,0:T(8,128)(2,1)S(1)} collective-permute-done((bf16[64,1024]{1,0:T(8,128)(2,1)S(1)}, bf16[64,1024]{1,0:T(8,128)(2,1)S(1)}, u32[]{:S(2)}, u32[]{:S(2)}) %collective-permute-start.9) | collective-permute-done | bytes 131104 | tf_op jit(solution)/shard_map/ppermute | solution.py:316
  28.0 0.0 collective-permute-done.12.refs_7_
  28.0 0.0 collective-permute-start.13
  28.0 0.0 collective-permute-done.4.refs_6_
  28.1 0.0 collective-permute-done.10.refs_2_
  28.1 0.0 collective-permute-done.11.refs_4_
  28.1 1.1 %shard_map.70 = (bf16[8,128,128]{2,1,0:T(8,128)(2,1)S(1)}, f32[8,128,1]{2,1,0:T(8,128)S(1)}, f32[128,1024]{1,0:T(8,128)S(1)}) custom-call(s32[1,256]{1,0:T(1,128)S(1)} %get-tuple-element.29.from_ref, bf16[128,1024]{1,0:T(8,128)(2,1)S(1)} %shard_map.69.refs_0_, bf16[128,1024]{1,0:T(8,128)(2,1)S(1)} %shard_map.66.refs_1_, ...), custom_call_target="tpu_custom_call" | custom-call | tf_op jit(solution)/shard_map/pallas_call | solution.py:289
  29.2 0.3 collective-permute-done.13.refs_0_
  29.6 0.3 shard_map.71
  29.8 0.1 collective-permute-start.14
  29.9 2.7 %collective-permute-start.15 = (bf16[32,1024]{1,0:T(8,128)(2,1)S(1)}, bf16[32,1024]{1,0:T(8,128)(2,1)S(1)}, u32[]{:S(2)}, u32[]{:S(2)}) collective-permute-start(bf16[32,1024]{1,0:T(8,128)(2,1)S(1)} %get-tuple-element.51), channel_id=1, source_target_pairs={{0,6},{1,7},{2,4},{3,5},{4,2},{5,3},{6,0},{7,1},{8,14},{9,15},{10,... | collective-permute-start | bytes 196616 | tf_op jit(solution)/shard_map/ppermute | solution.py:316
  32.6 1.9 %collective-permute-start.16 = (bf16[32,1024]{1,0:T(8,128)(2,1)S(1)}, bf16[32,1024]{1,0:T(8,128)(2,1)S(1)}, u32[]{:S(2)}, u32[]{:S(2)}) collective-permute-start(bf16[32,1024]{1,0:T(8,128)(2,1)S(1)} %get-tuple-element.52), channel_id=1, source_target_pairs={{0,4},{1,5},{2,0},{3,1},{4,6},{5,7},{6,2},{7,3},{8,12},{9,13},{10,... | collective-permute-start | bytes 196616 | tf_op jit(solution)/shard_map/ppermute | solution.py:316
  34.6 3.5 %collective-permute-done.14.refs_1_ = bf16[32,1024]{1,0:T(8,128)(2,1)S(1)} collective-permute-done((bf16[32,1024]{1,0:T(8,128)(2,1)S(1)}, bf16[32,1024]{1,0:T(8,128)(2,1)S(1)}, u32[]{:S(2)}, u32[]{:S(2)}) %collective-permute-start.14) | collective-permute-done | bytes 65568 | tf_op jit(solution)/shard_map/ppermute | solution.py:316
  38.1 0.0 collective-permute-done.15.refs_2_
  38.1 0.0 collective-permute-done.16.refs_3_
  38.1 0.7 %shard_map.72 = bf16[32,4096]{1,0:T(8,128)(2,1)} custom-call(bf16[32,1024]{1,0:T(8,128)(2,1)S(1)} %get-tuple-element.49.refs_0_, bf16[32,1024]{1,0:T(8,128)(2,1)S(1)} %collective-permute-done.14.refs_1_, bf16[32,1024]{1,0:T(8,128)(2,1)S(1)} %collective-permute-done.15.refs_2_, bf16[32,1024]{1,0:T(8,128)(2,1)S(1)} %collective-permute-done.16.refs_3_), custom_call_target="tpu_custom_call" | custom-call | tf_op jit(solution)/shard_map/pallas_call | solution.py:396
  (4 shorter events, 0.1 us)
Async XLA Ops:
  1.3 9.5 %collective-permute-start = (bf16[32,1024]{1,0:T(8,128)(2,1)S(1)}, bf16[32,1024]{1,0:T(8,128)(2,1)S(1)}, u32[]{:S(2)}, u32[]{:S(2)}) collective-permute-start(bf16[32,1024]{1,0:T(8,128)(2,1)S(1)} %get-tuple-element.32), channel_id=1, source_target_pairs={{0,6},{1,7},{2,4},{3,5},{4,2},{5,3},{6,0},{7,1},{8,14},{9,15},{10,... | collective-permute-start | bytes 196616 | tf_op jit(solution)/shard_map/ppermute | solution.py:316
  6.4 6.1 %collective-permute-start.1 = (bf16[32,1024]{1,0:T(8,128)(2,1)S(1)}, bf16[32,1024]{1,0:T(8,128)(2,1)S(1)}, u32[]{:S(2)}, u32[]{:S(2)}) collective-permute-start(bf16[32,1024]{1,0:T(8,128)(2,1)S(1)} %get-tuple-element.33), channel_id=1, source_target_pairs={{0,2},{1,3},{2,6},{3,7},{4,0},{5,1},{6,4},{7,5},{8,10},{9,11},{10,... | collective-permute-start | bytes 196616 | tf_op jit(solution)/shard_map/ppermute | solution.py:316
  6.4 6.5 %collective-permute-start.2 = (bf16[32,1024]{1,0:T(8,128)(2,1)S(1)}, bf16[32,1024]{1,0:T(8,128)(2,1)S(1)}, u32[]{:S(2)}, u32[]{:S(2)}) collective-permute-start(bf16[32,1024]{1,0:T(8,128)(2,1)S(1)} %get-tuple-element.34), channel_id=1, source_target_pairs={{0,4},{1,5},{2,0},{3,1},{4,6},{5,7},{6,2},{7,3},{8,12},{9,13},{10,... | collective-permute-start | bytes 196616 | tf_op jit(solution)/shard_map/ppermute | solution.py:316
  9.3 7.2 %collective-permute-start.6 = (bf16[32,1024]{1,0:T(8,128)(2,1)S(1)}, bf16[32,1024]{1,0:T(8,128)(2,1)S(1)}, u32[]{:S(2)}, u32[]{:S(2)}) collective-permute-start(bf16[32,1024]{1,0:T(8,128)(2,1)S(1)} %get-tuple-element.39), channel_id=1, source_target_pairs={{0,2},{1,3},{2,6},{3,7},{4,0},{5,1},{6,4},{7,5},{8,10},{9,11},{10,... | collective-permute-start | bytes 196616 | tf_op jit(solution)/shard_map/ppermute | solution.py:316
  9.3 7.2 %collective-permute-start.7 = (bf16[32,1024]{1,0:T(8,128)(2,1)S(1)}, bf16[32,1024]{1,0:T(8,128)(2,1)S(1)}, u32[]{:S(2)}, u32[]{:S(2)}) collective-permute-start(bf16[32,1024]{1,0:T(8,128)(2,1)S(1)} %get-tuple-element.40), channel_id=1, source_target_pairs={{0,6},{1,7},{2,4},{3,5},{4,2},{5,3},{6,0},{7,1},{8,14},{9,15},{10,... | collective-permute-start | bytes 196616 | tf_op jit(solution)/shard_map/ppermute | solution.py:316
  10.8 6.3 %collective-permute-start.8 = (bf16[32,1024]{1,0:T(8,128)(2,1)S(1)}, bf16[32,1024]{1,0:T(8,128)(2,1)S(1)}, u32[]{:S(2)}, u32[]{:S(2)}) collective-permute-start(bf16[32,1024]{1,0:T(8,128)(2,1)S(1)} %get-tuple-element.41), channel_id=1, source_target_pairs={{0,4},{1,5},{2,0},{3,1},{4,6},{5,7},{6,2},{7,3},{8,12},{9,13},{10,... | collective-permute-start | bytes 196616 | tf_op jit(solution)/shard_map/ppermute | solution.py:316
  12.5 8.0 %collective-permute-start.5 = (bf16[64,1024]{1,0:T(8,128)(2,1)S(1)}, bf16[64,1024]{1,0:T(8,128)(2,1)S(1)}, u32[]{:S(2)}, u32[]{:S(2)}) collective-permute-start(bf16[64,1024]{1,0:T(8,128)(2,1)S(1)} %get-tuple-element.36), channel_id=1, source_target_pairs={{0,2},{1,3},{2,0},{3,1},{4,6},{5,7},{6,4},{7,5},{8,10},{9,11},{10,... | collective-permute-start | bytes 393224 | tf_op jit(solution)/shard_map/ppermute | solution.py:316
  12.9 12.2 %collective-permute-start.3 = (bf16[128,1024]{1,0:T(8,128)(2,1)S(1)}, bf16[128,1024]{1,0:T(8,128)(2,1)S(1)}, u32[]{:S(2)}, u32[]{:S(2)}) collective-permute-start(bf16[128,1024]{1,0:T(8,128)(2,1)S(1)} %shard_map.66.refs_1_), channel_id=1, source_target_pairs={{0,8},{8,16},{16,24},{1,9},{9,17},{17,25},{2,10},{10,18},{18,26},{... | collective-permute-start | bytes 786440 | tf_op jit(solution)/shard_map/ppermute | solution.py:22
  17.1 11.0 %collective-permute-start.12 = (bf16[128,1024]{1,0:T(8,128)(2,1)S(1)}, bf16[128,1024]{1,0:T(8,128)(2,1)S(1)}, u32[]{:S(2)}, u32[]{:S(2)}) collective-permute-start(bf16[128,1024]{1,0:T(8,128)(2,1)S(1)} %shard_map.67.refs_3_), channel_id=1, source_target_pairs={{0,8},{8,16},{16,24},{1,9},{9,17},{17,25},{2,10},{10,18},{18,26},{... | collective-permute-start | bytes 786440 | tf_op jit(solution)/shard_map/ppermute | solution.py:22
  20.5 7.5 %collective-permute-start.9 = (bf16[64,1024]{1,0:T(8,128)(2,1)S(1)}, bf16[64,1024]{1,0:T(8,128)(2,1)S(1)}, u32[]{:S(2)}, u32[]{:S(2)}) collective-permute-start(bf16[64,1024]{1,0:T(8,128)(2,1)S(1)} %shard_map.68), channel_id=1, source_target_pairs={{0,4},{1,5},{2,6},{3,7},{4,0},{5,1},{6,2},{7,3},{8,12},{9,13},{10,... | collective-permute-start | bytes 393224 | tf_op jit(solution)/shard_map/ppermute | solution.py:316
  25.1 3.0 %collective-permute-start.11 = (bf16[128,1024]{1,0:T(8,128)(2,1)S(1)}, bf16[128,1024]{1,0:T(8,128)(2,1)S(1)}, u32[]{:S(2)}, u32[]{:S(2)}) collective-permute-start(bf16[128,1024]{1,0:T(8,128)(2,1)S(1)} %shard_map.67.refs_3_), channel_id=1, source_target_pairs={{0,1},{1,0},{2,3},{3,2},{4,5},{5,4},{6,7},{7,6},{8,9},{9,8},{10,11... | collective-permute-start | bytes 786440 | tf_op jit(solution)/shard_map/ppermute | solution.py:319
  25.1 2.9 %collective-permute-start.4 = (bf16[128,1024]{1,0:T(8,128)(2,1)S(1)}, bf16[128,1024]{1,0:T(8,128)(2,1)S(1)}, u32[]{:S(2)}, u32[]{:S(2)}) collective-permute-start(bf16[128,1024]{1,0:T(8,128)(2,1)S(1)} %collective-permute-done.3.refs_5_), channel_id=1, source_target_pairs={{0,1},{1,0},{2,3},{3,2},{4,5},{5,4},{6,7},{7,6},{8,9},{9,8},{10,11... | collective-permute-start | bytes 786440 | tf_op jit(solution)/shard_map/ppermute | solution.py:319
  25.6 2.4 %collective-permute-start.10 = (bf16[128,1024]{1,0:T(8,128)(2,1)S(1)}, bf16[128,1024]{1,0:T(8,128)(2,1)S(1)}, u32[]{:S(2)}, u32[]{:S(2)}) collective-permute-start(bf16[128,1024]{1,0:T(8,128)(2,1)S(1)} %shard_map.66.refs_1_), channel_id=1, source_target_pairs={{0,1},{1,0},{2,3},{3,2},{4,5},{5,4},{6,7},{7,6},{8,9},{9,8},{10,11... | collective-permute-start | bytes 786440 | tf_op jit(solution)/shard_map/ppermute | solution.py:319
  28.0 1.5 %collective-permute-start.13 = (bf16[128,1024]{1,0:T(8,128)(2,1)S(1)}, bf16[128,1024]{1,0:T(8,128)(2,1)S(1)}, u32[]{:S(2)}, u32[]{:S(2)}) collective-permute-start(bf16[128,1024]{1,0:T(8,128)(2,1)S(1)} %collective-permute-done.12.refs_7_), channel_id=1, source_target_pairs={{0,1},{1,0},{2,3},{3,2},{4,5},{5,4},{6,7},{7,6},{8,9},{9,8},{10,11... | collective-permute-start | bytes 786440 | tf_op jit(solution)/shard_map/ppermute | solution.py:319
  29.8 8.3 %collective-permute-start.14 = (bf16[32,1024]{1,0:T(8,128)(2,1)S(1)}, bf16[32,1024]{1,0:T(8,128)(2,1)S(1)}, u32[]{:S(2)}, u32[]{:S(2)}) collective-permute-start(bf16[32,1024]{1,0:T(8,128)(2,1)S(1)} %get-tuple-element.50), channel_id=1, source_target_pairs={{0,2},{1,3},{2,6},{3,7},{4,0},{5,1},{6,4},{7,5},{8,10},{9,11},{10,... | collective-permute-start | bytes 196616 | tf_op jit(solution)/shard_map/ppermute | solution.py:316
  29.9 8.2 %collective-permute-start.15 = (bf16[32,1024]{1,0:T(8,128)(2,1)S(1)}, bf16[32,1024]{1,0:T(8,128)(2,1)S(1)}, u32[]{:S(2)}, u32[]{:S(2)}) collective-permute-start(bf16[32,1024]{1,0:T(8,128)(2,1)S(1)} %get-tuple-element.51), channel_id=1, source_target_pairs={{0,6},{1,7},{2,4},{3,5},{4,2},{5,3},{6,0},{7,1},{8,14},{9,15},{10,... | collective-permute-start | bytes 196616 | tf_op jit(solution)/shard_map/ppermute | solution.py:316
  32.6 5.5 %collective-permute-start.16 = (bf16[32,1024]{1,0:T(8,128)(2,1)S(1)}, bf16[32,1024]{1,0:T(8,128)(2,1)S(1)}, u32[]{:S(2)}, u32[]{:S(2)}) collective-permute-start(bf16[32,1024]{1,0:T(8,128)(2,1)S(1)} %get-tuple-element.52), channel_id=1, source_target_pairs={{0,4},{1,5},{2,0},{3,1},{4,6},{5,7},{6,2},{7,3},{8,12},{9,13},{10,... | collective-permute-start | bytes 196616 | tf_op jit(solution)/shard_map/ppermute | solution.py:316

commit v7 on v6

--- a/solution.py
+++ b/solution.py
@@ -267,8 +267,13 @@
     sources = [chip] + [ROUTES[route][1](chip) for route in OUT_ORDER]
     run_copies(
         [
-            pltpu.make_async_copy(part, out_ref.at[:, span_of(source, width)], sems.at[place])
+            pltpu.make_async_copy(
+                part.at[pl.ds(piece * 16, 16)],
+                out_ref.at[pl.ds(piece * 16, 16), span_of(source, width)],
+                sems.at[place, piece],
+            )
             for place, (part, source) in enumerate(zip(parts, sources))
+            for piece in range(part.shape[0] // 16)
         ]
     )
 
@@ -398,7 +403,7 @@
         out_shape=jax.ShapeDtypeStruct((rows, HEADS * HD), jnp.bfloat16),
         in_specs=[VMEM] * CHIPS,
         out_specs=ANY,
-        scratch_shapes=[pltpu.SemaphoreType.DMA((CHIPS,))],
+        scratch_shapes=[pltpu.SemaphoreType.DMA((CHIPS, rows // 16))],
     )(*(pltpu.with_memory_space_constraint(part, pltpu.VMEM) for part in returned))
     return out[None]
 

time: 39.1 us -> 39.2 us (level)
  no operation moved by 1% of the time
where the time goes in v7:
time: 39.2 us; the launch traced here: 38.9 us
  starting transfers between devices  26 us (66%)
  waiting for transfers between devices  7.2 us (18%)
  Pallas kernels  4.22 us (11%)
  between operations  1.43 us (4%)
    ppermute x11, starting transfers between devices, to_chip(): lax.ppermute(part, 'seq', [(i, 2 * target(i // 2) + i % 2) for i in range...  18.6 us
    ppermute x11, waiting for transfers between devices, to_chip(): lax.ppermute(part, 'seq', [(i, 2 * target(i // 2) + i % 2) for i in range...  6.87 us
    ppermute x2, starting transfers between devices, passed_along(): return lax.ppermute(block, axis, route)  6.82 us
    pallas_call x8, Pallas kernels, run(): call(*(pltpu.with_memory_space_constraint(operand, spec.memory_space) if...  3.46 us
  transfers between devices with their start and end apart: 17, of which 6 were waited for; matrix products, arithmetic and copies ran while one was open for 0% of the time, Pallas kernels for 5%

profile of v7, /device:TPU:0, one launch (start us, length us, event | category | flops | bytes accessed | tf_op | source)
XLA Modules:
  0.0 38.9 jit_solution(2622281415799579803)
XLA Ops:
  0.0 1.3 %shard_map.65 = (bf16[32,1024]{1,0:T(8,128)(2,1)S(1)}, bf16[32,1024]{1,0:T(8,128)(2,1)S(1)}, bf16[32,1024]{1,0:T(8,128)(2,1)S(1)}, bf16[32,1024]{1,0:T(8,128)(2,...) custom-call(bf16[32,4096]{1,0:T(8,128)(2,1)} %bitcast.4, ...), custom_call_target="tpu_custom_call" | custom-call | tf_op jit(solution)/shard_map/pallas_call | solution.py:294
  1.3 5.1 %collective-permute-start = (bf16[32,1024]{1,0:T(8,128)(2,1)S(1)}, bf16[32,1024]{1,0:T(8,128)(2,1)S(1)}, u32[]{:S(2)}, u32[]{:S(2)}) collective-permute-start(bf16[32,1024]{1,0:T(8,128)(2,1)S(1)} %get-tuple-element.32), channel_id=1, source_target_pairs={{0,6},{1,7},{2,4},{3,5},{4,2},{5,3},{6,0},{7,1},{8,14},{9,15},{10,... | collective-permute-start | bytes 196616 | tf_op jit(solution)/shard_map/ppermute | solution.py:321
  6.4 0.0 collective-permute-start.1
  6.4 2.9 %collective-permute-start.2 = (bf16[32,1024]{1,0:T(8,128)(2,1)S(1)}, bf16[32,1024]{1,0:T(8,128)(2,1)S(1)}, u32[]{:S(2)}, u32[]{:S(2)}) collective-permute-start(bf16[32,1024]{1,0:T(8,128)(2,1)S(1)} %get-tuple-element.34), channel_id=1, source_target_pairs={{0,4},{1,5},{2,0},{3,1},{4,6},{5,7},{6,2},{7,3},{8,12},{9,13},{10,... | collective-permute-start | bytes 196616 | tf_op jit(solution)/shard_map/ppermute | solution.py:321
  9.3 0.0 collective-permute-start.6
  9.3 1.5 %collective-permute-start.7 = (bf16[32,1024]{1,0:T(8,128)(2,1)S(1)}, bf16[32,1024]{1,0:T(8,128)(2,1)S(1)}, u32[]{:S(2)}, u32[]{:S(2)}) collective-permute-start(bf16[32,1024]{1,0:T(8,128)(2,1)S(1)} %get-tuple-element.40), channel_id=1, source_target_pairs={{0,6},{1,7},{2,4},{3,5},{4,2},{5,3},{6,0},{7,1},{8,14},{9,15},{10,... | collective-permute-start | bytes 196616 | tf_op jit(solution)/shard_map/ppermute | solution.py:321
  10.8 0.0 collective-permute-done.refs_1_
  10.8 1.5 %collective-permute-start.8 = (bf16[32,1024]{1,0:T(8,128)(2,1)S(1)}, bf16[32,1024]{1,0:T(8,128)(2,1)S(1)}, u32[]{:S(2)}, u32[]{:S(2)}) collective-permute-start(bf16[32,1024]{1,0:T(8,128)(2,1)S(1)} %get-tuple-element.41), channel_id=1, source_target_pairs={{0,4},{1,5},{2,0},{3,1},{4,6},{5,7},{6,2},{7,3},{8,12},{9,13},{10,... | collective-permute-start | bytes 196616 | tf_op jit(solution)/shard_map/ppermute | solution.py:321
  12.2 0.3 collective-permute-done.1.refs_2_
  12.5 0.3 collective-permute-start.5
  12.9 0.0 collective-permute-done.2.refs_3_
  12.9 3.4 %collective-permute-start.3 = (bf16[128,1024]{1,0:T(8,128)(2,1)S(1)}, bf16[128,1024]{1,0:T(8,128)(2,1)S(1)}, u32[]{:S(2)}, u32[]{:S(2)}) collective-permute-start(bf16[128,1024]{1,0:T(8,128)(2,1)S(1)} %shard_map.66.refs_1_), channel_id=1, source_target_pairs={{0,8},{8,16},{16,24},{1,9},{9,17},{17,25},{2,10},{10,18},{18,26},{... | collective-permute-start | bytes 786440 | tf_op jit(solution)/shard_map/ppermute | solution.py:22
  16.3 0.2 collective-permute-done.6.refs_1_
  16.5 0.0 collective-permute-done.7.refs_2_
  16.5 0.6 %collective-permute-done.8.refs_3_ = bf16[32,1024]{1,0:T(8,128)(2,1)S(1)} collective-permute-done((bf16[32,1024]{1,0:T(8,128)(2,1)S(1)}, bf16[32,1024]{1,0:T(8,128)(2,1)S(1)}, u32[]{:S(2)}, u32[]{:S(2)}) %collective-permute-start.8) | collective-permute-done | bytes 65568 | tf_op jit(solution)/shard_map/ppermute | solution.py:321
  17.1 3.4 %collective-permute-start.12 = (bf16[128,1024]{1,0:T(8,128)(2,1)S(1)}, bf16[128,1024]{1,0:T(8,128)(2,1)S(1)}, u32[]{:S(2)}, u32[]{:S(2)}) collective-permute-start(bf16[128,1024]{1,0:T(8,128)(2,1)S(1)} %shard_map.67.refs_3_), channel_id=1, source_target_pairs={{0,8},{8,16},{16,24},{1,9},{9,17},{17,25},{2,10},{10,18},{18,26},{... | collective-permute-start | bytes 786440 | tf_op jit(solution)/shard_map/ppermute | solution.py:22
  20.5 0.0 collective-permute-done.5.refs_1_.near_ref
  20.5 2.5 %collective-permute-start.9 = (bf16[64,1024]{1,0:T(8,128)(2,1)S(1)}, bf16[64,1024]{1,0:T(8,128)(2,1)S(1)}, u32[]{:S(2)}, u32[]{:S(2)}) collective-permute-start(bf16[64,1024]{1,0:T(8,128)(2,1)S(1)} %shard_map.68), channel_id=1, source_target_pairs={{0,4},{1,5},{2,6},{3,7},{4,0},{5,1},{6,2},{7,3},{8,12},{9,13},{10,... | collective-permute-start | bytes 393224 | tf_op jit(solution)/shard_map/ppermute | solution.py:321
  24.3 0.7 %shard_map.64 = (s32[1,256]{1,0:T(1,128)S(1)}, f32[1,1024]{1,0:T(1,128)S(1)}) custom-call(s32[1]{0:T(128)S(6)} %copy.7.cache_ref, s32[1]{0:T(128)S(6)} %copy.8.time_ref, f32[50,4096]{1,0:T(8,128)} %gate_ref.1), custom_call_target="tpu_custom_call" | custom-call | tf_op jit(solution)/shard_map/pallas_call | solution.py:294
  25.1 0.1 collective-permute-start.11
  25.1 0.0 collective-permute-done.3.refs_5_
  25.1 0.5 %collective-permute-start.4 = (bf16[128,1024]{1,0:T(8,128)(2,1)S(1)}, bf16[128,1024]{1,0:T(8,128)(2,1)S(1)}, u32[]{:S(2)}, u32[]{:S(2)}) collective-permute-start(bf16[128,1024]{1,0:T(8,128)(2,1)S(1)} %collective-permute-done.3.refs_5_), channel_id=1, source_target_pairs={{0,1},{1,0},{2,3},{3,2},{4,5},{5,4},{6,7},{7,6},{8,9},{9,8},{10,11... | collective-permute-start | bytes 786440 | tf_op jit(solution)/shard_map/ppermute | solution.py:324
  25.6 0.1 collective-permute-start.10
  25.7 2.3 %collective-permute-done.9.far_ref = bf16[64,1024]{1,0:T(8,128)(2,1)S(1)} collective-permute-done((bf16[64,1024]{1,0:T(8,128)(2,1)S(1)}, bf16[64,1024]{1,0:T(8,128)(2,1)S(1)}, u32[]{:S(2)}, u32[]{:S(2)}) %collective-permute-start.9) | collective-permute-done | bytes 131104 | tf_op jit(solution)/shard_map/ppermute | solution.py:321
  28.0 0.0 collective-permute-done.12.refs_7_
  28.0 0.0 collective-permute-start.13
  28.0 0.0 collective-permute-done.4.refs_6_
  28.1 0.0 collective-permute-done.10.refs_2_
  28.1 0.0 collective-permute-done.11.refs_4_
  28.1 1.1 %shard_map.70 = (bf16[8,128,128]{2,1,0:T(8,128)(2,1)S(1)}, f32[8,128,1]{2,1,0:T(8,128)S(1)}, f32[128,1024]{1,0:T(8,128)S(1)}) custom-call(s32[1,256]{1,0:T(1,128)S(1)} %get-tuple-element.29.from_ref, bf16[128,1024]{1,0:T(8,128)(2,1)S(1)} %shard_map.69.refs_0_, bf16[128,1024]{1,0:T(8,128)(2,1)S(1)} %shard_map.66.refs_1_, ...), custom_call_target="tpu_custom_call" | custom-call | tf_op jit(solution)/shard_map/pallas_call | solution.py:294
  29.2 0.3 collective-permute-done.13.refs_0_
  29.6 0.3 shard_map.71
  29.8 0.1 collective-permute-start.14
  29.9 2.7 %collective-permute-start.15 = (bf16[32,1024]{1,0:T(8,128)(2,1)S(1)}, bf16[32,1024]{1,0:T(8,128)(2,1)S(1)}, u32[]{:S(2)}, u32[]{:S(2)}) collective-permute-start(bf16[32,1024]{1,0:T(8,128)(2,1)S(1)} %get-tuple-element.51), channel_id=1, source_target_pairs={{0,6},{1,7},{2,4},{3,5},{4,2},{5,3},{6,0},{7,1},{8,14},{9,15},{10,... | collective-permute-start | bytes 196616 | tf_op jit(solution)/shard_map/ppermute | solution.py:321
  32.6 1.9 %collective-permute-start.16 = (bf16[32,1024]{1,0:T(8,128)(2,1)S(1)}, bf16[32,1024]{1,0:T(8,128)(2,1)S(1)}, u32[]{:S(2)}, u32[]{:S(2)}) collective-permute-start(bf16[32,1024]{1,0:T(8,128)(2,1)S(1)} %get-tuple-element.52), channel_id=1, source_target_pairs={{0,4},{1,5},{2,0},{3,1},{4,6},{5,7},{6,2},{7,3},{8,12},{9,13},{10,... | collective-permute-start | bytes 196616 | tf_op jit(solution)/shard_map/ppermute | solution.py:321
  34.6 3.5 %collective-permute-done.14.refs_1_ = bf16[32,1024]{1,0:T(8,128)(2,1)S(1)} collective-permute-done((bf16[32,1024]{1,0:T(8,128)(2,1)S(1)}, bf16[32,1024]{1,0:T(8,128)(2,1)S(1)}, u32[]{:S(2)}, u32[]{:S(2)}) %collective-permute-start.14) | collective-permute-done | bytes 65568 | tf_op jit(solution)/shard_map/ppermute | solution.py:321
  38.1 0.0 collective-permute-done.15.refs_2_
  38.1 0.0 collective-permute-done.16.refs_3_
  38.1 0.8 %shard_map.72 = bf16[32,4096]{1,0:T(8,128)(2,1)} custom-call(bf16[32,1024]{1,0:T(8,128)(2,1)S(1)} %get-tuple-element.49.refs_0_, bf16[32,1024]{1,0:T(8,128)(2,1)S(1)} %collective-permute-done.14.refs_1_, bf16[32,1024]{1,0:T(8,128)(2,1)S(1)} %collective-permute-done.15.refs_2_, bf16[32,1024]{1,0:T(8,128)(2,1)S(1)} %collective-permute-done.16.refs_3_), custom_call_target="tpu_custom_call" | custom-call | tf_op jit(solution)/shard_map/pallas_call | solution.py:401
  (4 shorter events, 0.1 us)
Async XLA Ops:
  1.3 9.5 %collective-permute-start = (bf16[32,1024]{1,0:T(8,128)(2,1)S(1)}, bf16[32,1024]{1,0:T(8,128)(2,1)S(1)}, u32[]{:S(2)}, u32[]{:S(2)}) collective-permute-start(bf16[32,1024]{1,0:T(8,128)(2,1)S(1)} %get-tuple-element.32), channel_id=1, source_target_pairs={{0,6},{1,7},{2,4},{3,5},{4,2},{5,3},{6,0},{7,1},{8,14},{9,15},{10,... | collective-permute-start | bytes 196616 | tf_op jit(solution)/shard_map/ppermute | solution.py:321
  6.4 6.1 %collective-permute-start.1 = (bf16[32,1024]{1,0:T(8,128)(2,1)S(1)}, bf16[32,1024]{1,0:T(8,128)(2,1)S(1)}, u32[]{:S(2)}, u32[]{:S(2)}) collective-permute-start(bf16[32,1024]{1,0:T(8,128)(2,1)S(1)} %get-tuple-element.33), channel_id=1, source_target_pairs={{0,2},{1,3},{2,6},{3,7},{4,0},{5,1},{6,4},{7,5},{8,10},{9,11},{10,... | collective-permute-start | bytes 196616 | tf_op jit(solution)/shard_map/ppermute | solution.py:321
  6.4 6.5 %collective-permute-start.2 = (bf16[32,1024]{1,0:T(8,128)(2,1)S(1)}, bf16[32,1024]{1,0:T(8,128)(2,1)S(1)}, u32[]{:S(2)}, u32[]{:S(2)}) collective-permute-start(bf16[32,1024]{1,0:T(8,128)(2,1)S(1)} %get-tuple-element.34), channel_id=1, source_target_pairs={{0,4},{1,5},{2,0},{3,1},{4,6},{5,7},{6,2},{7,3},{8,12},{9,13},{10,... | collective-permute-start | bytes 196616 | tf_op jit(solution)/shard_map/ppermute | solution.py:321
  9.3 7.2 %collective-permute-start.6 = (bf16[32,1024]{1,0:T(8,128)(2,1)S(1)}, bf16[32,1024]{1,0:T(8,128)(2,1)S(1)}, u32[]{:S(2)}, u32[]{:S(2)}) collective-permute-start(bf16[32,1024]{1,0:T(8,128)(2,1)S(1)} %get-tuple-element.39), channel_id=1, source_target_pairs={{0,2},{1,3},{2,6},{3,7},{4,0},{5,1},{6,4},{7,5},{8,10},{9,11},{10,... | collective-permute-start | bytes 196616 | tf_op jit(solution)/shard_map/ppermute | solution.py:321
  9.3 7.2 %collective-permute-start.7 = (bf16[32,1024]{1,0:T(8,128)(2,1)S(1)}, bf16[32,1024]{1,0:T(8,128)(2,1)S(1)}, u32[]{:S(2)}, u32[]{:S(2)}) collective-permute-start(bf16[32,1024]{1,0:T(8,128)(2,1)S(1)} %get-tuple-element.40), channel_id=1, source_target_pairs={{0,6},{1,7},{2,4},{3,5},{4,2},{5,3},{6,0},{7,1},{8,14},{9,15},{10,... | collective-permute-start | bytes 196616 | tf_op jit(solution)/shard_map/ppermute | solution.py:321
  10.8 6.3 %collective-permute-start.8 = (bf16[32,1024]{1,0:T(8,128)(2,1)S(1)}, bf16[32,1024]{1,0:T(8,128)(2,1)S(1)}, u32[]{:S(2)}, u32[]{:S(2)}) collective-permute-start(bf16[32,1024]{1,0:T(8,128)(2,1)S(1)} %get-tuple-element.41), channel_id=1, source_target_pairs={{0,4},{1,5},{2,0},{3,1},{4,6},{5,7},{6,2},{7,3},{8,12},{9,13},{10,... | collective-permute-start | bytes 196616 | tf_op jit(solution)/shard_map/ppermute | solution.py:321
  12.5 8.0 %collective-permute-start.5 = (bf16[64,1024]{1,0:T(8,128)(2,1)S(1)}, bf16[64,1024]{1,0:T(8,128)(2,1)S(1)}, u32[]{:S(2)}, u32[]{:S(2)}) collective-permute-start(bf16[64,1024]{1,0:T(8,128)(2,1)S(1)} %get-tuple-element.36), channel_id=1, source_target_pairs={{0,2},{1,3},{2,0},{3,1},{4,6},{5,7},{6,4},{7,5},{8,10},{9,11},{10,... | collective-permute-start | bytes 393224 | tf_op jit(solution)/shard_map/ppermute | solution.py:321
  12.9 12.2 %collective-permute-start.3 = (bf16[128,1024]{1,0:T(8,128)(2,1)S(1)}, bf16[128,1024]{1,0:T(8,128)(2,1)S(1)}, u32[]{:S(2)}, u32[]{:S(2)}) collective-permute-start(bf16[128,1024]{1,0:T(8,128)(2,1)S(1)} %shard_map.66.refs_1_), channel_id=1, source_target_pairs={{0,8},{8,16},{16,24},{1,9},{9,17},{17,25},{2,10},{10,18},{18,26},{... | collective-permute-start | bytes 786440 | tf_op jit(solution)/shard_map/ppermute | solution.py:22
  17.1 11.0 %collective-permute-start.12 = (bf16[128,1024]{1,0:T(8,128)(2,1)S(1)}, bf16[128,1024]{1,0:T(8,128)(2,1)S(1)}, u32[]{:S(2)}, u32[]{:S(2)}) collective-permute-start(bf16[128,1024]{1,0:T(8,128)(2,1)S(1)} %shard_map.67.refs_3_), channel_id=1, source_target_pairs={{0,8},{8,16},{16,24},{1,9},{9,17},{17,25},{2,10},{10,18},{18,26},{... | collective-permute-start | bytes 786440 | tf_op jit(solution)/shard_map/ppermute | solution.py:22
  20.5 7.5 %collective-permute-start.9 = (bf16[64,1024]{1,0:T(8,128)(2,1)S(1)}, bf16[64,1024]{1,0:T(8,128)(2,1)S(1)}, u32[]{:S(2)}, u32[]{:S(2)}) collective-permute-start(bf16[64,1024]{1,0:T(8,128)(2,1)S(1)} %shard_map.68), channel_id=1, source_target_pairs={{0,4},{1,5},{2,6},{3,7},{4,0},{5,1},{6,2},{7,3},{8,12},{9,13},{10,... | collective-permute-start | bytes 393224 | tf_op jit(solution)/shard_map/ppermute | solution.py:321
  25.1 3.0 %collective-permute-start.11 = (bf16[128,1024]{1,0:T(8,128)(2,1)S(1)}, bf16[128,1024]{1,0:T(8,128)(2,1)S(1)}, u32[]{:S(2)}, u32[]{:S(2)}) collective-permute-start(bf16[128,1024]{1,0:T(8,128)(2,1)S(1)} %shard_map.67.refs_3_), channel_id=1, source_target_pairs={{0,1},{1,0},{2,3},{3,2},{4,5},{5,4},{6,7},{7,6},{8,9},{9,8},{10,11... | collective-permute-start | bytes 786440 | tf_op jit(solution)/shard_map/ppermute | solution.py:324
  25.1 2.9 %collective-permute-start.4 = (bf16[128,1024]{1,0:T(8,128)(2,1)S(1)}, bf16[128,1024]{1,0:T(8,128)(2,1)S(1)}, u32[]{:S(2)}, u32[]{:S(2)}) collective-permute-start(bf16[128,1024]{1,0:T(8,128)(2,1)S(1)} %collective-permute-done.3.refs_5_), channel_id=1, source_target_pairs={{0,1},{1,0},{2,3},{3,2},{4,5},{5,4},{6,7},{7,6},{8,9},{9,8},{10,11... | collective-permute-start | bytes 786440 | tf_op jit(solution)/shard_map/ppermute | solution.py:324
  25.6 2.4 %collective-permute-start.10 = (bf16[128,1024]{1,0:T(8,128)(2,1)S(1)}, bf16[128,1024]{1,0:T(8,128)(2,1)S(1)}, u32[]{:S(2)}, u32[]{:S(2)}) collective-permute-start(bf16[128,1024]{1,0:T(8,128)(2,1)S(1)} %shard_map.66.refs_1_), channel_id=1, source_target_pairs={{0,1},{1,0},{2,3},{3,2},{4,5},{5,4},{6,7},{7,6},{8,9},{9,8},{10,11... | collective-permute-start | bytes 786440 | tf_op jit(solution)/shard_map/ppermute | solution.py:324
  28.0 1.5 %collective-permute-start.13 = (bf16[128,1024]{1,0:T(8,128)(2,1)S(1)}, bf16[128,1024]{1,0:T(8,128)(2,1)S(1)}, u32[]{:S(2)}, u32[]{:S(2)}) collective-permute-start(bf16[128,1024]{1,0:T(8,128)(2,1)S(1)} %collective-permute-done.12.refs_7_), channel_id=1, source_target_pairs={{0,1},{1,0},{2,3},{3,2},{4,5},{5,4},{6,7},{7,6},{8,9},{9,8},{10,11... | collective-permute-start | bytes 786440 | tf_op jit(solution)/shard_map/ppermute | solution.py:324
  29.8 8.3 %collective-permute-start.14 = (bf16[32,1024]{1,0:T(8,128)(2,1)S(1)}, bf16[32,1024]{1,0:T(8,128)(2,1)S(1)}, u32[]{:S(2)}, u32[]{:S(2)}) collective-permute-start(bf16[32,1024]{1,0:T(8,128)(2,1)S(1)} %get-tuple-element.50), channel_id=1, source_target_pairs={{0,2},{1,3},{2,6},{3,7},{4,0},{5,1},{6,4},{7,5},{8,10},{9,11},{10,... | collective-permute-start | bytes 196616 | tf_op jit(solution)/shard_map/ppermute | solution.py:321
  29.9 8.2 %collective-permute-start.15 = (bf16[32,1024]{1,0:T(8,128)(2,1)S(1)}, bf16[32,1024]{1,0:T(8,128)(2,1)S(1)}, u32[]{:S(2)}, u32[]{:S(2)}) collective-permute-start(bf16[32,1024]{1,0:T(8,128)(2,1)S(1)} %get-tuple-element.51), channel_id=1, source_target_pairs={{0,6},{1,7},{2,4},{3,5},{4,2},{5,3},{6,0},{7,1},{8,14},{9,15},{10,... | collective-permute-start | bytes 196616 | tf_op jit(solution)/shard_map/ppermute | solution.py:321
  32.6 5.5 %collective-permute-start.16 = (bf16[32,1024]{1,0:T(8,128)(2,1)S(1)}, bf16[32,1024]{1,0:T(8,128)(2,1)S(1)}, u32[]{:S(2)}, u32[]{:S(2)}) collective-permute-start(bf16[32,1024]{1,0:T(8,128)(2,1)S(1)} %get-tuple-element.52), channel_id=1, source_target_pairs={{0,4},{1,5},{2,0},{3,1},{4,6},{5,7},{6,2},{7,3},{8,12},{9,13},{10,... | collective-permute-start | bytes 196616 | tf_op jit(solution)/shard_map/ppermute | solution.py:321

commit v8 on v6

--- a/solution.py
+++ b/solution.py
@@ -125,7 +125,7 @@
 
 
 ROUTES = ((following, preceding), (facing, facing), (preceding, following))
-OUT_ORDER = (0, 1, 2)
+OUT_ORDER = (2, 0, 1)
 KEY_ORDER = (1, 0, 2)
 VALUE_ORDER = (0, 1, 2)
 
@@ -376,7 +376,7 @@
         keys,
         with_core(after(keys, seen_from, gate_row)),
         values,
-        with_core(values),
+        with_core(after(values, seen_from, gate_row)),
         past_keys,
         past_keys_too,
         past_values,

time: 39.1 us -> 39.2 us (level)
  no operation moved by 1% of the time
where the time goes in v8:
time: 39.2 us; the launch traced here: 38.9 us
  starting transfers between devices  26.1 us (67%)
  waiting for transfers between devices  7.21 us (18%)
  Pallas kernels  4.19 us (11%)
  between operations  1.42 us (4%)
    ppermute x11, starting transfers between devices, to_chip(): lax.ppermute(part, 'seq', [(i, 2 * target(i // 2) + i % 2) for i in range...  18.6 us
    ppermute x11, waiting for transfers between devices, to_chip(): lax.ppermute(part, 'seq', [(i, 2 * target(i // 2) + i % 2) for i in range...  6.87 us
    ppermute x2, starting transfers between devices, passed_along(): return lax.ppermute(block, axis, route)  6.82 us
    pallas_call x8, Pallas kernels, run(): call(*(pltpu.with_memory_space_constraint(operand, spec.memory_space) if...  3.46 us
  transfers between devices with their start and end apart: 17, of which 6 were waited for; matrix products, arithmetic and copies ran while one was open for 0% of the time, Pallas kernels for 5%

profile of v8, /device:TPU:0, one launch (start us, length us, event | category | flops | bytes accessed | tf_op | source)
XLA Modules:
  0.0 38.9 jit_solution(9298882138837039284)
XLA Ops:
  0.0 1.3 %shard_map.65 = (bf16[32,1024]{1,0:T(8,128)(2,1)S(1)}, bf16[32,1024]{1,0:T(8,128)(2,1)S(1)}, bf16[32,1024]{1,0:T(8,128)(2,1)S(1)}, bf16[32,1024]{1,0:T(8,128)(2,...) custom-call(bf16[32,4096]{1,0:T(8,128)(2,1)} %bitcast.4, ...), custom_call_target="tpu_custom_call" | custom-call | tf_op jit(solution)/shard_map/pallas_call | solution.py:289
  1.3 5.1 %collective-permute-start = (bf16[32,1024]{1,0:T(8,128)(2,1)S(1)}, bf16[32,1024]{1,0:T(8,128)(2,1)S(1)}, u32[]{:S(2)}, u32[]{:S(2)}) collective-permute-start(bf16[32,1024]{1,0:T(8,128)(2,1)S(1)} %get-tuple-element.33), channel_id=1, source_target_pairs={{0,6},{1,7},{2,4},{3,5},{4,2},{5,3},{6,0},{7,1},{8,14},{9,15},{10,... | collective-permute-start | bytes 196616 | tf_op jit(solution)/shard_map/ppermute | solution.py:316
  6.4 0.0 collective-permute-start.1
  6.4 2.9 %collective-permute-start.2 = (bf16[32,1024]{1,0:T(8,128)(2,1)S(1)}, bf16[32,1024]{1,0:T(8,128)(2,1)S(1)}, u32[]{:S(2)}, u32[]{:S(2)}) collective-permute-start(bf16[32,1024]{1,0:T(8,128)(2,1)S(1)} %get-tuple-element.35), channel_id=1, source_target_pairs={{0,4},{1,5},{2,0},{3,1},{4,6},{5,7},{6,2},{7,3},{8,12},{9,13},{10,... | collective-permute-start | bytes 196616 | tf_op jit(solution)/shard_map/ppermute | solution.py:316
  9.3 0.0 collective-permute-start.6
  9.3 1.5 %collective-permute-start.7 = (bf16[32,1024]{1,0:T(8,128)(2,1)S(1)}, bf16[32,1024]{1,0:T(8,128)(2,1)S(1)}, u32[]{:S(2)}, u32[]{:S(2)}) collective-permute-start(bf16[32,1024]{1,0:T(8,128)(2,1)S(1)} %get-tuple-element.41), channel_id=1, source_target_pairs={{0,6},{1,7},{2,4},{3,5},{4,2},{5,3},{6,0},{7,1},{8,14},{9,15},{10,... | collective-permute-start | bytes 196616 | tf_op jit(solution)/shard_map/ppermute | solution.py:316
  10.8 0.0 collective-permute-done.refs_1_
  10.8 1.5 %collective-permute-start.8 = (bf16[32,1024]{1,0:T(8,128)(2,1)S(1)}, bf16[32,1024]{1,0:T(8,128)(2,1)S(1)}, u32[]{:S(2)}, u32[]{:S(2)}) collective-permute-start(bf16[32,1024]{1,0:T(8,128)(2,1)S(1)} %get-tuple-element.42), channel_id=1, source_target_pairs={{0,4},{1,5},{2,0},{3,1},{4,6},{5,7},{6,2},{7,3},{8,12},{9,13},{10,... | collective-permute-start | bytes 196616 | tf_op jit(solution)/shard_map/ppermute | solution.py:316
  12.2 0.3 collective-permute-done.1.refs_2_
  12.5 0.3 collective-permute-start.5
  12.9 0.0 collective-permute-done.2.refs_3_
  12.9 3.4 %collective-permute-start.3 = (bf16[128,1024]{1,0:T(8,128)(2,1)S(1)}, bf16[128,1024]{1,0:T(8,128)(2,1)S(1)}, u32[]{:S(2)}, u32[]{:S(2)}) collective-permute-start(bf16[128,1024]{1,0:T(8,128)(2,1)S(1)} %shard_map.66.refs_1_), channel_id=1, source_target_pairs={{0,8},{8,16},{16,24},{1,9},{9,17},{17,25},{2,10},{10,18},{18,26},{... | collective-permute-start | bytes 786440 | tf_op jit(solution)/shard_map/ppermute | solution.py:22
  16.3 0.2 collective-permute-done.6.refs_1_
  16.5 0.0 collective-permute-done.7.refs_2_
  16.5 0.6 %collective-permute-done.8.refs_3_ = bf16[32,1024]{1,0:T(8,128)(2,1)S(1)} collective-permute-done((bf16[32,1024]{1,0:T(8,128)(2,1)S(1)}, bf16[32,1024]{1,0:T(8,128)(2,1)S(1)}, u32[]{:S(2)}, u32[]{:S(2)}) %collective-permute-start.8) | collective-permute-done | bytes 65568 | tf_op jit(solution)/shard_map/ppermute | solution.py:316
  17.1 3.4 %collective-permute-start.12 = (bf16[128,1024]{1,0:T(8,128)(2,1)S(1)}, bf16[128,1024]{1,0:T(8,128)(2,1)S(1)}, u32[]{:S(2)}, u32[]{:S(2)}) collective-permute-start(bf16[128,1024]{1,0:T(8,128)(2,1)S(1)} %shard_map.67.refs_3_), channel_id=1, source_target_pairs={{0,8},{8,16},{16,24},{1,9},{9,17},{17,25},{2,10},{10,18},{18,26},{... | collective-permute-start | bytes 786440 | tf_op jit(solution)/shard_map/ppermute | solution.py:22
  20.5 0.0 collective-permute-done.5.refs_1_.near_ref
  20.5 2.5 %collective-permute-start.9 = (bf16[64,1024]{1,0:T(8,128)(2,1)S(1)}, bf16[64,1024]{1,0:T(8,128)(2,1)S(1)}, u32[]{:S(2)}, u32[]{:S(2)}) collective-permute-start(bf16[64,1024]{1,0:T(8,128)(2,1)S(1)} %shard_map.68), channel_id=1, source_target_pairs={{0,4},{1,5},{2,6},{3,7},{4,0},{5,1},{6,2},{7,3},{8,12},{9,13},{10,... | collective-permute-start | bytes 393224 | tf_op jit(solution)/shard_map/ppermute | solution.py:316
  24.3 0.7 %shard_map.64 = (s32[1,256]{1,0:T(1,128)S(1)}, f32[1,1024]{1,0:T(1,128)S(1)}) custom-call(s32[1]{0:T(128)S(6)} %copy.7.cache_ref, s32[1]{0:T(128)S(6)} %copy.8.time_ref, f32[50,4096]{1,0:T(8,128)} %gate_ref.1), custom_call_target="tpu_custom_call" | custom-call | tf_op jit(solution)/shard_map/pallas_call | solution.py:289
  25.1 0.1 collective-permute-start.10
  25.1 0.0 collective-permute-done.3.refs_5_
  25.1 0.5 %collective-permute-start.4 = (bf16[128,1024]{1,0:T(8,128)(2,1)S(1)}, bf16[128,1024]{1,0:T(8,128)(2,1)S(1)}, u32[]{:S(2)}, u32[]{:S(2)}) collective-permute-start(bf16[128,1024]{1,0:T(8,128)(2,1)S(1)} %collective-permute-done.3.refs_5_), channel_id=1, source_target_pairs={{0,1},{1,0},{2,3},{3,2},{4,5},{5,4},{6,7},{7,6},{8,9},{9,8},{10,11... | collective-permute-start | bytes 786440 | tf_op jit(solution)/shard_map/ppermute | solution.py:319
  25.6 0.1 collective-permute-start.11
  25.7 2.3 %collective-permute-done.9.far_ref = bf16[64,1024]{1,0:T(8,128)(2,1)S(1)} collective-permute-done((bf16[64,1024]{1,0:T(8,128)(2,1)S(1)}, bf16[64,1024]{1,0:T(8,128)(2,1)S(1)}, u32[]{:S(2)}, u32[]{:S(2)}) %collective-permute-start.9) | collective-permute-done | bytes 131104 | tf_op jit(solution)/shard_map/ppermute | solution.py:316
  28.0 0.0 collective-permute-done.12.refs_7_
  28.0 0.0 collective-permute-start.13
  28.0 0.0 collective-permute-done.4.refs_6_
  28.1 0.0 collective-permute-done.10.refs_2_
  28.1 0.0 collective-permute-done.11.refs_4_
  28.1 1.1 %shard_map.70 = (bf16[8,128,128]{2,1,0:T(8,128)(2,1)S(1)}, f32[8,128,1]{2,1,0:T(8,128)S(1)}, f32[128,1024]{1,0:T(8,128)S(1)}) custom-call(s32[1,256]{1,0:T(1,128)S(1)} %get-tuple-element.30.from_ref, bf16[128,1024]{1,0:T(8,128)(2,1)S(1)} %shard_map.69.refs_0_, bf16[128,1024]{1,0:T(8,128)(2,1)S(1)} %shard_map.66.refs_1_, ...), custom_call_target="tpu_custom_call" | custom-call | tf_op jit(solution)/shard_map/pallas_call | solution.py:289
  29.2 0.3 collective-permute-done.13.refs_0_
  29.6 0.3 shard_map.71
  29.8 1.0 %collective-permute-start.14 = (bf16[32,1024]{1,0:T(8,128)(2,1)S(1)}, bf16[32,1024]{1,0:T(8,128)(2,1)S(1)}, u32[]{:S(2)}, u32[]{:S(2)}) collective-permute-start(bf16[32,1024]{1,0:T(8,128)(2,1)S(1)} %get-tuple-element.52), channel_id=1, source_target_pairs={{0,4},{1,5},{2,0},{3,1},{4,6},{5,7},{6,2},{7,3},{8,12},{9,13},{10,... | collective-permute-start | bytes 196616 | tf_op jit(solution)/shard_map/ppermute | solution.py:316
  30.9 1.0 %collective-permute-start.15 = (bf16[32,1024]{1,0:T(8,128)(2,1)S(1)}, bf16[32,1024]{1,0:T(8,128)(2,1)S(1)}, u32[]{:S(2)}, u32[]{:S(2)}) collective-permute-start(bf16[32,1024]{1,0:T(8,128)(2,1)S(1)} %get-tuple-element.53), channel_id=1, source_target_pairs={{0,2},{1,3},{2,6},{3,7},{4,0},{5,1},{6,4},{7,5},{8,10},{9,11},{10,... | collective-permute-start | bytes 196616 | tf_op jit(solution)/shard_map/ppermute | solution.py:316
  31.9 2.7 %collective-permute-start.16 = (bf16[32,1024]{1,0:T(8,128)(2,1)S(1)}, bf16[32,1024]{1,0:T(8,128)(2,1)S(1)}, u32[]{:S(2)}, u32[]{:S(2)}) collective-permute-start(bf16[32,1024]{1,0:T(8,128)(2,1)S(1)} %get-tuple-element.54), channel_id=1, source_target_pairs={{0,6},{1,7},{2,4},{3,5},{4,2},{5,3},{6,0},{7,1},{8,14},{9,15},{10,... | collective-permute-start | bytes 196616 | tf_op jit(solution)/shard_map/ppermute | solution.py:316
  34.6 0.0 collective-permute-done.14.refs_1_
  34.6 3.5 %collective-permute-done.15.refs_2_ = bf16[32,1024]{1,0:T(8,128)(2,1)S(1)} collective-permute-done((bf16[32,1024]{1,0:T(8,128)(2,1)S(1)}, bf16[32,1024]{1,0:T(8,128)(2,1)S(1)}, u32[]{:S(2)}, u32[]{:S(2)}) %collective-permute-start.15) | collective-permute-done | bytes 65568 | tf_op jit(solution)/shard_map/ppermute | solution.py:316
  38.1 0.0 collective-permute-done.16.refs_3_
  38.1 0.7 %shard_map.72 = bf16[32,4096]{1,0:T(8,128)(2,1)} custom-call(bf16[32,1024]{1,0:T(8,128)(2,1)S(1)} %get-tuple-element.51.refs_0_, bf16[32,1024]{1,0:T(8,128)(2,1)S(1)} %collective-permute-done.14.refs_1_, bf16[32,1024]{1,0:T(8,128)(2,1)S(1)} %collective-permute-done.15.refs_2_, bf16[32,1024]{1,0:T(8,128)(2,1)S(1)} %collective-permute-done.16.refs_3_), custom_call_target="tpu_custom_call" | custom-call | tf_op jit(solution)/shard_map/pallas_call | solution.py:396
  (4 shorter events, 0.1 us)
Async XLA Ops:
  1.3 9.5 %collective-permute-start = (bf16[32,1024]{1,0:T(8,128)(2,1)S(1)}, bf16[32,1024]{1,0:T(8,128)(2,1)S(1)}, u32[]{:S(2)}, u32[]{:S(2)}) collective-permute-start(bf16[32,1024]{1,0:T(8,128)(2,1)S(1)} %get-tuple-element.33), channel_id=1, source_target_pairs={{0,6},{1,7},{2,4},{3,5},{4,2},{5,3},{6,0},{7,1},{8,14},{9,15},{10,... | collective-permute-start | bytes 196616 | tf_op jit(solution)/shard_map/ppermute | solution.py:316
  6.4 6.1 %collective-permute-start.1 = (bf16[32,1024]{1,0:T(8,128)(2,1)S(1)}, bf16[32,1024]{1,0:T(8,128)(2,1)S(1)}, u32[]{:S(2)}, u32[]{:S(2)}) collective-permute-start(bf16[32,1024]{1,0:T(8,128)(2,1)S(1)} %get-tuple-element.34), channel_id=1, source_target_pairs={{0,2},{1,3},{2,6},{3,7},{4,0},{5,1},{6,4},{7,5},{8,10},{9,11},{10,... | collective-permute-start | bytes 196616 | tf_op jit(solution)/shard_map/ppermute | solution.py:316
  6.4 6.5 %collective-permute-start.2 = (bf16[32,1024]{1,0:T(8,128)(2,1)S(1)}, bf16[32,1024]{1,0:T(8,128)(2,1)S(1)}, u32[]{:S(2)}, u32[]{:S(2)}) collective-permute-start(bf16[32,1024]{1,0:T(8,128)(2,1)S(1)} %get-tuple-element.35), channel_id=1, source_target_pairs={{0,4},{1,5},{2,0},{3,1},{4,6},{5,7},{6,2},{7,3},{8,12},{9,13},{10,... | collective-permute-start | bytes 196616 | tf_op jit(solution)/shard_map/ppermute | solution.py:316
  9.3 7.2 %collective-permute-start.6 = (bf16[32,1024]{1,0:T(8,128)(2,1)S(1)}, bf16[32,1024]{1,0:T(8,128)(2,1)S(1)}, u32[]{:S(2)}, u32[]{:S(2)}) collective-permute-start(bf16[32,1024]{1,0:T(8,128)(2,1)S(1)} %get-tuple-element.40), channel_id=1, source_target_pairs={{0,2},{1,3},{2,6},{3,7},{4,0},{5,1},{6,4},{7,5},{8,10},{9,11},{10,... | collective-permute-start | bytes 196616 | tf_op jit(solution)/shard_map/ppermute | solution.py:316
  9.3 7.2 %collective-permute-start.7 = (bf16[32,1024]{1,0:T(8,128)(2,1)S(1)}, bf16[32,1024]{1,0:T(8,128)(2,1)S(1)}, u32[]{:S(2)}, u32[]{:S(2)}) collective-permute-start(bf16[32,1024]{1,0:T(8,128)(2,1)S(1)} %get-tuple-element.41), channel_id=1, source_target_pairs={{0,6},{1,7},{2,4},{3,5},{4,2},{5,3},{6,0},{7,1},{8,14},{9,15},{10,... | collective-permute-start | bytes 196616 | tf_op jit(solution)/shard_map/ppermute | solution.py:316
  10.8 6.3 %collective-permute-start.8 = (bf16[32,1024]{1,0:T(8,128)(2,1)S(1)}, bf16[32,1024]{1,0:T(8,128)(2,1)S(1)}, u32[]{:S(2)}, u32[]{:S(2)}) collective-permute-start(bf16[32,1024]{1,0:T(8,128)(2,1)S(1)} %get-tuple-element.42), channel_id=1, source_target_pairs={{0,4},{1,5},{2,0},{3,1},{4,6},{5,7},{6,2},{7,3},{8,12},{9,13},{10,... | collective-permute-start | bytes 196616 | tf_op jit(solution)/shard_map/ppermute | solution.py:316
  12.5 8.0 %collective-permute-start.5 = (bf16[64,1024]{1,0:T(8,128)(2,1)S(1)}, bf16[64,1024]{1,0:T(8,128)(2,1)S(1)}, u32[]{:S(2)}, u32[]{:S(2)}) collective-permute-start(bf16[64,1024]{1,0:T(8,128)(2,1)S(1)} %get-tuple-element.37), channel_id=1, source_target_pairs={{0,2},{1,3},{2,0},{3,1},{4,6},{5,7},{6,4},{7,5},{8,10},{9,11},{10,... | collective-permute-start | bytes 393224 | tf_op jit(solution)/shard_map/ppermute | solution.py:316
  12.9 12.2 %collective-permute-start.3 = (bf16[128,1024]{1,0:T(8,128)(2,1)S(1)}, bf16[128,1024]{1,0:T(8,128)(2,1)S(1)}, u32[]{:S(2)}, u32[]{:S(2)}) collective-permute-start(bf16[128,1024]{1,0:T(8,128)(2,1)S(1)} %shard_map.66.refs_1_), channel_id=1, source_target_pairs={{0,8},{8,16},{16,24},{1,9},{9,17},{17,25},{2,10},{10,18},{18,26},{... | collective-permute-start | bytes 786440 | tf_op jit(solution)/shard_map/ppermute | solution.py:22
  17.1 11.0 %collective-permute-start.12 = (bf16[128,1024]{1,0:T(8,128)(2,1)S(1)}, bf16[128,1024]{1,0:T(8,128)(2,1)S(1)}, u32[]{:S(2)}, u32[]{:S(2)}) collective-permute-start(bf16[128,1024]{1,0:T(8,128)(2,1)S(1)} %shard_map.67.refs_3_), channel_id=1, source_target_pairs={{0,8},{8,16},{16,24},{1,9},{9,17},{17,25},{2,10},{10,18},{18,26},{... | collective-permute-start | bytes 786440 | tf_op jit(solution)/shard_map/ppermute | solution.py:22
  20.5 7.5 %collective-permute-start.9 = (bf16[64,1024]{1,0:T(8,128)(2,1)S(1)}, bf16[64,1024]{1,0:T(8,128)(2,1)S(1)}, u32[]{:S(2)}, u32[]{:S(2)}) collective-permute-start(bf16[64,1024]{1,0:T(8,128)(2,1)S(1)} %shard_map.68), channel_id=1, source_target_pairs={{0,4},{1,5},{2,6},{3,7},{4,0},{5,1},{6,2},{7,3},{8,12},{9,13},{10,... | collective-permute-start | bytes 393224 | tf_op jit(solution)/shard_map/ppermute | solution.py:316
  25.1 3.0 %collective-permute-start.10 = (bf16[128,1024]{1,0:T(8,128)(2,1)S(1)}, bf16[128,1024]{1,0:T(8,128)(2,1)S(1)}, u32[]{:S(2)}, u32[]{:S(2)}) collective-permute-start(bf16[128,1024]{1,0:T(8,128)(2,1)S(1)} %shard_map.66.refs_1_), channel_id=1, source_target_pairs={{0,1},{1,0},{2,3},{3,2},{4,5},{5,4},{6,7},{7,6},{8,9},{9,8},{10,11... | collective-permute-start | bytes 786440 | tf_op jit(solution)/shard_map/ppermute | solution.py:319
  25.1 2.9 %collective-permute-start.4 = (bf16[128,1024]{1,0:T(8,128)(2,1)S(1)}, bf16[128,1024]{1,0:T(8,128)(2,1)S(1)}, u32[]{:S(2)}, u32[]{:S(2)}) collective-permute-start(bf16[128,1024]{1,0:T(8,128)(2,1)S(1)} %collective-permute-done.3.refs_5_), channel_id=1, source_target_pairs={{0,1},{1,0},{2,3},{3,2},{4,5},{5,4},{6,7},{7,6},{8,9},{9,8},{10,11... | collective-permute-start | bytes 786440 | tf_op jit(solution)/shard_map/ppermute | solution.py:319
  25.6 2.5 %collective-permute-start.11 = (bf16[128,1024]{1,0:T(8,128)(2,1)S(1)}, bf16[128,1024]{1,0:T(8,128)(2,1)S(1)}, u32[]{:S(2)}, u32[]{:S(2)}) collective-permute-start(bf16[128,1024]{1,0:T(8,128)(2,1)S(1)} %shard_map.67.refs_3_), channel_id=1, source_target_pairs={{0,1},{1,0},{2,3},{3,2},{4,5},{5,4},{6,7},{7,6},{8,9},{9,8},{10,11... | collective-permute-start | bytes 786440 | tf_op jit(solution)/shard_map/ppermute | solution.py:319
  28.0 1.5 %collective-permute-start.13 = (bf16[128,1024]{1,0:T(8,128)(2,1)S(1)}, bf16[128,1024]{1,0:T(8,128)(2,1)S(1)}, u32[]{:S(2)}, u32[]{:S(2)}) collective-permute-start(bf16[128,1024]{1,0:T(8,128)(2,1)S(1)} %collective-permute-done.12.refs_7_), channel_id=1, source_target_pairs={{0,1},{1,0},{2,3},{3,2},{4,5},{5,4},{6,7},{7,6},{8,9},{9,8},{10,11... | collective-permute-start | bytes 786440 | tf_op jit(solution)/shard_map/ppermute | solution.py:319
  29.8 4.8 %collective-permute-start.14 = (bf16[32,1024]{1,0:T(8,128)(2,1)S(1)}, bf16[32,1024]{1,0:T(8,128)(2,1)S(1)}, u32[]{:S(2)}, u32[]{:S(2)}) collective-permute-start(bf16[32,1024]{1,0:T(8,128)(2,1)S(1)} %get-tuple-element.52), channel_id=1, source_target_pairs={{0,4},{1,5},{2,0},{3,1},{4,6},{5,7},{6,2},{7,3},{8,12},{9,13},{10,... | collective-permute-start | bytes 196616 | tf_op jit(solution)/shard_map/ppermute | solution.py:316
  30.9 7.3 %collective-permute-start.15 = (bf16[32,1024]{1,0:T(8,128)(2,1)S(1)}, bf16[32,1024]{1,0:T(8,128)(2,1)S(1)}, u32[]{:S(2)}, u32[]{:S(2)}) collective-permute-start(bf16[32,1024]{1,0:T(8,128)(2,1)S(1)} %get-tuple-element.53), channel_id=1, source_target_pairs={{0,2},{1,3},{2,6},{3,7},{4,0},{5,1},{6,4},{7,5},{8,10},{9,11},{10,... | collective-permute-start | bytes 196616 | tf_op jit(solution)/shard_map/ppermute | solution.py:316
  31.9 6.2 %collective-permute-start.16 = (bf16[32,1024]{1,0:T(8,128)(2,1)S(1)}, bf16[32,1024]{1,0:T(8,128)(2,1)S(1)}, u32[]{:S(2)}, u32[]{:S(2)}) collective-permute-start(bf16[32,1024]{1,0:T(8,128)(2,1)S(1)} %get-tuple-element.54), channel_id=1, source_target_pairs={{0,6},{1,7},{2,4},{3,5},{4,2},{5,3},{6,0},{7,1},{8,14},{9,15},{10,... | collective-permute-start | bytes 196616 | tf_op jit(solution)/shard_map/ppermute | solution.py:316

commit v9 on v6

--- a/solution.py
+++ b/solution.py
@@ -149,13 +149,14 @@
     copies = []
     for part, (index, chips) in zip(parts, cuts):
         for place, chip in enumerate(chips):
-            copies.append(
-                pltpu.make_async_copy(
-                    whole[index].at[:, span_of(chip(here), width)],
-                    part.at[pl.ds(place * rows, rows)],
-                    sems.at[len(copies)],
+            for piece in range(0, rows, 16):
+                copies.append(
+                    pltpu.make_async_copy(
+                        whole[index].at[pl.ds(piece, 16), span_of(chip(here), width)],
+                        part.at[pl.ds(place * rows + piece, 16)],
+                        sems.at[len(copies)],
+                    )
                 )
-            )
     run_copies(copies)
 
 
@@ -334,7 +335,7 @@
         functools.partial(pack_kernel, cuts),
         [HBM] * 3,
         tuple(block(len(chips)) for _, chips in cuts),
-        scratch=[pltpu.SemaphoreType.DMA((3 * CHIPS,))],
+        scratch=[pltpu.SemaphoreType.DMA((3 * CHIPS * rows // 16,))],
     )(key_rows[0], value_rows[0], query_rows[0])
     key_parts, value_parts, query_parts = parts[:CHIPS], parts[CHIPS:2 * CHIPS], parts[2 * CHIPS:]
 

time: 39.1 us -> 39.2 us (level)
  no operation moved by 1% of the time
where the time goes in v9:
time: 39.2 us; the launch traced here: 38.9 us
  starting transfers between devices  26 us (66%)
  waiting for transfers between devices  7.2 us (18%)
  Pallas kernels  4.23 us (11%)
  between operations  1.43 us (4%)
    ppermute x11, starting transfers between devices, to_chip(): lax.ppermute(part, 'seq', [(i, 2 * target(i // 2) + i % 2) for i in range...  18.6 us
    ppermute x11, waiting for transfers between devices, to_chip(): lax.ppermute(part, 'seq', [(i, 2 * target(i // 2) + i % 2) for i in range...  6.87 us
    ppermute x2, starting transfers between devices, passed_along(): return lax.ppermute(block, axis, route)  6.82 us
    pallas_call x8, Pallas kernels, run(): call(*(pltpu.with_memory_space_constraint(operand, spec.memory_space) if...  3.5 us
  transfers between devices with their start and end apart: 17, of which 6 were waited for; matrix products, arithmetic and copies ran while one was open for 0% of the time, Pallas kernels for 5%

profile of v9, /device:TPU:0, one launch (start us, length us, event | category | flops | bytes accessed | tf_op | source)
XLA Modules:
  0.0 38.9 jit_solution(18092845481690776930)
XLA Ops:
  0.0 1.3 %shard_map.65 = (bf16[32,1024]{1,0:T(8,128)(2,1)S(1)}, bf16[32,1024]{1,0:T(8,128)(2,1)S(1)}, bf16[32,1024]{1,0:T(8,128)(2,1)S(1)}, bf16[32,1024]{1,0:T(8,128)(2,...) custom-call(bf16[32,4096]{1,0:T(8,128)(2,1)} %bitcast.4, ...), custom_call_target="tpu_custom_call" | custom-call | tf_op jit(solution)/shard_map/pallas_call | solution.py:290
  1.3 5.1 %collective-permute-start = (bf16[32,1024]{1,0:T(8,128)(2,1)S(1)}, bf16[32,1024]{1,0:T(8,128)(2,1)S(1)}, u32[]{:S(2)}, u32[]{:S(2)}) collective-permute-start(bf16[32,1024]{1,0:T(8,128)(2,1)S(1)} %get-tuple-element.32), channel_id=1, source_target_pairs={{0,6},{1,7},{2,4},{3,5},{4,2},{5,3},{6,0},{7,1},{8,14},{9,15},{10,... | collective-permute-start | bytes 196616 | tf_op jit(solution)/shard_map/ppermute | solution.py:317
  6.4 0.0 collective-permute-start.1
  6.4 2.9 %collective-permute-start.2 = (bf16[32,1024]{1,0:T(8,128)(2,1)S(1)}, bf16[32,1024]{1,0:T(8,128)(2,1)S(1)}, u32[]{:S(2)}, u32[]{:S(2)}) collective-permute-start(bf16[32,1024]{1,0:T(8,128)(2,1)S(1)} %get-tuple-element.34), channel_id=1, source_target_pairs={{0,4},{1,5},{2,0},{3,1},{4,6},{5,7},{6,2},{7,3},{8,12},{9,13},{10,... | collective-permute-start | bytes 196616 | tf_op jit(solution)/shard_map/ppermute | solution.py:317
  9.3 0.0 collective-permute-start.6
  9.4 1.5 %collective-permute-start.7 = (bf16[32,1024]{1,0:T(8,128)(2,1)S(1)}, bf16[32,1024]{1,0:T(8,128)(2,1)S(1)}, u32[]{:S(2)}, u32[]{:S(2)}) collective-permute-start(bf16[32,1024]{1,0:T(8,128)(2,1)S(1)} %get-tuple-element.40), channel_id=1, source_target_pairs={{0,6},{1,7},{2,4},{3,5},{4,2},{5,3},{6,0},{7,1},{8,14},{9,15},{10,... | collective-permute-start | bytes 196616 | tf_op jit(solution)/shard_map/ppermute | solution.py:317
  10.8 0.0 collective-permute-done.refs_1_
  10.8 1.5 %collective-permute-start.8 = (bf16[32,1024]{1,0:T(8,128)(2,1)S(1)}, bf16[32,1024]{1,0:T(8,128)(2,1)S(1)}, u32[]{:S(2)}, u32[]{:S(2)}) collective-permute-start(bf16[32,1024]{1,0:T(8,128)(2,1)S(1)} %get-tuple-element.41), channel_id=1, source_target_pairs={{0,4},{1,5},{2,0},{3,1},{4,6},{5,7},{6,2},{7,3},{8,12},{9,13},{10,... | collective-permute-start | bytes 196616 | tf_op jit(solution)/shard_map/ppermute | solution.py:317
  12.3 0.3 collective-permute-done.1.refs_2_
  12.6 0.3 collective-permute-start.5
  12.9 0.0 collective-permute-done.2.refs_3_
  12.9 3.4 %collective-permute-start.3 = (bf16[128,1024]{1,0:T(8,128)(2,1)S(1)}, bf16[128,1024]{1,0:T(8,128)(2,1)S(1)}, u32[]{:S(2)}, u32[]{:S(2)}) collective-permute-start(bf16[128,1024]{1,0:T(8,128)(2,1)S(1)} %shard_map.66.refs_1_), channel_id=1, source_target_pairs={{0,8},{8,16},{16,24},{1,9},{9,17},{17,25},{2,10},{10,18},{18,26},{... | collective-permute-start | bytes 786440 | tf_op jit(solution)/shard_map/ppermute | solution.py:22
  16.4 0.2 collective-permute-done.6.refs_1_
  16.5 0.0 collective-permute-done.7.refs_2_
  16.5 0.6 %collective-permute-done.8.refs_3_ = bf16[32,1024]{1,0:T(8,128)(2,1)S(1)} collective-permute-done((bf16[32,1024]{1,0:T(8,128)(2,1)S(1)}, bf16[32,1024]{1,0:T(8,128)(2,1)S(1)}, u32[]{:S(2)}, u32[]{:S(2)}) %collective-permute-start.8) | collective-permute-done | bytes 65568 | tf_op jit(solution)/shard_map/ppermute | solution.py:317
  17.1 3.4 %collective-permute-start.12 = (bf16[128,1024]{1,0:T(8,128)(2,1)S(1)}, bf16[128,1024]{1,0:T(8,128)(2,1)S(1)}, u32[]{:S(2)}, u32[]{:S(2)}) collective-permute-start(bf16[128,1024]{1,0:T(8,128)(2,1)S(1)} %shard_map.67.refs_3_), channel_id=1, source_target_pairs={{0,8},{8,16},{16,24},{1,9},{9,17},{17,25},{2,10},{10,18},{18,26},{... | collective-permute-start | bytes 786440 | tf_op jit(solution)/shard_map/ppermute | solution.py:22
  20.5 0.0 collective-permute-done.5.refs_1_.near_ref
  20.6 2.5 %collective-permute-start.9 = (bf16[64,1024]{1,0:T(8,128)(2,1)S(1)}, bf16[64,1024]{1,0:T(8,128)(2,1)S(1)}, u32[]{:S(2)}, u32[]{:S(2)}) collective-permute-start(bf16[64,1024]{1,0:T(8,128)(2,1)S(1)} %shard_map.68), channel_id=1, source_target_pairs={{0,4},{1,5},{2,6},{3,7},{4,0},{5,1},{6,2},{7,3},{8,12},{9,13},{10,... | collective-permute-start | bytes 393224 | tf_op jit(solution)/shard_map/ppermute | solution.py:317
  24.4 0.7 %shard_map.64 = (s32[1,256]{1,0:T(1,128)S(1)}, f32[1,1024]{1,0:T(1,128)S(1)}) custom-call(s32[1]{0:T(128)S(6)} %copy.7.cache_ref, s32[1]{0:T(128)S(6)} %copy.8.time_ref, f32[50,4096]{1,0:T(8,128)} %gate_ref.1), custom_call_target="tpu_custom_call" | custom-call | tf_op jit(solution)/shard_map/pallas_call | solution.py:290
  25.1 0.1 collective-permute-start.11
  25.2 0.0 collective-permute-done.3.refs_5_
  25.2 0.5 %collective-permute-start.4 = (bf16[128,1024]{1,0:T(8,128)(2,1)S(1)}, bf16[128,1024]{1,0:T(8,128)(2,1)S(1)}, u32[]{:S(2)}, u32[]{:S(2)}) collective-permute-start(bf16[128,1024]{1,0:T(8,128)(2,1)S(1)} %collective-permute-done.3.refs_5_), channel_id=1, source_target_pairs={{0,1},{1,0},{2,3},{3,2},{4,5},{5,4},{6,7},{7,6},{8,9},{9,8},{10,11... | collective-permute-start | bytes 786440 | tf_op jit(solution)/shard_map/ppermute | solution.py:320
  25.7 0.1 collective-permute-start.10
  25.8 2.3 %collective-permute-done.9.far_ref = bf16[64,1024]{1,0:T(8,128)(2,1)S(1)} collective-permute-done((bf16[64,1024]{1,0:T(8,128)(2,1)S(1)}, bf16[64,1024]{1,0:T(8,128)(2,1)S(1)}, u32[]{:S(2)}, u32[]{:S(2)}) %collective-permute-start.9) | collective-permute-done | bytes 131104 | tf_op jit(solution)/shard_map/ppermute | solution.py:317
  28.1 0.0 collective-permute-done.12.refs_7_
  28.1 0.0 collective-permute-start.13
  28.1 0.0 collective-permute-done.4.refs_6_
  28.1 0.0 collective-permute-done.10.refs_2_
  28.1 0.0 collective-permute-done.11.refs_4_
  28.1 1.1 %shard_map.70 = (bf16[8,128,128]{2,1,0:T(8,128)(2,1)S(1)}, f32[8,128,1]{2,1,0:T(8,128)S(1)}, f32[128,1024]{1,0:T(8,128)S(1)}) custom-call(s32[1,256]{1,0:T(1,128)S(1)} %get-tuple-element.29.from_ref, bf16[128,1024]{1,0:T(8,128)(2,1)S(1)} %shard_map.69.refs_0_, bf16[128,1024]{1,0:T(8,128)(2,1)S(1)} %shard_map.66.refs_1_, ...), custom_call_target="tpu_custom_call" | custom-call | tf_op jit(solution)/shard_map/pallas_call | solution.py:290
  29.3 0.3 collective-permute-done.13.refs_0_
  29.6 0.3 shard_map.71
  29.9 0.1 collective-permute-start.14
  29.9 2.7 %collective-permute-start.15 = (bf16[32,1024]{1,0:T(8,128)(2,1)S(1)}, bf16[32,1024]{1,0:T(8,128)(2,1)S(1)}, u32[]{:S(2)}, u32[]{:S(2)}) collective-permute-start(bf16[32,1024]{1,0:T(8,128)(2,1)S(1)} %get-tuple-element.51), channel_id=1, source_target_pairs={{0,6},{1,7},{2,4},{3,5},{4,2},{5,3},{6,0},{7,1},{8,14},{9,15},{10,... | collective-permute-start | bytes 196616 | tf_op jit(solution)/shard_map/ppermute | solution.py:317
  32.7 1.9 %collective-permute-start.16 = (bf16[32,1024]{1,0:T(8,128)(2,1)S(1)}, bf16[32,1024]{1,0:T(8,128)(2,1)S(1)}, u32[]{:S(2)}, u32[]{:S(2)}) collective-permute-start(bf16[32,1024]{1,0:T(8,128)(2,1)S(1)} %get-tuple-element.52), channel_id=1, source_target_pairs={{0,4},{1,5},{2,0},{3,1},{4,6},{5,7},{6,2},{7,3},{8,12},{9,13},{10,... | collective-permute-start | bytes 196616 | tf_op jit(solution)/shard_map/ppermute | solution.py:317
  34.6 3.5 %collective-permute-done.14.refs_1_ = bf16[32,1024]{1,0:T(8,128)(2,1)S(1)} collective-permute-done((bf16[32,1024]{1,0:T(8,128)(2,1)S(1)}, bf16[32,1024]{1,0:T(8,128)(2,1)S(1)}, u32[]{:S(2)}, u32[]{:S(2)}) %collective-permute-start.14) | collective-permute-done | bytes 65568 | tf_op jit(solution)/shard_map/ppermute | solution.py:317
  38.2 0.0 collective-permute-done.15.refs_2_
  38.2 0.0 collective-permute-done.16.refs_3_
  38.2 0.7 %shard_map.72 = bf16[32,4096]{1,0:T(8,128)(2,1)} custom-call(bf16[32,1024]{1,0:T(8,128)(2,1)S(1)} %get-tuple-element.49.refs_0_, bf16[32,1024]{1,0:T(8,128)(2,1)S(1)} %collective-permute-done.14.refs_1_, bf16[32,1024]{1,0:T(8,128)(2,1)S(1)} %collective-permute-done.15.refs_2_, bf16[32,1024]{1,0:T(8,128)(2,1)S(1)} %collective-permute-done.16.refs_3_), custom_call_target="tpu_custom_call" | custom-call | tf_op jit(solution)/shard_map/pallas_call | solution.py:397
  (4 shorter events, 0.1 us)
Async XLA Ops:
  1.3 9.5 %collective-permute-start = (bf16[32,1024]{1,0:T(8,128)(2,1)S(1)}, bf16[32,1024]{1,0:T(8,128)(2,1)S(1)}, u32[]{:S(2)}, u32[]{:S(2)}) collective-permute-start(bf16[32,1024]{1,0:T(8,128)(2,1)S(1)} %get-tuple-element.32), channel_id=1, source_target_pairs={{0,6},{1,7},{2,4},{3,5},{4,2},{5,3},{6,0},{7,1},{8,14},{9,15},{10,... | collective-permute-start | bytes 196616 | tf_op jit(solution)/shard_map/ppermute | solution.py:317
  6.4 6.1 %collective-permute-start.1 = (bf16[32,1024]{1,0:T(8,128)(2,1)S(1)}, bf16[32,1024]{1,0:T(8,128)(2,1)S(1)}, u32[]{:S(2)}, u32[]{:S(2)}) collective-permute-start(bf16[32,1024]{1,0:T(8,128)(2,1)S(1)} %get-tuple-element.33), channel_id=1, source_target_pairs={{0,2},{1,3},{2,6},{3,7},{4,0},{5,1},{6,4},{7,5},{8,10},{9,11},{10,... | collective-permute-start | bytes 196616 | tf_op jit(solution)/shard_map/ppermute | solution.py:317
  6.4 6.5 %collective-permute-start.2 = (bf16[32,1024]{1,0:T(8,128)(2,1)S(1)}, bf16[32,1024]{1,0:T(8,128)(2,1)S(1)}, u32[]{:S(2)}, u32[]{:S(2)}) collective-permute-start(bf16[32,1024]{1,0:T(8,128)(2,1)S(1)} %get-tuple-element.34), channel_id=1, source_target_pairs={{0,4},{1,5},{2,0},{3,1},{4,6},{5,7},{6,2},{7,3},{8,12},{9,13},{10,... | collective-permute-start | bytes 196616 | tf_op jit(solution)/shard_map/ppermute | solution.py:317
  9.3 7.2 %collective-permute-start.6 = (bf16[32,1024]{1,0:T(8,128)(2,1)S(1)}, bf16[32,1024]{1,0:T(8,128)(2,1)S(1)}, u32[]{:S(2)}, u32[]{:S(2)}) collective-permute-start(bf16[32,1024]{1,0:T(8,128)(2,1)S(1)} %get-tuple-element.39), channel_id=1, source_target_pairs={{0,2},{1,3},{2,6},{3,7},{4,0},{5,1},{6,4},{7,5},{8,10},{9,11},{10,... | collective-permute-start | bytes 196616 | tf_op jit(solution)/shard_map/ppermute | solution.py:317
  9.4 7.2 %collective-permute-start.7 = (bf16[32,1024]{1,0:T(8,128)(2,1)S(1)}, bf16[32,1024]{1,0:T(8,128)(2,1)S(1)}, u32[]{:S(2)}, u32[]{:S(2)}) collective-permute-start(bf16[32,1024]{1,0:T(8,128)(2,1)S(1)} %get-tuple-element.40), channel_id=1, source_target_pairs={{0,6},{1,7},{2,4},{3,5},{4,2},{5,3},{6,0},{7,1},{8,14},{9,15},{10,... | collective-permute-start | bytes 196616 | tf_op jit(solution)/shard_map/ppermute | solution.py:317
  10.8 6.3 %collective-permute-start.8 = (bf16[32,1024]{1,0:T(8,128)(2,1)S(1)}, bf16[32,1024]{1,0:T(8,128)(2,1)S(1)}, u32[]{:S(2)}, u32[]{:S(2)}) collective-permute-start(bf16[32,1024]{1,0:T(8,128)(2,1)S(1)} %get-tuple-element.41), channel_id=1, source_target_pairs={{0,4},{1,5},{2,0},{3,1},{4,6},{5,7},{6,2},{7,3},{8,12},{9,13},{10,... | collective-permute-start | bytes 196616 | tf_op jit(solution)/shard_map/ppermute | solution.py:317
  12.6 8.0 %collective-permute-start.5 = (bf16[64,1024]{1,0:T(8,128)(2,1)S(1)}, bf16[64,1024]{1,0:T(8,128)(2,1)S(1)}, u32[]{:S(2)}, u32[]{:S(2)}) collective-permute-start(bf16[64,1024]{1,0:T(8,128)(2,1)S(1)} %get-tuple-element.36), channel_id=1, source_target_pairs={{0,2},{1,3},{2,0},{3,1},{4,6},{5,7},{6,4},{7,5},{8,10},{9,11},{10,... | collective-permute-start | bytes 393224 | tf_op jit(solution)/shard_map/ppermute | solution.py:317
  12.9 12.2 %collective-permute-start.3 = (bf16[128,1024]{1,0:T(8,128)(2,1)S(1)}, bf16[128,1024]{1,0:T(8,128)(2,1)S(1)}, u32[]{:S(2)}, u32[]{:S(2)}) collective-permute-start(bf16[128,1024]{1,0:T(8,128)(2,1)S(1)} %shard_map.66.refs_1_), channel_id=1, source_target_pairs={{0,8},{8,16},{16,24},{1,9},{9,17},{17,25},{2,10},{10,18},{18,26},{... | collective-permute-start | bytes 786440 | tf_op jit(solution)/shard_map/ppermute | solution.py:22
  17.1 11.0 %collective-permute-start.12 = (bf16[128,1024]{1,0:T(8,128)(2,1)S(1)}, bf16[128,1024]{1,0:T(8,128)(2,1)S(1)}, u32[]{:S(2)}, u32[]{:S(2)}) collective-permute-start(bf16[128,1024]{1,0:T(8,128)(2,1)S(1)} %shard_map.67.refs_3_), channel_id=1, source_target_pairs={{0,8},{8,16},{16,24},{1,9},{9,17},{17,25},{2,10},{10,18},{18,26},{... | collective-permute-start | bytes 786440 | tf_op jit(solution)/shard_map/ppermute | solution.py:22
  20.6 7.5 %collective-permute-start.9 = (bf16[64,1024]{1,0:T(8,128)(2,1)S(1)}, bf16[64,1024]{1,0:T(8,128)(2,1)S(1)}, u32[]{:S(2)}, u32[]{:S(2)}) collective-permute-start(bf16[64,1024]{1,0:T(8,128)(2,1)S(1)} %shard_map.68), channel_id=1, source_target_pairs={{0,4},{1,5},{2,6},{3,7},{4,0},{5,1},{6,2},{7,3},{8,12},{9,13},{10,... | collective-permute-start | bytes 393224 | tf_op jit(solution)/shard_map/ppermute | solution.py:317
  25.1 3.0 %collective-permute-start.11 = (bf16[128,1024]{1,0:T(8,128)(2,1)S(1)}, bf16[128,1024]{1,0:T(8,128)(2,1)S(1)}, u32[]{:S(2)}, u32[]{:S(2)}) collective-permute-start(bf16[128,1024]{1,0:T(8,128)(2,1)S(1)} %shard_map.67.refs_3_), channel_id=1, source_target_pairs={{0,1},{1,0},{2,3},{3,2},{4,5},{5,4},{6,7},{7,6},{8,9},{9,8},{10,11... | collective-permute-start | bytes 786440 | tf_op jit(solution)/shard_map/ppermute | solution.py:320
  25.2 2.9 %collective-permute-start.4 = (bf16[128,1024]{1,0:T(8,128)(2,1)S(1)}, bf16[128,1024]{1,0:T(8,128)(2,1)S(1)}, u32[]{:S(2)}, u32[]{:S(2)}) collective-permute-start(bf16[128,1024]{1,0:T(8,128)(2,1)S(1)} %collective-permute-done.3.refs_5_), channel_id=1, source_target_pairs={{0,1},{1,0},{2,3},{3,2},{4,5},{5,4},{6,7},{7,6},{8,9},{9,8},{10,11... | collective-permute-start | bytes 786440 | tf_op jit(solution)/shard_map/ppermute | solution.py:320
  25.7 2.4 %collective-permute-start.10 = (bf16[128,1024]{1,0:T(8,128)(2,1)S(1)}, bf16[128,1024]{1,0:T(8,128)(2,1)S(1)}, u32[]{:S(2)}, u32[]{:S(2)}) collective-permute-start(bf16[128,1024]{1,0:T(8,128)(2,1)S(1)} %shard_map.66.refs_1_), channel_id=1, source_target_pairs={{0,1},{1,0},{2,3},{3,2},{4,5},{5,4},{6,7},{7,6},{8,9},{9,8},{10,11... | collective-permute-start | bytes 786440 | tf_op jit(solution)/shard_map/ppermute | solution.py:320
  28.1 1.5 %collective-permute-start.13 = (bf16[128,1024]{1,0:T(8,128)(2,1)S(1)}, bf16[128,1024]{1,0:T(8,128)(2,1)S(1)}, u32[]{:S(2)}, u32[]{:S(2)}) collective-permute-start(bf16[128,1024]{1,0:T(8,128)(2,1)S(1)} %collective-permute-done.12.refs_7_), channel_id=1, source_target_pairs={{0,1},{1,0},{2,3},{3,2},{4,5},{5,4},{6,7},{7,6},{8,9},{9,8},{10,11... | collective-permute-start | bytes 786440 | tf_op jit(solution)/shard_map/ppermute | solution.py:320
  29.9 8.3 %collective-permute-start.14 = (bf16[32,1024]{1,0:T(8,128)(2,1)S(1)}, bf16[32,1024]{1,0:T(8,128)(2,1)S(1)}, u32[]{:S(2)}, u32[]{:S(2)}) collective-permute-start(bf16[32,1024]{1,0:T(8,128)(2,1)S(1)} %get-tuple-element.50), channel_id=1, source_target_pairs={{0,2},{1,3},{2,6},{3,7},{4,0},{5,1},{6,4},{7,5},{8,10},{9,11},{10,... | collective-permute-start | bytes 196616 | tf_op jit(solution)/shard_map/ppermute | solution.py:317
  29.9 8.2 %collective-permute-start.15 = (bf16[32,1024]{1,0:T(8,128)(2,1)S(1)}, bf16[32,1024]{1,0:T(8,128)(2,1)S(1)}, u32[]{:S(2)}, u32[]{:S(2)}) collective-permute-start(bf16[32,1024]{1,0:T(8,128)(2,1)S(1)} %get-tuple-element.51), channel_id=1, source_target_pairs={{0,6},{1,7},{2,4},{3,5},{4,2},{5,3},{6,0},{7,1},{8,14},{9,15},{10,... | collective-permute-start | bytes 196616 | tf_op jit(solution)/shard_map/ppermute | solution.py:317
  32.7 5.5 %collective-permute-start.16 = (bf16[32,1024]{1,0:T(8,128)(2,1)S(1)}, bf16[32,1024]{1,0:T(8,128)(2,1)S(1)}, u32[]{:S(2)}, u32[]{:S(2)}) collective-permute-start(bf16[32,1024]{1,0:T(8,128)(2,1)S(1)} %get-tuple-element.52), channel_id=1, source_target_pairs={{0,4},{1,5},{2,0},{3,1},{4,6},{5,7},{6,2},{7,3},{8,12},{9,13},{10,... | collective-permute-start | bytes 196616 | tf_op jit(solution)/shard_map/ppermute | solution.py:317
